TPU v7x, 128 devices: a whole 4x4x4 slice. The times are simulated.
128 devices in a mesh: row: 16 (over z, x), col: 2 (over y_hi), edge: 4 (over y_lo, core).
Axes of the slice: x: 4, y: 4 (y_hi: 2, y_lo: 2; y = y_hi * 2 + y_lo), z: 4, core: 2. Of those that a mesh axis runs over, the one named last changes fastest.
Arguments:
- features: bfloat16 [65536, 256], P('row', 'col'), may hold values from -6 to 6
- tiles: bfloat16 [45056, 128, 128], P(('row', 'edge')), may hold values from -0.078125 to 0.078125
- tile_rows: int32 [45056], P(('row', 'edge')), may hold values from 0 to 31
- tile_cols: int32 [45056], P(('row', 'edge')), may hold values from 0 to 95
- tile_count: int32 [64], P(('row', 'edge')), may hold values from 88 to 704, as said below
- w_self: bfloat16 [256, 256], P(None, 'col'), may hold values from -0.375 to 0.375
- w_neigh: bfloat16 [256, 256], P(None, 'col'), may hold values from -0.375 to 0.375
- bias: float32 [256], P('col'), may hold values from -3 to 3
- cotangent: bfloat16 [65536, 256], P(('row', 'edge'), 'col'), may hold values from -6 to 6
Outputs:
- output: bfloat16 [65536, 256], P(('row', 'edge'), 'col')
- features_grad: float32 [65536, 256], P(('row', 'edge'), 'col')
- w_self_grad: float32 [256, 256], P(None, 'col')
- w_neigh_grad: float32 [256, 256], P(None, 'col')
- bias_grad: float32 [256], P('col')
Inputs may be any that keep to these rules, and one draw needn't show every extreme that they name: `tile_count`: some list uses all 704 slots in every draw.
All inputs are finite; a program needn't handle non-finite values.
Results may differ from a plain program's by a relative error of at most 0.012.
Values may be sent and summed in bfloat16 or wider, within the bound.
A program may use at most 128 MiB of HBM per device.

v0:
```python
import math

import jax
import jax.numpy as jnp
from jax import lax
from jax.sharding import PartitionSpec as P


def passed_along(array, axis, by):
    size = lax.axis_size(axis)
    return lax.ppermute(array, axis, [(i, (i + by) % size) for i in range(size)])


def with_halo(array, sides, width):
    for axis, dim in sides:
        size, length = (lax.axis_size(axis), array.shape[dim])
        up = [(i, (i + 1) % size) for i in range(size)]
        down = [(j, i) for i, j in up]
        last = lax.slice_in_dim(array, length - width, length, axis=dim)
        initial = lax.slice_in_dim(array, 0, width, axis=dim)
        before = lax.ppermute(last, axis, up)
        after = lax.ppermute(initial, axis, down)
        array = jnp.concatenate([before, array, after], axis=dim)
    return array


def grouped(array, group):
    return array.reshape((array.shape[0] // group, group) + array.shape[1:])


def return_parts(left, middle, right):
    from_after = passed_along(left.astype(jnp.bfloat16), "row", -1).astype(left.dtype)
    from_before = passed_along(right.astype(jnp.bfloat16), "row", 1).astype(right.dtype)
    return middle + from_after + from_before


def edge_reduce(parts):
    return lax.psum_scatter(
        parts.astype(jnp.bfloat16), "edge", scatter_dimension=1, tiled=True
    ).astype(jnp.float32)


def local(features, tiles, tile_rows, tile_cols, tile_count, w_self, w_neigh, bias, cotangent):
    f32 = jnp.float32
    rows_dev, half = features.shape
    tile_size = tiles.shape[1]
    blocks = rows_dev // tile_size
    slots = tiles.shape[0]
    group = 64
    share = rows_dev // lax.axis_size("edge")
    nodes = rows_dev * lax.axis_size("row")
    count = tile_count[0]
    tile_groups = grouped(tiles, group)
    row_groups = grouped(tile_rows, group)
    col_groups = grouped(tile_cols, group)
    starts = jnp.arange(slots // group, dtype=jnp.int32) * group
    offsets = jnp.arange(group, dtype=jnp.int32)
    window = with_halo(features, (("row", 0),), rows_dev)
    window_blocks = window.reshape(3 * blocks, tile_size, half)

    def forward_step(total, items):
        tile_grp, row_grp, col_grp, start = items

        def forward_work(current):
            picked = window_blocks[col_grp]
            prod = jnp.einsum("gij,gjf->gif", tile_grp, picked, preferred_element_type=f32)
            live = (start + offsets < count).astype(f32)
            return current.at[row_grp].add(prod * live[:, None, None])

        return (lax.cond(start < count, forward_work, lambda current: current, total), None)

    initial = jnp.zeros((blocks, tile_size, half), f32)
    partial_sum, _ = lax.scan(forward_step, initial, (tile_groups, row_groups, col_groups, starts))
    agg = lax.psum_scatter(
        partial_sum.reshape(rows_dev, half), "edge", scatter_dimension=0, tiled=True
    ).astype(jnp.bfloat16)
    own = lax.dynamic_slice_in_dim(features, lax.axis_index("edge") * share, share, 0)
    own_full, agg_full = (
        lax.all_gather(own, "col", axis=1, tiled=True),
        lax.all_gather(agg, "col", axis=1, tiled=True),
    )
    pre = (
        jnp.dot(own_full, w_self, preferred_element_type=f32)
        + jnp.dot(agg_full, w_neigh, preferred_element_type=f32)
        + bias[None, :]
    )
    sigm = jax.nn.sigmoid(pre)
    output = (pre * sigm).astype(jnp.bfloat16)
    grad_pre = cotangent.astype(f32) * sigm * (1.0 + pre * (1.0 - sigm))
    grad_low = grad_pre.astype(jnp.bfloat16)
    over_rows = (((0,), (0,)), ((), ()))
    self_weight = lax.dot_general(own_full, grad_low, over_rows, preferred_element_type=f32)
    neigh_weight = lax.dot_general(agg_full, grad_low, over_rows, preferred_element_type=f32)
    bias_part = jnp.sum(grad_pre, axis=0)
    self_weight, neigh_weight, bias_total = lax.psum(
        (self_weight, neigh_weight, bias_part), ("row", "edge")
    )
    scale = 1.0 / math.sqrt(nodes)
    over_cols = (((1,), (1,)), ((), ()))
    self_back = lax.dot_general(grad_low, w_self, over_cols, preferred_element_type=f32)
    agg_back = lax.dot_general(grad_low, w_neigh, over_cols, preferred_element_type=f32)
    self_back, agg_back = (
        lax.psum_scatter(self_back, "col", scatter_dimension=1, tiled=True),
        lax.psum_scatter(agg_back, "col", scatter_dimension=1, tiled=True),
    )
    rows_back = lax.all_gather(agg_back.astype(jnp.bfloat16), "edge", axis=0, tiled=True)
    rows_blocks = rows_back.reshape(blocks, tile_size, half)

    def backward_step(total, items):
        tile_grp, row_grp, col_grp, start = items

        def backward_work(current):
            picked = rows_blocks[row_grp]
            prod = jnp.einsum("gji,gjf->gif", tile_grp, picked, preferred_element_type=f32)
            live = (start + offsets < count).astype(f32)
            return current.at[col_grp].add(prod * live[:, None, None])

        return (lax.cond(start < count, backward_work, lambda current: current, total), None)

    back_initial = jnp.zeros((3 * blocks, tile_size, half), f32)
    back_total, _ = lax.scan(
        backward_step, back_initial, (tile_groups, row_groups, col_groups, starts)
    )
    parts = back_total.reshape(3, rows_dev, half)
    joined = return_parts(parts[0], parts[1], parts[2])
    neigh_back = edge_reduce(joined[None])[0]
    features_grad = self_back + neigh_back
    return (output, features_grad, self_weight * scale, neigh_weight * scale, bias_total * scale)


def solution(mesh):
    return jax.shard_map(
        local,
        mesh=mesh,
        in_specs=(
            P("row", "col"),
            P(("row", "edge"), None, None),
            P(("row", "edge")),
            P(("row", "edge")),
            P(("row", "edge")),
            P(None, "col"),
            P(None, "col"),
            P("col"),
            P(("row", "edge"), "col"),
        ),
        out_specs=(
            P(("row", "edge"), "col"),
            P(("row", "edge"), "col"),
            P(None, "col"),
            P(None, "col"),
            P("col"),
        ),
        check_vma=False,
    )
```

profile of v0, /device:TPU:1, one launch (start us, length us, event | category | flops | bytes accessed | tf_op | source)
XLA Modules:
  0.0 934.7 jit_solution(10934245037310073539)
XLA Ops:
  7.2 2.1 collective-permute-start
  9.3 4.8 collective-permute-start.1
  15.7 21.5 %collective-permute-done = bf16[4096,128]{1,0:T(8,128)(2,1)S(1)} collective-permute-done((bf16[4096,128]{1,0:T(8,128)(2,1)}, bf16[4096,128]{1,0:T(8,128)(2,1)S(1)}, u32[]{:S(2)}, u32[]{:S(2)}) %collective-permute-start) | collective-permute-done | bytes 1048608 | tf_op jit(solution)/shard_map/ppermute | solution.py:21
  37.2 12.6 %pad_maximum_fusion = bf16[12288,128]{1,0:T(8,128)(2,1)} fusion(bf16[4096,128]{1,0:T(8,128)(2,1)S(1)} %collective-permute-done.1, bf16[4096,128]{1,0:T(8,128)(2,1)} %param.17, bf16[4096,128]{1,0:T(8,128)(2,1)S(1)} %collective-permute-done), kind=kLoop, calls=%fused_computation.34 | loop fusion | flops 9437184 | bytes 6291456 | tf_op jit(solution)/shard_map/concatenate | solution.py:23
  50.0 59.4 %while.28 = (s32[]{:T(128)}, f32[32,128,128]{2,1,0:T(8,128)S(1)}, s32[11]{0:T(128)S(1)}, s32[]{:T(128)}, s32[11,64]{1,0:T(8,128)S(1)}, /*index=5*/bf16[11,64,128...) while((s32[]{:T(128)}, f32[32,128,128]{2,1,0:T(8,128)S(1)}, ...), condition=%wide.region_4.5_spmd.clone, body=%wide.region_0.4_spmd.clone.sunk | while | flops 270534208 | bytes 25173460 | solution.py:73
  51.9 19.1 %conditional.6 = (f32[32,128,128]{2,1,0:T(8,128)S(1)}) conditional(s32[]{:T(128)} %convert_element_type.75, f32[32,128,128]{2,1,0:T(8,128)S(1)} %get-tuple-element.469, (s32[11,64]{1,0:T(8,128)S(1)}, s32[]{:T(128)}, bf16[11,64,128,128]{3,2,1,0:T(8,128)(2,1)}, s32[11,64]{1,0:T(8,128)S(1)}, bf16[96,128,128]{2,1,0:T(8,128)(2,1)}, /*index=5*/s32[]{:T(128)}, ...), branch_computations={%region_1.1_spmd, %region_2.3_spmd} | conditional | flops 270534208 | bytes 25173012 | solution.py:70
  52.0 4.1 gather_fusion
  56.1 1.3 compare_convert_fusion
  57.4 4.9 convolution_multiply_fusion
  62.3 8.8 scatter_fusion
  73.0 19.1 %conditional.6 = (f32[32,128,128]{2,1,0:T(8,128)S(1)}) conditional(s32[]{:T(128)} %convert_element_type.75, f32[32,128,128]{2,1,0:T(8,128)S(1)} %get-tuple-element.469, (s32[11,64]{1,0:T(8,128)S(1)}, s32[]{:T(128)}, bf16[11,64,128,128]{3,2,1,0:T(8,128)(2,1)}, s32[11,64]{1,0:T(8,128)S(1)}, bf16[96,128,128]{2,1,0:T(8,128)(2,1)}, /*index=5*/s32[]{:T(128)}, ...), branch_computations={%region_1.1_spmd, %region_2.3_spmd} | conditional | flops 270534208 | bytes 25173012 | solution.py:70
  73.0 4.1 gather_fusion
  77.1 1.3 compare_convert_fusion
  78.4 4.9 convolution_multiply_fusion
  83.3 8.8 scatter_fusion
  109.5 1.3 copy-done.2
  111.8 7.4 all_gather.9
  119.6 191.3 %reduce-scatter.5.cloned.1.call-done = f32[1024,128]{1,0:T(8,128)} async-done(((f32[4096,128]{1,0:T(8,128)}), f32[1024,128]{1,0:T(8,128)}) %reduce-scatter.5.cloned.1.call-update) | async-done | bytes 524304 | tf_op jit(solution)/shard_map/reduce_scatter | solution.py:74
  310.8 1.1 convert_element_type.52
  311.9 9.7 %all_gather.10 = bf16[1024,256]{1,0:T(8,128)(2,1)S(1)} all-gather(bf16[1024,128]{1,0:T(8,128)(2,1)S(1)} %convert_element_type.52), channel_id=1, replica_groups=mesh['row'=16,'col'=2,'edge'=4] {'col'}, dimensions={1}, use_global_device_ids=true | all-gather | bytes 786432 | tf_op jit(solution)/shard_map/all_gather | solution.py:80
  321.6 1.2 fusion.21
  322.7 1.3 fusion.25
  324.1 26.0 %reduce-scatter.9.cloned.1.call-done = f32[1024,128]{1,0:T(8,128)} async-done(((f32[1024,256]{1,0:T(8,128)}), f32[1024,128]{1,0:T(8,128)}) %reduce-scatter.9.cloned.1.call-update) | async-done | bytes 524304 | tf_op jit(solution)/shard_map/reduce_scatter | solution.py:104
  350.1 1.8 convert_element_type.56
  354.0 30.5 %copy.14 = bf16[704,128,128]{1,2,0:T(8,128)(2,1)} copy(bf16[704,128,128]{2,1,0:T(8,128)(2,1)} %bitcast.80) | data formatting | bytes 46137344 | tf_op args[1]
  384.5 1.3 fusion.24
  386.1 3.4 broadcast_in_dim.15
  389.5 61.3 %while.29 = (s32[]{:T(128)}, f32[96,128,128]{2,1,0:T(8,128)}, s32[11]{0:T(128)S(1)}, s32[]{:T(128)}, s32[11,64]{1,0:T(8,128)S(1)}, /*index=5*/bf16[11,64,128,128...) while((s32[]{:T(128)}, f32[96,128,128]{2,1,0:T(8,128)}, ...), condition=%wide.region_12.13_spmd.clone, body=%wide.region_8.0_spmd.clone.sunk | while | flops 270534208 | bytes 25173460 | solution.py:121
  391.4 20.1 %conditional.7 = (f32[96,128,128]{2,1,0:T(8,128)}) conditional(s32[]{:T(128)} %convert_element_type.76, f32[96,128,128]{2,1,0:T(8,128)} %get-tuple-element.496, (s32[11,64]{1,0:T(8,128)S(1)}, s32[]{:T(128)}, bf16[11,64,128,128]{2,3,1,0:T(8,128)(2,1)}, s32[11,64]{1,0:T(8,128)S(1)}, bf16[32,128,128]{2,1,0:T(8,128)(2,1)S(1)}, /*index=5*/s32[]{:T(128)}, ...), branch_computations={%region_9.9_spmd, %region_10.11_spmd} | conditional | flops 270534208 | bytes 25173012 | solution.py:118
  392.4 1.3 compare_convert_fusion.1
  393.7 4.2 convolution_multiply_fusion.1
  397.9 13.6 %scatter_fusion.1 = f32[96,128,128]{2,1,0:T(8,128)} fusion(f32[96,128,128]{2,1,0:T(8,128)} %get-tuple-element.241, s32[64]{0:T(128)S(1)} %get-tuple-element.351, f32[64,128,128]{2,1,0:T(8,128)} %convolution_multiply_fusion.1), kind=kCustom, calls=%fused_computation.3 | custom fusion | flops 1048576 | bytes 12583168 | tf_op jit(solution)/shard_map/while/body/eval_jaxpr/cond/branch_1_fun/scatter-add | solution.py:116
  413.4 20.1 %conditional.7 = (f32[96,128,128]{2,1,0:T(8,128)}) conditional(s32[]{:T(128)} %convert_element_type.76, f32[96,128,128]{2,1,0:T(8,128)} %get-tuple-element.496, (s32[11,64]{1,0:T(8,128)S(1)}, s32[]{:T(128)}, bf16[11,64,128,128]{2,3,1,0:T(8,128)(2,1)}, s32[11,64]{1,0:T(8,128)S(1)}, bf16[32,128,128]{2,1,0:T(8,128)(2,1)S(1)}, /*index=5*/s32[]{:T(128)}, ...), branch_computations={%region_9.9_spmd, %region_10.11_spmd} | conditional | flops 270534208 | bytes 25173012 | solution.py:118
  414.4 1.3 compare_convert_fusion.1
  415.7 4.2 convolution_multiply_fusion.1
  419.9 13.6 %scatter_fusion.1 = f32[96,128,128]{2,1,0:T(8,128)} fusion(f32[96,128,128]{2,1,0:T(8,128)} %get-tuple-element.241, s32[64]{0:T(128)S(1)} %get-tuple-element.351, f32[64,128,128]{2,1,0:T(8,128)} %convolution_multiply_fusion.1), kind=kCustom, calls=%fused_computation.3 | custom fusion | flops 1048576 | bytes 12583168 | tf_op jit(solution)/shard_map/while/body/eval_jaxpr/cond/branch_1_fun/scatter-add | solution.py:116
  450.9 3.5 convert.5
  454.5 65.1 %collective-permute-start.2 = (bf16[4096,128]{1,0:T(8,128)(2,1)S(1)}, bf16[4096,128]{1,0:T(8,128)(2,1)S(1)}, u32[]{:S(2)}, u32[]{:S(2)}) collective-permute-start(bf16[4096,128]{1,0:T(8,128)(2,1)S(1)} %bitcast.84), channel_id=1, source_target_pairs={{0,120},{8,0},{16,8},{24,16},{32,24},{40,32},{48,40},{56,48},{64,5... | collective-permute-start | bytes 3145736 | tf_op jit(solution)/shard_map/ppermute | solution.py:11
  519.7 1.8 slice.14
  521.4 10.1 %collective-permute-done.2 = bf16[4096,128]{1,0:T(8,128)(2,1)S(1)} collective-permute-done((bf16[4096,128]{1,0:T(8,128)(2,1)S(1)}, bf16[4096,128]{1,0:T(8,128)(2,1)S(1)}, u32[]{:S(2)}, u32[]{:S(2)}) %collective-permute-start.2) | collective-permute-done | bytes 1048608 | tf_op jit(solution)/shard_map/ppermute | solution.py:11
  531.5 5.2 collective-permute-done.3
  536.7 1.3 fusion.19
  538.1 252.1 %psum.23 = f32[128]{0:T(128)S(1)} all-reduce(f32[128]{0:T(128)S(1)} %get-tuple-element.347), channel_id=1, replica_groups=mesh['row'=16,'col'=2,'edge'=4] {'row','edge'}, use_global_device_ids=true, to_apply=%region_17.18 | all-reduce | flops 128 | bytes 1024 | tf_op jit(solution)/shard_map/psum | solution.py:95
  790.7 87.5 %all-reduce.3.cloned.1.call-done = (f32[256,128]{1,0:T(8,128)}, f32[256,128]{1,0:T(8,128)}) async-done(((f32[256,128]{1,0:T(8,128)}, f32[256,128]{1,0:T(8,128)}), (f32[256,128]{1,0:T(8,128)}, f32[256,128]{1,0:T(8,128)})) %all-reduce.3.cloned.1.call-update) | async-done | bytes 262160 | tf_op jit(solution)/shard_map/psum | solution.py:95
  878.2 1.7 broadcast_multiply_fusion
  879.9 23.9 %reduce-scatter.7.cloned.1.call-done = f32[1024,128]{1,0:T(8,128)} async-done(((f32[1024,256]{1,0:T(8,128)}), f32[1024,128]{1,0:T(8,128)}) %reduce-scatter.7.cloned.1.call-update) | async-done | bytes 524304 | tf_op jit(solution)/shard_map/reduce_scatter | solution.py:103
  903.8 22.1 %reduce-scatter.11.cloned.1.call-done = bf16[1,1024,128]{2,1,0:T(8,128)(2,1)} async-done(((bf16[1,4096,128]{2,1,0:T(8,128)(2,1)}), bf16[1,1024,128]{2,1,0:T(8,128)(2,1)}) %reduce-scatter.11.cloned.1.call-update) | async-done | bytes 262160 | tf_op jit(solution)/shard_map/reduce_scatter | solution.py:38
  925.9 1.9 convert_add_fusion
  (110 shorter events, 21.4 us)
Async XLA Ops:
  7.2 314.4 %copy-start = (bf16[256,128]{1,0:T(8,128)(2,1)S(1)}, bf16[256,128]{1,0:T(8,128)(2,1)}, u32[]{:S(2)}) copy-start(bf16[256,128]{1,0:T(8,128)(2,1)} %param.23) | copy-start | bytes 196612
  7.2 303.6 %reduce-scatter.5.cloned.1.call-start = ((), (), s32[]{:S(2)}) async-start(), calls=%async_computation.4 | async-start | bytes 2621440 | tf_op jit(solution)/shard_map/reduce_scatter | solution.py:74
  7.2 29.9 %collective-permute-start = (bf16[4096,128]{1,0:T(8,128)(2,1)}, bf16[4096,128]{1,0:T(8,128)(2,1)S(1)}, u32[]{:S(2)}, u32[]{:S(2)}) collective-permute-start(bf16[4096,128]{1,0:T(8,128)(2,1)} %param.17), channel_id=1, source_target_pairs={{0,8},{8,16},{16,24},{24,32},{32,40},{40,48},{48,56},{56,64},{64,7... | collective-permute-start | bytes 3145736 | tf_op jit(solution)/shard_map/ppermute | solution.py:21
  9.3 27.8 %collective-permute-start.1 = (bf16[4096,128]{1,0:T(8,128)(2,1)}, bf16[4096,128]{1,0:T(8,128)(2,1)S(1)}, u32[]{:S(2)}, u32[]{:S(2)}) collective-permute-start(bf16[4096,128]{1,0:T(8,128)(2,1)} %param.17), channel_id=1, source_target_pairs={{8,0},{16,8},{24,16},{32,24},{40,32},{48,40},{56,48},{64,56},{72,6... | collective-permute-start | bytes 3145736 | tf_op jit(solution)/shard_map/ppermute | solution.py:22
  109.4 1.3 copy-start.2
  109.5 9.8 %copy-start.4 = (bf16[256,128]{1,0:T(8,128)(2,1)S(1)}, bf16[256,128]{1,0:T(8,128)(2,1)}, u32[]{:S(2)}) copy-start(bf16[256,128]{1,0:T(8,128)(2,1)} %param.22) | copy-start | bytes 196612
  109.5 212.1 %copy-start.5 = (bf16[1024,128]{1,0:T(8,128)(2,1)S(1)}, bf16[1024,128]{1,0:T(8,128)(2,1)}, u32[]{:S(2)}) copy-start(bf16[1024,128]{1,0:T(8,128)(2,1)} %param.25) | copy-start | bytes 786436
  109.5 212.1 %copy-start.6 = (f32[128]{0:T(128)S(1)}, f32[128]{0:T(128)}, u32[]{:S(2)}) copy-start(f32[128]{0:T(128)} %param.24) | copy-start | bytes 1540
  110.8 239.3 %reduce-scatter.9.cloned.1.call-start = ((), (), s32[]{:S(2)}) async-start(), calls=%async_computation.6 | async-start | bytes 1572864 | tf_op jit(solution)/shard_map/reduce_scatter | solution.py:104
  324.0 62.0 %all-gather.2.cloned.1.call-start = ((), (), s32[]{:S(2)}) async-start(), calls=%async_computation.7 | async-start | bytes 1310720 | tf_op jit(solution)/shard_map/all_gather | solution.py:106
  351.9 526.3 %all-reduce.3.cloned.1.call-start = ((), (), s32[]{:S(2)}) async-start(), calls=%async_computation.9 | async-start | bytes 524288 | tf_op jit(solution)/shard_map/psum | solution.py:95
  354.0 549.8 %reduce-scatter.7.cloned.1.call-start = ((), (), s32[]{:S(2)}) async-start(), calls=%async_computation.5 | async-start | bytes 1572864 | tf_op jit(solution)/shard_map/reduce_scatter | solution.py:103
  385.8 540.1 %reduce-scatter.11.cloned.1.call-start = ((), (), s32[]{:S(2)}) async-start(), calls=%async_computation.8 | async-start | bytes 1310720 | tf_op jit(solution)/shard_map/reduce_scatter | solution.py:38
  386.1 3.4 copy-start.3
  454.5 77.0 %collective-permute-start.2 = (bf16[4096,128]{1,0:T(8,128)(2,1)S(1)}, bf16[4096,128]{1,0:T(8,128)(2,1)S(1)}, u32[]{:S(2)}, u32[]{:S(2)}) collective-permute-start(bf16[4096,128]{1,0:T(8,128)(2,1)S(1)} %bitcast.84), channel_id=1, source_target_pairs={{0,120},{8,0},{16,8},{24,16},{32,24},{40,32},{48,40},{56,48},{64,5... | collective-permute-start | bytes 3145736 | tf_op jit(solution)/shard_map/ppermute | solution.py:11
  519.6 17.1 %collective-permute-start.3 = (bf16[4096,128]{1,0:T(8,128)(2,1)S(1)}, bf16[4096,128]{1,0:T(8,128)(2,1)S(1)}, u32[]{:S(2)}, u32[]{:S(2)}) collective-permute-start(bf16[4096,128]{1,0:T(8,128)(2,1)S(1)} %bitcast.83), channel_id=1, source_target_pairs={{0,8},{8,16},{16,24},{24,32},{32,40},{40,48},{48,56},{56,64},{64,7... | collective-permute-start | bytes 3145736 | tf_op jit(solution)/shard_map/ppermute | solution.py:11
  519.7 408.2 %copy-start.1 = (bf16[256,128]{1,0:T(8,128)(2,1)S(1)}, bf16[256,128]{1,0:T(8,128)(2,1)}, u32[]{:S(2)}) copy-start(bf16[256,128]{1,0:T(8,128)(2,1)} %param.23) | copy-start | bytes 196612
Sparse Core Ops, SparseCore 0:
  110.9 199.8 reduce-scatter.4
  324.1 25.9 reduce-scatter.8
  352.4 20.4 all-gather.1
  375.9 502.2 all-reduce.2
  880.5 23.2 reduce-scatter.6
  906.1 19.8 reduce-scatter.10
where the time goes:
time: 941 us; the launch traced here: 935 us
  waiting for transfers between devices  388 us (41%)
  blocking collectives  269 us (29%)
  other arithmetic  74.4 us (8%)
  starting transfers between devices  72.5 us (8%)
  local copies, waits for them, and re-layouts  62.9 us (7%)
  loops' own time  29.5 us (3%)
  matrix products  24.2 us (3%)
  between operations  14.3 us (2%)
    psum x1, blocking collectives, local(): lax.psum((self_weight, neigh_weight, bias_part), ('row', 'edge'))  252 us
    reduce_scatter x1, waiting for transfers between devices, local(): lax.psum_scatter(partial_sum.reshape(rows_dev, half), 'edge', scatter_dim...  191 us
    psum x1, waiting for transfers between devices, local(): lax.psum((self_weight, neigh_weight, bias_part), ('row', 'edge'))  87.5 us
    ppermute x2, starting transfers between devices, passed_along(): lax.ppermute(array, axis, [(i, (i + by) % size) for i in range(size)])  65.1 us
    unnamed x15, local copies, waits for them, and re-layouts  31.8 us
    scatter-add x2, other arithmetic, backward_work(): return current.at[col_grp].add(prod * live[:, None, None])  27.2 us
    reduce_scatter x1, waiting for transfers between devices, local(): lax.psum_scatter(agg_back, 'col', scatter_dimension=1, tiled=True)  26 us
    reduce_scatter x1, waiting for transfers between devices, local(): lax.psum_scatter(self_back, 'col', scatter_dimension=1, tiled=True)  23.9 us
  transfers between devices with their start and end apart: 10, of which 8 were waited for; matrix products, arithmetic and copies ran while one was open for 10% of the time, Pallas kernels for 0%

commit v1 on v0

v1 whole, which is shorter than its diff:
```python
import functools
import math

import jax
import jax.numpy as jnp
from jax import lax
from jax.experimental import pallas as pl
from jax.experimental.pallas import tpu as pltpu
from jax.sharding import PartitionSpec as P

F32 = jnp.float32
BF16 = jnp.bfloat16
UNROLL = 16
CHUNK = 176
MIB = 1024 * 1024


def passed_along(array, axis, by):
    size = lax.axis_size(axis)
    return lax.ppermute(array, axis, [(i, (i + by) % size) for i in range(size)])


def tile_loop(count, rows, cols, tiles, ring, sems, total, product, target):
    chunks = lax.div(count + CHUNK - 1, CHUNK)

    def fetch(c):
        return pltpu.make_async_copy(tiles.at[pl.ds(c * CHUNK, CHUNK)], ring.at[lax.rem(c, 2)], sems.at[lax.rem(c, 2)])

    spare = total.shape[0] - 1

    def chunk_step(c, carry):
        fetch(c).wait()

        @pl.when(c + 1 < chunks)
        def _():
            fetch(c + 1).start()

        base = c * CHUNK
        limit = jnp.minimum(count - base, CHUNK)

        def group_step(g, inner):
            start = g * UNROLL
            products = [
                product(base + start + u, ring[lax.rem(c, 2), start + u]) for u in range(UNROLL)
            ]
            for u in range(UNROLL):
                slot = base + start + u
                total[jnp.where(slot < count, target(slot), spare)] += products[u]
            return inner

        return lax.fori_loop(0, lax.div(limit + UNROLL - 1, UNROLL), group_step, carry)

    return fetch, chunks, chunk_step


def forward_kernel(rows, cols, count_ref, before, own, after, tiles, out, window, ring, total, sems, halo_sems):
    blocks = own.shape[0]
    count = count_ref[0]
    fetch, chunks, chunk_step = tile_loop(
        count, rows, cols, tiles, ring, sems, total,
        lambda slot, tile: jnp.dot(tile, window[cols[slot]], preferred_element_type=F32),
        lambda slot: rows[slot],
    )
    copies = [
        pltpu.make_async_copy(part, window.at[pl.ds(k * blocks, blocks)], halo_sems.at[k])
        for k, part in enumerate((before, own, after))
    ]
    fetch(0).start()
    for copy in copies:
        copy.start()
    total[...] = jnp.zeros_like(total)
    for copy in copies:
        copy.wait()
    lax.fori_loop(0, chunks, chunk_step, 0)
    out[...] = total[:blocks].astype(BF16)


def backward_kernel(rows, cols, count_ref, grads, tiles, out, ring, total, sems):
    count = count_ref[0]
    fetch, chunks, chunk_step = tile_loop(
        count, rows, cols, tiles, ring, sems, total,
        lambda slot, tile: jnp.dot(grads[rows[slot]], tile, preferred_element_type=F32),
        lambda slot: cols[slot],
    )
    fetch(0).start()
    total[...] = jnp.zeros_like(total)
    lax.fori_loop(0, chunks, chunk_step, 0)
    out[...] = total[: out.shape[0]].astype(BF16)


SMEM = pl.BlockSpec(memory_space=pltpu.SMEM)
VMEM = pl.BlockSpec(memory_space=pltpu.VMEM)
ANY = pl.BlockSpec(memory_space=pl.ANY)


def forward_sum(tile_rows, tile_cols, tile_count, before, own, after, tiles):
    blocks, size, half = own.shape
    return pl.pallas_call(
        forward_kernel,
        out_shape=jax.ShapeDtypeStruct((blocks, size, half), BF16),
        in_specs=[SMEM] * 3 + [ANY] * 4,
        out_specs=VMEM,
        scratch_shapes=[
            pltpu.VMEM((3 * blocks, size, half), BF16),
            pltpu.VMEM((2, CHUNK, size, size), BF16),
            pltpu.VMEM((blocks + 1, size, half), F32),
            pltpu.SemaphoreType.DMA((2,)),
            pltpu.SemaphoreType.DMA((3,)),
        ],
        compiler_params=pltpu.CompilerParams(vmem_limit_bytes=48 * MIB),
        cost_estimate=pl.CostEstimate(flops=2 * 704 * 128**3, bytes_accessed=704 * 32768, transcendentals=0),
        name="forward_sum",
    )(tile_rows, tile_cols, tile_count, before, own, after, tiles)


def backward_sum(tile_rows, tile_cols, tile_count, grads, tiles):
    blocks, half, size = grads.shape
    return pl.pallas_call(
        backward_kernel,
        out_shape=jax.ShapeDtypeStruct((3 * blocks, half, size), BF16),
        in_specs=[SMEM] * 3 + [VMEM, ANY],
        out_specs=VMEM,
        scratch_shapes=[
            pltpu.VMEM((2, CHUNK, size, size), BF16),
            pltpu.VMEM((3 * blocks + 1, half, size), F32),
            pltpu.SemaphoreType.DMA((2,)),
        ],
        compiler_params=pltpu.CompilerParams(vmem_limit_bytes=48 * MIB),
        cost_estimate=pl.CostEstimate(flops=2 * 704 * 128**3, bytes_accessed=704 * 32768, transcendentals=0),
        name="backward_sum",
    )(tile_rows, tile_cols, tile_count, grads, tiles)


def local(features, tiles, tile_rows, tile_cols, tile_count, w_self, w_neigh, bias, cotangent):
    rows_dev, half = features.shape
    size = tiles.shape[1]
    blocks = rows_dev // size
    share = rows_dev // lax.axis_size("edge")
    nodes = rows_dev * lax.axis_size("row")

    own_blocks = features.reshape(blocks, size, half)
    before = passed_along(own_blocks, "row", 1)
    after = passed_along(own_blocks, "row", -1)
    own = lax.dynamic_slice_in_dim(features, lax.axis_index("edge") * share, share, 0)
    own_full = lax.all_gather(own, "col", axis=1, tiled=True)
    partial = forward_sum(tile_rows, tile_cols, tile_count, before, own_blocks, after, tiles)
    agg = lax.psum_scatter(partial.reshape(rows_dev, half), "edge", scatter_dimension=0, tiled=True)
    agg_full = lax.all_gather(agg, "col", axis=1, tiled=True)
    pre = (
        jnp.dot(own_full, w_self, preferred_element_type=F32)
        + jnp.dot(agg_full, w_neigh, preferred_element_type=F32)
        + bias[None, :]
    )
    sigm = jax.nn.sigmoid(pre)
    output = (pre * sigm).astype(BF16)
    grad_pre = cotangent.astype(F32) * sigm * (1.0 + pre * (1.0 - sigm))
    grad_low = grad_pre.astype(BF16)
    over_rows = (((0,), (0,)), ((), ()))
    self_weight = lax.dot_general(own_full, grad_low, over_rows, preferred_element_type=F32)
    neigh_weight = lax.dot_general(agg_full, grad_low, over_rows, preferred_element_type=F32)
    bias_part = jnp.sum(grad_pre, axis=0)
    self_weight, neigh_weight, bias_total = lax.psum(
        (self_weight, neigh_weight, bias_part), ("row", "edge")
    )
    scale = 1.0 / math.sqrt(nodes)
    over_cols = (((1,), (1,)), ((), ()))
    self_back = lax.dot_general(grad_low, w_self, over_cols, preferred_element_type=F32)
    agg_back = lax.dot_general(grad_low, w_neigh, over_cols, preferred_element_type=F32)
    self_back, agg_back = (
        lax.psum_scatter(self_back, "col", scatter_dimension=1, tiled=True),
        lax.psum_scatter(agg_back, "col", scatter_dimension=1, tiled=True),
    )
    flipped = agg_back.astype(BF16).reshape(share // size, size, half).swapaxes(1, 2)
    grads = lax.all_gather(flipped, "edge", axis=0, tiled=True)
    parts = backward_sum(tile_rows, tile_cols, tile_count, grads, tiles).reshape(3, blocks, half, size)
    from_after = passed_along(parts[0], "row", -1)
    from_before = passed_along(parts[2], "row", 1)
    joined = (parts[1].astype(F32) + from_after.astype(F32) + from_before.astype(F32)).astype(BF16)
    neigh_back = lax.psum_scatter(joined, "edge", scatter_dimension=0, tiled=True)
    neigh_back = neigh_back.astype(F32).swapaxes(1, 2).reshape(share, half)
    features_grad = self_back + neigh_back
    return (output, features_grad, self_weight * scale, neigh_weight * scale, bias_total * scale)


def solution(mesh):
    return jax.shard_map(
        local,
        mesh=mesh,
        in_specs=(
            P("row", "col"),
            P(("row", "edge"), None, None),
            P(("row", "edge")),
            P(("row", "edge")),
            P(("row", "edge")),
            P(None, "col"),
            P(None, "col"),
            P("col"),
            P(("row", "edge"), "col"),
        ),
        out_specs=(
            P(("row", "edge"), "col"),
            P(("row", "edge"), "col"),
            P(None, "col"),
            P(None, "col"),
            P("col"),
        ),
        check_vma=False,
    )
```

time: 941 us -> 726 us (0.77)
  blocking collectives: 269 us -> 157 us
  waiting for transfers between devices: 388 us -> 499 us
  other arithmetic: 74.4 us -> 9.2 us
  starting transfers between devices: 72.5 us -> 10.2 us
  local copies, waits for them, and re-layouts: 62.9 us -> 8.15 us
  loops' own time: 29.5 us -> 0 us
  Pallas kernels: 0 us -> 20.2 us
  matrix products: 24.2 us -> 6 us
    psum x1, waiting for transfers between devices: 87.5 us -> 340 us  [local(): lax.psum((self_weight, neigh_weight, bias_part), ('row', 'edge'))]
    reduce_scatter x2, waiting for transfers between devices: 213 us -> 37.5 us  [the longest x1 20.1 us: local(): lax.psum_scatter(joined, 'edge', scatter_dimension=0, tiled=True)]
    psum x1, blocking collectives: 252 us -> 138 us  [local(): lax.psum((self_weight, neigh_weight, bias_part), ('row', 'edge'))]
    ppermute x2 -> x4, starting transfers between devices: 65.1 us -> 9.91 us  [passed_along(): lax.ppermute(array, axis, [(i, (i + by) % size) for i in range(size)])]
    scatter-add x4 -> x0, other arithmetic: 44.7 us -> none  [the longest x2 27.2 us: backward_work(): return current.at[col_grp].add(prod * live[:, None, None])]
    ppermute x2 -> x4, waiting for transfers between devices: 15.3 us -> 49 us  [passed_along(): lax.ppermute(array, axis, [(i, (i + by) % size) for i in range(size)])]
    another operation x24 -> x0, loops' own time: 29.5 us -> none  [the longest x1 14.6 us: local(): lax.scan(forward_step, initial, (tile_groups, row_groups, col_groups, sta...]
    unnamed x15 -> x28, local copies, waits for them, and re-layouts: 31.8 us -> 4.67 us
  transfers between devices with their start and end apart: 10 -> 10, of which waited for: 8 -> 9; matrix products, arithmetic and copies ran while one was open for 10% -> 2% of each run, Pallas kernels for 0% -> 0%
where the time goes in v1:
time: 726 us; the launch traced here: 725 us
  waiting for transfers between devices  499 us (69%)
  blocking collectives  157 us (22%)
  Pallas kernels  20.2 us (3%)
  between operations  14.9 us (2%)
  starting transfers between devices  10.2 us (1%)
  other arithmetic  9.2 us (1%)
  local copies, waits for them, and re-layouts  8.15 us (1%)
    psum x1, waiting for transfers between devices, local(): lax.psum((self_weight, neigh_weight, bias_part), ('row', 'edge'))  340 us
    psum x1, blocking collectives, local(): lax.psum((self_weight, neigh_weight, bias_part), ('row', 'edge'))  138 us
    ppermute x4, waiting for transfers between devices, passed_along(): lax.ppermute(array, axis, [(i, (i + by) % size) for i in range(size)])  49 us
    reduce_scatter x1, waiting for transfers between devices, local(): lax.psum_scatter(self_back, 'col', scatter_dimension=1, tiled=True)  26.3 us
    reduce_scatter x1, waiting for transfers between devices, local(): lax.psum_scatter(agg_back, 'col', scatter_dimension=1, tiled=True)  25.5 us
    all_gather x1, waiting for transfers between devices, local(): grads = lax.all_gather(flipped, 'edge', axis=0, tiled=True)  20.6 us
    reduce_scatter x1, waiting for transfers between devices, local(): lax.psum_scatter(joined, 'edge', scatter_dimension=0, tiled=True)  20.1 us
    reduce_scatter x1, waiting for transfers between devices, local(): lax.psum_scatter(partial.reshape(rows_dev, half), 'edge', scatter_dimensi...  17.4 us
  transfers between devices with their start and end apart: 10, of which 9 were waited for; matrix products, arithmetic and copies ran while one was open for 2% of the time, Pallas kernels for 0%

profile of v1, /device:TPU:1, one launch (start us, length us, event | category | flops | bytes accessed | tf_op | source)
XLA Modules:
  0.0 725.2 jit_solution(7654835172474558661)
XLA Ops:
  7.2 0.0 reduce-scatter.5.cloned.1.call-start
  7.2 2.1 collective-permute-start
  9.3 4.8 collective-permute-start.1
  14.8 22.4 %collective-permute-done.before = bf16[32,128,128]{2,1,0:T(8,128)(2,1)S(1)} collective-permute-done((bf16[32,128,128]{2,1,0:T(8,128)(2,1)}, bf16[32,128,128]{2,1,0:T(8,128)(2,1)S(1)}, u32[]{:S(2)}, u32[]{:S(2)}) %collective-permute-start) | collective-permute-done | bytes 1048608 | tf_op jit(solution)/shard_map/ppermute | solution.py:20
  37.2 1.2 copy-done.1
  38.4 0.7 copy-done.3
  39.1 0.7 copy-done.5
  39.8 10.6 %forward_sum.1 = bf16[32,128,128]{2,1,0:T(8,128)(2,1)} custom-call(s32[704]{0:T(1024)S(1)} %copy-done.3, s32[704]{0:T(1024)S(1)} %copy-done.5, s32[1]{0:T(128)S(6)} %copy.20.count_ref, bf16[32,128,128]{2,1,0:T(8,128)(2,1)S(1)} %collective-permute-done.before, bf16[32,128,128]{2,1,0:T(8,128)(2,1)S(1)} %bitcast.23, ...), custom_call_target="tpu_custom_call" | custom-call | flops 2952790016 | bytes 23068672 | tf_op jit(solution)/shard_map/forward_sum/pallas_call | solution.py:98
  50.4 0.0 reduce-scatter.5.cloned.1.call-update
  50.4 0.0 reduce-scatter.9.cloned.1.call-start
  50.5 1.0 constant_dynamic-slice_fusion
  51.4 8.8 %all_gather.9 = bf16[1024,256]{1,0:T(8,128)(2,1)S(1)} all-gather(bf16[1024,128]{1,0:T(8,128)(2,1)S(1)} %constant_dynamic-slice_fusion), channel_id=1, replica_groups=mesh['row'=16,'col'=2,'edge'=4] {'col'}, dimensions={1}, use_global_device_ids=true | all-gather | bytes 786432 | tf_op jit(solution)/shard_map/all_gather | solution.py:145
  60.3 0.8 copy-done.7
  61.1 0.3 fusion.3
  61.3 17.4 %reduce-scatter.5.cloned.1.call-done = bf16[1024,128]{1,0:T(8,128)(2,1)} async-done(((bf16[4096,128]{1,0:T(8,128)(2,1)}), bf16[1024,128]{1,0:T(8,128)(2,1)}) %reduce-scatter.5.cloned.1.call-update) | async-done | bytes 262160 | tf_op jit(solution)/shard_map/reduce_scatter | solution.py:147
  78.7 10.3 %all_gather.10 = bf16[1024,256]{1,0:T(8,128)(2,1)S(1)} all-gather(bf16[1024,128]{1,0:T(8,128)(2,1)} %reduce-scatter.5.cloned.1.call-done), channel_id=1, replica_groups=mesh['row'=16,'col'=2,'edge'=4] {'col'}, dimensions={1}, use_global_device_ids=true | all-gather | bytes 786432 | tf_op jit(solution)/shard_map/all_gather | solution.py:148
  89.1 1.2 fusion.1
  90.2 1.3 fusion.5
  91.5 0.0 reduce-scatter.9.cloned.1.call-update
  91.5 0.0 all-gather.2.cloned.1.call-start
  91.6 25.5 %reduce-scatter.9.cloned.1.call-done = f32[1024,128]{1,0:T(8,128)} async-done(((f32[1024,256]{1,0:T(8,128)}), f32[1024,128]{1,0:T(8,128)}) %reduce-scatter.9.cloned.1.call-update) | async-done | bytes 524304 | tf_op jit(solution)/shard_map/reduce_scatter | solution.py:171
  117.1 1.1 convert_element_type.28
  118.2 0.9 copy.16
  119.1 0.0 all-reduce.3.cloned.1.call-start
  119.1 20.6 %all-gather.2.cloned.1.call-done.grads = bf16[32,128,128]{2,1,0:T(8,128)(2,1)} async-done(((bf16[8,128,128]{2,1,0:T(8,128)(2,1)}), bf16[32,128,128]{2,1,0:T(8,128)(2,1)}) %all-gather.2.cloned.1.call-update) | async-done | bytes 1048592 | tf_op jit(solution)/shard_map/all_gather | solution.py:174
  139.7 1.2 copy-done.2
  141.0 9.7 %backward_sum.1 = bf16[96,128,128]{2,1,0:T(8,128)(2,1)S(1)} custom-call(s32[704]{0:T(1024)S(1)} %copy-done.4, s32[704]{0:T(1024)S(1)} %copy-done.6, s32[1]{0:T(128)S(6)} %copy.20.count_ref, bf16[32,128,128]{2,1,0:T(8,128)(2,1)S(1)} %copy-done.2, bf16[704,128,128]{2,1,0:T(8,128)(2,1)} %tiles.3), custom_call_target="tpu_custom_call" | custom-call | flops 2952790016 | bytes 23068672 | tf_op jit(solution)/shard_map/backward_sum/pallas_call | solution.py:118
  150.7 1.4 fusion.2
  152.1 3.0 collective-permute-start.2
  155.1 1.0 fusion.7
  156.1 1.0 fusion.6
  157.1 0.0 all-reduce.3.cloned.1.call-update
  157.1 0.0 reduce-scatter.11.cloned.1.call-start
  157.2 21.1 %collective-permute-done.2 = bf16[32,128,128]{2,1,0:T(8,128)(2,1)} collective-permute-done((bf16[32,128,128]{2,1,0:T(8,128)(2,1)}, bf16[32,128,128]{2,1,0:T(8,128)(2,1)}, u32[]{:S(2)}, u32[]{:S(2)}) %collective-permute-start.2) | collective-permute-done | bytes 1048608 | tf_op jit(solution)/shard_map/ppermute | solution.py:20
  178.2 5.6 collective-permute-done.3
  183.8 3.1 add_convert_fusion
  186.9 0.0 reduce-scatter.11.cloned.1.call-update
  186.9 0.0 reduce-scatter.7.cloned.1.call-start
  187.0 1.3 fusion.4
  188.3 138.3 %psum.23 = f32[128]{0:T(128)S(1)} all-reduce(f32[128]{0:T(128)S(1)} %get-tuple-element.7), channel_id=1, replica_groups=mesh['row'=16,'col'=2,'edge'=4] {'row','edge'}, use_global_device_ids=true, to_apply=%region_7.0 | all-reduce | flops 128 | bytes 1024 | tf_op jit(solution)/shard_map/psum | solution.py:162
  326.6 0.5 broadcast_multiply_fusion.2
  327.1 340.1 %all-reduce.3.cloned.1.call-done = (f32[256,128]{1,0:T(8,128)}, f32[256,128]{1,0:T(8,128)}) async-done(((f32[256,128]{1,0:T(8,128)}, f32[256,128]{1,0:T(8,128)}), (f32[256,128]{1,0:T(8,128)}, f32[256,128]{1,0:T(8,128)})) %all-reduce.3.cloned.1.call-update) | async-done | bytes 262160 | tf_op jit(solution)/shard_map/psum | solution.py:162
  667.2 1.7 broadcast_multiply_fusion
  668.9 20.1 %reduce-scatter.11.cloned.1.call-done = bf16[8,128,128]{2,1,0:T(8,128)(2,1)} async-done(((bf16[32,128,128]{2,1,0:T(8,128)(2,1)}), bf16[8,128,128]{2,1,0:T(8,128)(2,1)}) %reduce-scatter.11.cloned.1.call-update) | async-done | bytes 262160 | tf_op jit(solution)/shard_map/reduce_scatter | solution.py:179
  689.0 1.0 convert_bitcast_fusion
  690.0 0.2 copy.17
  690.2 26.3 %reduce-scatter.7.cloned.1.call-done = f32[1024,128]{1,0:T(8,128)} async-done(((f32[1024,256]{1,0:T(8,128)}), f32[1024,128]{1,0:T(8,128)}) %reduce-scatter.7.cloned.1.call-update) | async-done | bytes 524304 | tf_op jit(solution)/shard_map/reduce_scatter | solution.py:170
  716.5 1.9 bitcast_add_fusion
  (27 shorter events, 0.1 us)
Async XLA Ops:
  7.2 81.9 %copy-start = (bf16[256,128]{1,0:T(8,128)(2,1)S(1)}, bf16[256,128]{1,0:T(8,128)(2,1)}, u32[]{:S(2)}) copy-start(bf16[256,128]{1,0:T(8,128)(2,1)} %param.15) | copy-start | bytes 196612
  7.2 71.6 %reduce-scatter.5.cloned.1.call-start = ((), (), s32[]{:S(2)}) async-start(), calls=%async_computation.4 | async-start | bytes 1310720 | tf_op jit(solution)/shard_map/reduce_scatter | solution.py:147
  7.2 29.9 %collective-permute-start = (bf16[32,128,128]{2,1,0:T(8,128)(2,1)}, bf16[32,128,128]{2,1,0:T(8,128)(2,1)S(1)}, u32[]{:S(2)}, u32[]{:S(2)}) collective-permute-start(bf16[32,128,128]{2,1,0:T(8,128)(2,1)} %bitcast.21), channel_id=1, source_target_pairs={{0,8},{8,16},{16,24},{24,32},{32,40},{40,48},{48,56},{56,64},{64,7... | collective-permute-start | bytes 3145736 | tf_op jit(solution)/shard_map/ppermute | solution.py:20
  9.3 27.8 %collective-permute-start.1 = (bf16[32,128,128]{2,1,0:T(8,128)(2,1)}, bf16[32,128,128]{2,1,0:T(8,128)(2,1)S(1)}, u32[]{:S(2)}, u32[]{:S(2)}) collective-permute-start(bf16[32,128,128]{2,1,0:T(8,128)(2,1)} %bitcast.22), channel_id=1, source_target_pairs={{0,120},{8,0},{16,8},{24,16},{32,24},{40,32},{48,40},{56,48},{64,5... | collective-permute-start | bytes 3145736 | tf_op jit(solution)/shard_map/ppermute | solution.py:20
  37.2 1.2 copy-start.1
  38.4 0.7 copy-start.3
  39.1 0.7 copy-start.5
  50.3 10.7 %copy-start.11 = (bf16[256,128]{1,0:T(8,128)(2,1)S(1)}, bf16[256,128]{1,0:T(8,128)(2,1)}, u32[]{:S(2)}) copy-start(bf16[256,128]{1,0:T(8,128)(2,1)} %param.14) | copy-start | bytes 196612
  50.4 38.7 %copy-start.12 = (bf16[1024,128]{1,0:T(8,128)(2,1)S(1)}, bf16[1024,128]{1,0:T(8,128)(2,1)}, u32[]{:S(2)}) copy-start(bf16[1024,128]{1,0:T(8,128)(2,1)} %param.17) | copy-start | bytes 786436
  50.4 38.7 %copy-start.13 = (f32[128]{0:T(128)S(1)}, f32[128]{0:T(128)}, u32[]{:S(2)}) copy-start(f32[128]{0:T(128)} %param.16) | copy-start | bytes 1540
  50.4 66.7 %reduce-scatter.9.cloned.1.call-start = ((), (), s32[]{:S(2)}) async-start(), calls=%async_computation.6 | async-start | bytes 1572864 | tf_op jit(solution)/shard_map/reduce_scatter | solution.py:171
  60.3 0.8 copy-start.7
  89.0 2.5 copy-start.9
  90.2 49.5 %copy-start.4 = (s32[704]{0:T(1024)S(1)}, s32[704]{0:T(1024)}, u32[]{:S(2)}) copy-start(s32[704]{0:T(1024)} %rows.3) | copy-start | bytes 8452
  90.2 49.5 %copy-start.6 = (s32[704]{0:T(1024)S(1)}, s32[704]{0:T(1024)}, u32[]{:S(2)}) copy-start(s32[704]{0:T(1024)} %cols.3) | copy-start | bytes 8452
  91.5 48.2 %all-gather.2.cloned.1.call-start = ((), (), s32[]{:S(2)}) async-start(), calls=%async_computation.7 | async-start | bytes 1310720 | tf_op jit(solution)/shard_map/all_gather | solution.py:174
  119.1 548.1 %all-reduce.3.cloned.1.call-start = ((), (), s32[]{:S(2)}) async-start(), calls=%async_computation.9 | async-start | bytes 524288 | tf_op jit(solution)/shard_map/psum | solution.py:162
  139.7 1.2 copy-start.2
  150.6 4.4 copy-start.10
  150.7 5.4 copy-start.8
  152.1 26.1 %collective-permute-start.2 = (bf16[32,128,128]{2,1,0:T(8,128)(2,1)}, bf16[32,128,128]{2,1,0:T(8,128)(2,1)}, u32[]{:S(2)}, u32[]{:S(2)}) collective-permute-start(bf16[32,128,128]{2,1,0:T(8,128)(2,1)} %get-tuple-element.9), channel_id=1, source_target_pairs={{0,120},{8,0},{16,8},{24,16},{32,24},{40,32},{48,40},{56,48},{64,5... | collective-permute-start | bytes 3145736 | tf_op jit(solution)/shard_map/ppermute | solution.py:20
  155.1 28.7 %collective-permute-start.3 = (bf16[32,128,128]{2,1,0:T(8,128)(2,1)}, bf16[32,128,128]{2,1,0:T(8,128)(2,1)}, u32[]{:S(2)}, u32[]{:S(2)}) collective-permute-start(bf16[32,128,128]{2,1,0:T(8,128)(2,1)} %get-tuple-element.10), channel_id=1, source_target_pairs={{0,8},{8,16},{16,24},{24,32},{32,40},{40,48},{48,56},{56,64},{64,7... | collective-permute-start | bytes 3145736 | tf_op jit(solution)/shard_map/ppermute | solution.py:20
  157.1 531.9 %reduce-scatter.11.cloned.1.call-start = ((), (), s32[]{:S(2)}) async-start(), calls=%async_computation.8 | async-start | bytes 1310720 | tf_op jit(solution)/shard_map/reduce_scatter | solution.py:179
  186.9 529.6 %reduce-scatter.7.cloned.1.call-start = ((), (), s32[]{:S(2)}) async-start(), calls=%async_computation.5 | async-start | bytes 1572864 | tf_op jit(solution)/shard_map/reduce_scatter | solution.py:170
Sparse Core Ops, SparseCore 0:
  50.5 28.1 reduce-scatter.4
  91.7 25.3 reduce-scatter.8
  119.2 20.4 all-gather.1
  157.2 509.9 all-reduce.2
  669.6 19.3 reduce-scatter.10
  691.2 25.2 reduce-scatter.6

commit v2 on v1

--- a/solution.py
+++ b/solution.py
@@ -15,9 +15,42 @@
 MIB = 1024 * 1024
 
 
-def passed_along(array, axis, by):
-    size = lax.axis_size(axis)
-    return lax.ppermute(array, axis, [(i, (i + by) % size) for i in range(size)])
+MESH = pl.DeviceIdType.MESH
+
+
+def place():
+    row, col, edge = (lax.axis_index(name) for name in ("row", "col", "edge"))
+    return row, col, edge, lax.rem(edge, 2), lax.div(edge, 2)
+
+
+def greet(peers):
+    barrier = pltpu.get_barrier_semaphore()
+    for peer in peers:
+        pl.semaphore_signal(barrier, inc=1, device_id=peer, device_id_type=MESH)
+    pl.semaphore_wait(barrier, len(peers))
+
+
+class Sender:
+    def __init__(self, send_sems, recv_sems):
+        self.send_sems, self.recv_sems, self.used = send_sems, recv_sems, []
+
+    def __call__(self, src, dst, peer):
+        index = len(self.used)
+        copy = pltpu.make_async_remote_copy(
+            src_ref=src,
+            dst_ref=dst,
+            send_sem=self.send_sems.at[index],
+            recv_sem=self.recv_sems.at[index],
+            device_id=peer,
+            device_id_type=MESH,
+        )
+        copy.start()
+        self.used.append(copy)
+        return copy
+
+    def finish(self):
+        for copy in self.used:
+            copy.wait_send()
 
 
 def tile_loop(count, rows, cols, tiles, ring, sems, total, product, target):
@@ -131,55 +164,422 @@
     )(tile_rows, tile_cols, tile_count, grads, tiles)
 
 
+HALO_CHUNKS = 4
+
+
+def halo_kernel(
+    features, cotangent, w_self, w_neigh, bias,
+    before, after, own_far, cot_far, w_self_far, w_neigh_far, bias_far,
+    send_sems, recv_sems,
+):
+    row, col, edge, core, _ = place()
+    rows = lax.axis_size("row")
+    up, down = {"row": lax.rem(row + 1, rows)}, {"row": lax.rem(row + rows - 1, rows)}
+    twin, partner = {"edge": edge + 1 - 2 * core}, {"col": 1 - col}
+    blocks = features.shape[0]
+    share = blocks // 8
+    greet([up, down, twin, partner])
+    send = Sender(send_sems, recv_sems)
+    step = blocks // 2 // HALO_CHUNKS
+    parts = [pl.ds(core * (blocks // 2) + i * step, step) for i in range(HALO_CHUNKS)]
+    arriving = []
+    for part in parts:
+        arriving.append(
+            (part, before, send(features.at[part], before.at[part], up))
+        )
+        arriving.append(
+            (part, after, send(features.at[part], after.at[part], down))
+        )
+    theirs = pl.ds(edge * 2 * share + (1 - col) * share, share)
+    theirs_cot = pl.ds((1 - col) * share, share)
+    swaps = [
+        send(features.at[theirs], own_far, partner),
+        send(cotangent.at[theirs_cot], cot_far, partner),
+        send(w_self, w_self_far, partner),
+        send(w_neigh, w_neigh_far, partner),
+        send(bias, bias_far, partner),
+    ]
+    handed = []
+    for part, side, copy in arriving:
+        copy.wait_recv()
+        handed.append(send(side.at[part], side.at[part], twin))
+    for copy in swaps + handed:
+        copy.wait_recv()
+    send.finish()
+
+
+def exchange_inputs(features, cotangent, w_self, w_neigh, bias):
+    blocks, size, half = features.shape
+    share = blocks // 8
+    shapes = [features, features] + [
+        jax.ShapeDtypeStruct((share, size, half), BF16),
+        jax.ShapeDtypeStruct((share, size, half), BF16),
+        w_self, w_neigh, bias,
+    ]
+    copies = 4 * HALO_CHUNKS + 5
+    return pl.pallas_call(
+        halo_kernel,
+        out_shape=[jax.ShapeDtypeStruct(s.shape, s.dtype) for s in shapes],
+        in_specs=[ANY] * 5,
+        out_specs=[ANY] * 7,
+        scratch_shapes=[pltpu.SemaphoreType.DMA((copies,)), pltpu.SemaphoreType.DMA((copies,))],
+        compiler_params=pltpu.CompilerParams(collective_id=1, has_side_effects=True),
+        name="exchange_inputs",
+    )(features, cotangent, w_self, w_neigh, bias)
+
+
+def mid_kernel(
+    partial, features, own_far, cotangent, cot_far, w_self, w_neigh, w_self_far, w_neigh_far, bias, bias_far,
+    grads, out_near, self_near, weight_near, bias_near, far,
+    got_core, sent_pair, kept, got_pair, sent_col, got_col, own, cot, weights, sent_grads,
+    local_sems, send_sems, recv_sems,
+):
+    row, col, edge, core, pair_side = place()
+    other = 1 - col
+    twin, pair, partner = {"edge": edge + 1 - 2 * core}, {"edge": lax.rem(edge + 2, 4)}, {"col": other}
+    diagonal = {"edge": lax.rem(edge + 2, 4), "col": other}
+    blocks, size, half = partial.shape
+    share = blocks // 8
+    near_rows = own_far.shape[0] * size
+    local = [
+        pltpu.make_async_copy(features.at[pl.ds(edge * 2 * share + col * share, share)], own, local_sems.at[0]),
+        pltpu.make_async_copy(cotangent.at[pl.ds(col * share, share)], cot, local_sems.at[1]),
+    ]
+    for copy in local:
+        copy.start()
+    greet([twin, pair, partner, diagonal])
+    send = Sender(send_sems, recv_sems)
+
+    def piece(side, on_core, column):
+        return pl.ds((2 * side + on_core) * 2 * share + column * share, share)
+
+    order = [(1 - pair_side, other), (1 - pair_side, col), (pair_side, other), (pair_side, col)]
+    to_twin = [
+        send(partial.at[piece(side, 1 - core, column)], got_core.at[i], twin)
+        for i, (side, column) in enumerate(order)
+    ]
+    near_w, far_w = pl.ds(pl.multiple_of(col * half, half), half), pl.ds(pl.multiple_of(other * half, half), half)
+    for k, (near, away) in enumerate(((w_self, w_self_far), (w_neigh, w_neigh_far))):
+        for j, rows in enumerate((near_w, far_w)):
+            at = pl.ds((2 * k + j) * half, half)
+            weights[at, :half] = near[rows, :]
+            weights[at, half:] = away[rows, :]
+
+    def summed(i):
+        to_twin[i].wait_recv()
+        side, column = order[i]
+        return partial[piece(side, core, column)].astype(F32) + got_core[i].astype(F32)
+
+    to_pair = []
+    for i in range(2):
+        sent_pair[i] = summed(i).astype(BF16)
+        to_pair.append(send(sent_pair.at[i], got_pair.at[i], pair))
+    for i in range(2):
+        kept[i] = summed(2 + i)
+    to_pair[0].wait_recv()
+    sent_col[...] = (kept[0] + got_pair[0].astype(F32)).astype(BF16)
+    to_partner = send(sent_col, got_col, partner)
+    for copy in local:
+        copy.wait()
+    to_pair[1].wait_recv()
+    agg_near = (kept[1] + got_pair[1].astype(F32)).astype(BF16)
+    to_partner.wait_recv()
+
+    def flat(blocks_of):
+        return blocks_of.reshape(near_rows, half)
+
+    mixed = jnp.concatenate(
+        [flat(own[...]), flat(own_far[...]), flat(agg_near), flat(got_col[...])], axis=1
+    )
+    pre = jnp.dot(mixed, weights[...], preferred_element_type=F32) + jnp.concatenate(
+        [bias[...], bias_far[...]], axis=1
+    )
+    sigm = jax.nn.sigmoid(pre)
+    cot_full = jnp.concatenate([flat(cot[...]), flat(cot_far[...])], axis=1).astype(F32)
+    grad_pre = cot_full * sigm * (1.0 + pre * (1.0 - sigm))
+    grad_low = grad_pre.astype(BF16)
+    over_cols = (((1,), (1,)), ((), ()))
+    agg_back = lax.dot_general(
+        weights[2 * half :, :], grad_low, over_cols, preferred_element_type=F32
+    ).astype(BF16)
+    mine = pl.ds(edge * 2 * share + col * share, share)
+    for b in range(share):
+        grads[edge * 2 * share + col * share + b] = agg_back[:half, b * size : (b + 1) * size]
+        sent_grads[b] = agg_back[half:, b * size : (b + 1) * size]
+    crossing = [
+        send(sent_grads, grads.at[mine], diagonal),
+        send(sent_grads, grads.at[mine], partner),
+        send(grads.at[mine], grads.at[mine], pair),
+    ]
+    handed = [send(grads.at[mine], grads.at[mine], twin)]
+
+    output = (pre * sigm).astype(BF16)
+    out_near[...] = output[:, :half]
+    far[:near_rows] = output[:, half:]
+    self_back = lax.dot_general(grad_low, weights[: 2 * half, :], over_cols, preferred_element_type=F32)
+    self_near[...] = self_back[:, :half]
+    far[near_rows : 2 * near_rows] = self_back[:, half:].astype(BF16)
+    parts = lax.dot_general(mixed, grad_low, (((0,), (0,)), ((), ())), preferred_element_type=F32)
+    for k in range(2):
+        for j, start in enumerate((col * half, other * half)):
+            at = (2 * k + j) * half
+            weight_near[pl.ds(pl.multiple_of(2 * k * half + start, half), half), :] = parts[at : at + half, :half]
+            far[pl.ds(pl.multiple_of(2 * near_rows + 2 * k * half + start, half), half), :] = (
+                parts[at : at + half, half:].astype(BF16)
+            )
+    bias_parts = jnp.sum(grad_pre.reshape(near_rows // 16, 16, 2 * half), axis=0)
+    bias_near[...] = bias_parts[:, :half]
+    far[2 * near_rows + 4 * half :] = bias_parts[:, half:].astype(BF16)
+
+    far_edge = lax.rem(edge + 2, 4)
+    homes = [
+        pl.ds(far_edge * 2 * share + other * share, share),
+        pl.ds(edge * 2 * share + other * share, share),
+        pl.ds(far_edge * 2 * share + col * share, share),
+    ]
+    for k in (1, 2, 0):
+        crossing[k].wait_recv()
+        handed.append(send(grads.at[homes[k]], grads.at[homes[k]], twin))
+    for copy in handed:
+        copy.wait_recv()
+    send.finish()
+
+
+def middle(partial, features, own_far, cotangent, cot_far, w_self, w_neigh, w_self_far, w_neigh_far, bias, bias_far):
+    blocks, size, half = partial.shape
+    share = blocks // 8
+    rows = share * size
+    copies = 4 + 2 + 1 + 3 + 4
+    piece = (share, size, half)
+    return pl.pallas_call(
+        mid_kernel,
+        out_shape=[
+            jax.ShapeDtypeStruct((blocks, half, size), BF16),
+            jax.ShapeDtypeStruct((rows, half), BF16),
+            jax.ShapeDtypeStruct((rows, half), F32),
+            jax.ShapeDtypeStruct((4 * half, half), F32),
+            jax.ShapeDtypeStruct((16, half), F32),
+            jax.ShapeDtypeStruct((2 * rows + 4 * half + 16, half), BF16),
+        ],
+        in_specs=[VMEM, ANY, VMEM, ANY] + [VMEM] * 7,
+        out_specs=[VMEM] * 6,
+        scratch_shapes=[
+            pltpu.VMEM((4,) + piece, BF16),
+            pltpu.VMEM((2,) + piece, BF16),
+            pltpu.VMEM((2,) + piece, F32),
+            pltpu.VMEM((2,) + piece, BF16),
+            pltpu.VMEM(piece, BF16),
+            pltpu.VMEM(piece, BF16),
+            pltpu.VMEM(piece, BF16),
+            pltpu.VMEM(piece, BF16),
+            pltpu.VMEM((4 * half, 2 * half), BF16),
+            pltpu.VMEM((share, half, size), BF16),
+            pltpu.SemaphoreType.DMA((2,)),
+            pltpu.SemaphoreType.DMA((copies,)),
+            pltpu.SemaphoreType.DMA((copies,)),
+        ],
+        compiler_params=pltpu.CompilerParams(collective_id=2, has_side_effects=True, vmem_limit_bytes=40 * MIB),
+        name="middle",
+    )(partial, features, own_far, cotangent, cot_far, w_self, w_neigh, w_self_far, w_neigh_far, bias, bias_far)
+
+
+def final_kernel(
+    scale, back, out_near, self_near, weight_near, bias_near, far,
+    output, features_grad, w_self_grad, w_neigh_grad, bias_grad,
+    got_core, sent_row, kept, got_row, sent_pair, got_pair,
+    w_all, w_sent0, w_got0, w_sent1, w_got1, w_sent2, w_got2, w_sent3, w_got3, w_total, bias_sum,
+    send_sems, recv_sems,
+):
+    row, col, edge, core, side = place()
+    rows = lax.axis_size("row")
+    x, z = lax.rem(row, 4), lax.div(row, 4)
+    twin, pair = {"edge": edge + 1 - 2 * core}, {"edge": lax.rem(edge + 2, 4)}
+    up, down = {"row": lax.rem(row + 1, rows)}, {"row": lax.rem(row + rows - 1, rows)}
+    along_x = [lax.rem(x + j, 4) for j in (1, 2, 3)]
+    along_z = [lax.rem(z + j, 4) for j in (1, 2, 3)]
+    x_peers = [{"row": z * 4 + to} for to in along_x]
+    z_peers = [{"row": to * 4 + x} for to in along_z]
+    greet([twin, pair, up, down] + x_peers + z_peers)
+    send = Sender(send_sems, recv_sems)
+    share = back.shape[0] // 3 // 4
+    near_rows, half = out_near.shape
+    blocks = back.shape[0] // 3
+
+    def piece(part, at_side, on_core):
+        return pl.ds(part * blocks + (2 * at_side + on_core) * share, share)
+
+    order = [(0, 1 - side), (2, 1 - side), (0, side), (2, side), (1, 1 - side), (1, side)]
+    to_twin = [
+        send(back.at[piece(part, at, 1 - core)], got_core.at[i], twin) for i, (part, at) in enumerate(order)
+    ]
+
+    top = 4 * half
+    w_all[...] = weight_near[...] + far[2 * near_rows : 2 * near_rows + top].astype(F32)
+    bias_sum[...] = bias_near[...] + far[2 * near_rows + top :].astype(F32)
+    w_sent0[: top // 2] = w_all[pl.ds(pl.multiple_of((1 - core) * (top // 2), 8), top // 2), :]
+    w_sent0[top // 2 :] = bias_sum[...]
+    w_step = send(w_sent0, w_got0, twin)
+
+    def summed(i):
+        to_twin[i].wait_recv()
+        part, at = order[i]
+        return back[piece(part, at, core)].astype(F32) + got_core[i].astype(F32)
+
+    to_row = []
+    for i in range(4):
+        sent_row[i] = summed(i).astype(BF16)
+        to_row.append(send(sent_row.at[i], got_row.at[i], down if i % 2 == 0 else up))
+
+    w_step.wait_recv()
+    start = pl.multiple_of(core * (top // 2), 8)
+    w_all[pl.ds(start, top // 2), :] += w_got0[: top // 2]
+    bias_sum[...] += w_got0[top // 2 :]
+    w_sent1[: top // 4] = w_all[pl.ds(pl.multiple_of(start + (1 - side) * (top // 4), 8), top // 4), :]
+    w_sent1[top // 4 :] = bias_sum[...]
+    w_step = send(w_sent1, w_got1, pair)
+    for i in range(2):
+        kept[i] = summed(4 + i)
+
+    w_step.wait_recv()
+    start = pl.multiple_of(start + side * (top // 4), 8)
+    w_all[pl.ds(start, top // 4), :] += w_got1[: top // 4]
+    bias_sum[...] += w_got1[top // 4 :]
+
+    def spread(start, many, sent, got, targets, peers):
+        steps = []
+        for j in range(3):
+            sent[j, :many] = w_all[pl.ds(pl.multiple_of(start + targets[j] * many, 8), many), :]
+            sent[j, many:] = bias_sum[...]
+            steps.append(send(sent.at[j], got.at[j], peers[j]))
+        return steps
+
+    def collect(start, many, got, steps):
+        for j in range(3):
+            steps[j].wait_recv()
+        at = pl.ds(start, many)
+        w_all[at, :] += got[0, :many] + got[1, :many] + got[2, :many]
+        bias_sum[...] += got[0, many:] + got[1, many:] + got[2, many:]
+
+    many = top // 16
+    steps = spread(start, many, w_sent2, w_got2, along_x, x_peers)
+    start = pl.multiple_of(start + x * many, 8)
+    collect(start, many, w_got2, steps)
+    many = top // 64
+    steps = spread(start, many, w_sent3, w_got3, along_z, z_peers)
+    start = pl.multiple_of(start + z * many, 8)
+    collect(start, many, w_got3, steps)
+    w_total[pl.ds(start, many), :] = w_all[pl.ds(start, many), :]
+    bias_grad[...] = jnp.sum(bias_sum[...], axis=0, keepdims=True) * scale
+    at = pl.ds(start, many)
+    steps = [send(w_total.at[at], w_total.at[at], peer) for peer in z_peers]
+
+    for i in range(2):
+        to_row[i].wait_recv()
+    sent_pair[...] = (kept[0] + got_row[0].astype(F32) + got_row[1].astype(F32)).astype(BF16)
+    to_pair = send(sent_pair, got_pair, pair)
+
+    for step in steps:
+        step.wait_recv()
+    start = pl.multiple_of(start - z * many, 8)
+    many = top // 16
+    at = pl.ds(start, many)
+    steps = [send(w_total.at[at], w_total.at[at], peer) for peer in x_peers]
+    for step in steps:
+        step.wait_recv()
+    start = pl.multiple_of(start - x * many, 8)
+    at = pl.ds(start, top // 4)
+    step = send(w_total.at[at], w_total.at[at], pair)
+
+    near, away = pl.multiple_of(col * near_rows, 8), pl.multiple_of((1 - col) * near_rows, 8)
+    output[pl.ds(pl.multiple_of(near, 16), near_rows), :] = out_near[...]
+    output[pl.ds(pl.multiple_of(away, 16), near_rows), :] = far[:near_rows]
+    features_grad[pl.ds(near, near_rows), :] = self_near[...]
+    features_grad[pl.ds(away, near_rows), :] = far[near_rows : 2 * near_rows].astype(F32)
+
+    step.wait_recv()
+    start = pl.multiple_of(start - side * (top // 4), 8)
+    at = pl.ds(start, top // 2)
+    step = send(w_total.at[at], w_total.at[at], twin)
+
+    for i in range(2, 4):
+        to_row[i].wait_recv()
+    kept[1] += got_row[2].astype(F32) + got_row[3].astype(F32)
+    to_pair.wait_recv()
+    size = back.shape[2]
+    for b in range(share):
+        features_grad[b * size : (b + 1) * size, :] += (kept[1, b] + got_pair[b].astype(F32)).T
+    step.wait_recv()
+    w_self_grad[...] = w_total[: top // 2] * scale
+    w_neigh_grad[...] = w_total[top // 2 :] * scale
+    send.finish()
+
+
+def finish(scale, back, out_near, self_near, weight_near, bias_near, far):
+    share, half, size = back.shape[0] // 12, back.shape[1], back.shape[2]
+    rows = out_near.shape[0]
+    top = weight_near.shape[0]
+    copies = 6 + 4 + 1 + 2 + 12 + 2
+    piece = (share, half, size)
+
+    def sent(lead, many):
+        return [pltpu.VMEM(lead + (many + 16, half), F32)] * 2
+
+    return pl.pallas_call(
+        functools.partial(final_kernel, scale),
+        out_shape=[
+            jax.ShapeDtypeStruct((2 * rows, half), BF16),
+            jax.ShapeDtypeStruct((2 * rows, half), F32),
+            jax.ShapeDtypeStruct((top // 2, half), F32),
+            jax.ShapeDtypeStruct((top // 2, half), F32),
+            jax.ShapeDtypeStruct((1, half), F32),
+        ],
+        in_specs=[VMEM] * 6,
+        out_specs=[VMEM] * 5,
+        scratch_shapes=[
+            pltpu.VMEM((6,) + piece, BF16),
+            pltpu.VMEM((4,) + piece, BF16),
+            pltpu.VMEM((2,) + piece, F32),
+            pltpu.VMEM((4,) + piece, BF16),
+            pltpu.VMEM(piece, BF16),
+            pltpu.VMEM(piece, BF16),
+            pltpu.VMEM((top, half), F32),
+            *sent((), top // 2),
+            *sent((), top // 4),
+            *sent((3,), top // 16),
+            *sent((3,), top // 64),
+            pltpu.VMEM((top, half), F32),
+            pltpu.VMEM((16, half), F32),
+            pltpu.SemaphoreType.DMA((copies,)),
+            pltpu.SemaphoreType.DMA((copies,)),
+        ],
+        compiler_params=pltpu.CompilerParams(collective_id=3, has_side_effects=True, vmem_limit_bytes=40 * MIB),
+        name="finish",
+    )(back, out_near, self_near, weight_near, bias_near, far)
+
+
 def local(features, tiles, tile_rows, tile_cols, tile_count, w_self, w_neigh, bias, cotangent):
     rows_dev, half = features.shape
     size = tiles.shape[1]
     blocks = rows_dev // size
-    share = rows_dev // lax.axis_size("edge")
     nodes = rows_dev * lax.axis_size("row")
-
-    own_blocks = features.reshape(blocks, size, half)
-    before = passed_along(own_blocks, "row", 1)
-    after = passed_along(own_blocks, "row", -1)
-    own = lax.dynamic_slice_in_dim(features, lax.axis_index("edge") * share, share, 0)
-    own_full = lax.all_gather(own, "col", axis=1, tiled=True)
-    partial = forward_sum(tile_rows, tile_cols, tile_count, before, own_blocks, after, tiles)
-    agg = lax.psum_scatter(partial.reshape(rows_dev, half), "edge", scatter_dimension=0, tiled=True)
-    agg_full = lax.all_gather(agg, "col", axis=1, tiled=True)
-    pre = (
-        jnp.dot(own_full, w_self, preferred_element_type=F32)
-        + jnp.dot(agg_full, w_neigh, preferred_element_type=F32)
-        + bias[None, :]
-    )
-    sigm = jax.nn.sigmoid(pre)
-    output = (pre * sigm).astype(BF16)
-    grad_pre = cotangent.astype(F32) * sigm * (1.0 + pre * (1.0 - sigm))
-    grad_low = grad_pre.astype(BF16)
-    over_rows = (((0,), (0,)), ((), ()))
-    self_weight = lax.dot_general(own_full, grad_low, over_rows, preferred_element_type=F32)
-    neigh_weight = lax.dot_general(agg_full, grad_low, over_rows, preferred_element_type=F32)
-    bias_part = jnp.sum(grad_pre, axis=0)
-    self_weight, neigh_weight, bias_total = lax.psum(
-        (self_weight, neigh_weight, bias_part), ("row", "edge")
-    )
     scale = 1.0 / math.sqrt(nodes)
-    over_cols = (((1,), (1,)), ((), ()))
-    self_back = lax.dot_general(grad_low, w_self, over_cols, preferred_element_type=F32)
-    agg_back = lax.dot_general(grad_low, w_neigh, over_cols, preferred_element_type=F32)
-    self_back, agg_back = (
-        lax.psum_scatter(self_back, "col", scatter_dimension=1, tiled=True),
-        lax.psum_scatter(agg_back, "col", scatter_dimension=1, tiled=True),
-    )
-    flipped = agg_back.astype(BF16).reshape(share // size, size, half).swapaxes(1, 2)
-    grads = lax.all_gather(flipped, "edge", axis=0, tiled=True)
-    parts = backward_sum(tile_rows, tile_cols, tile_count, grads, tiles).reshape(3, blocks, half, size)
-    from_after = passed_along(parts[0], "row", -1)
-    from_before = passed_along(parts[2], "row", 1)
-    joined = (parts[1].astype(F32) + from_after.astype(F32) + from_before.astype(F32)).astype(BF16)
-    neigh_back = lax.psum_scatter(joined, "edge", scatter_dimension=0, tiled=True)
-    neigh_back = neigh_back.astype(F32).swapaxes(1, 2).reshape(share, half)
-    features_grad = self_back + neigh_back
-    return (output, features_grad, self_weight * scale, neigh_weight * scale, bias_total * scale)
+
+    own = features.reshape(blocks, size, half)
+    cot = cotangent.reshape(-1, size, half)
+    bias_row = bias.reshape(1, half)
+    before, after, own_far, cot_far, w_self_far, w_neigh_far, bias_far = exchange_inputs(
+        own, cot, w_self, w_neigh, bias_row
+    )
+    partial = forward_sum(tile_rows, tile_cols, tile_count, before, own, after, tiles)
+    grads, out_near, self_near, weight_near, bias_near, far = middle(
+        partial, own, own_far, cot, cot_far, w_self, w_neigh, w_self_far, w_neigh_far, bias_row, bias_far
+    )
+    far = lax.ppermute(far, "col", [(0, 1), (1, 0)])
+    back = backward_sum(tile_rows, tile_cols, tile_count, grads, tiles)
+    output, features_grad, w_self_grad, w_neigh_grad, bias_grad = finish(
+        scale, back, out_near, self_near, weight_near, bias_near, far
+    )
+    return (output, features_grad, w_self_grad, w_neigh_grad, bias_grad.reshape(half))
 
 
 def solution(mesh):

time: 726 us -> 125 us (0.17)
  waiting for transfers between devices: 499 us -> 0.01 us
  blocking collectives: 157 us -> 0 us
  Pallas kernels: 20.2 us -> 113 us
  between operations: 14.9 us -> 1.52 us
  other arithmetic: 9.2 us -> 0 us
  starting transfers between devices: 10.2 us -> 1.5 us
    psum x1 -> x0, waiting for transfers between devices: 340 us -> none  [local(): lax.psum((self_weight, neigh_weight, bias_part), ('row', 'edge'))]
    psum x1 -> x0, blocking collectives: 138 us -> none  [local(): lax.psum((self_weight, neigh_weight, bias_part), ('row', 'edge'))]
    reduce_scatter x4 -> x0, waiting for transfers between devices: 89.3 us -> none  [the longest x1 26.3 us: local(): lax.psum_scatter(self_back, 'col', scatter_dimension=1, tiled=True)]
    pallas_call x0 -> x3, Pallas kernels: none -> 78.7 us  [the longest x1 32.1 us: finish(): pl.pallas_call(functools.partial(final_kernel, scale), out_shape=[jax.Sha...]
    ppermute x4 -> x1, waiting for transfers between devices: 49 us -> 0.01 us  [local(): far = lax.ppermute(far, 'col', [(0, 1), (1, 0)])]
    all_gather x1 -> x0, waiting for transfers between devices: 20.6 us -> none  [local(): grads = lax.all_gather(flipped, 'edge', axis=0, tiled=True)]
    all_gather x2 -> x0, blocking collectives: 19.1 us -> none  [the longest x1 10.3 us: local(): agg_full = lax.all_gather(agg, 'col', axis=1, tiled=True)]
    ppermute x4 -> x1, starting transfers between devices: 9.91 us -> 1.5 us  [local(): far = lax.ppermute(far, 'col', [(0, 1), (1, 0)])]
  transfers between devices with their start and end apart: 10 -> 1, of which waited for: 9 -> 0; matrix products, arithmetic and copies ran while one was open for 2% -> 0% of each run, Pallas kernels for 0% -> 14%
where the time goes in v2:
time: 125 us
  Pallas kernels  113 us (90%)
  local copies, waits for them, and re-layouts  8.41 us (7%)
  between operations  1.52 us (1%)
  starting transfers between devices  1.5 us (1%)
    pallas_call x1, Pallas kernels, finish(): pl.pallas_call(functools.partial(final_kernel, scale), out_shape=[jax.Sha...  32.1 us
    pallas_call x1, Pallas kernels, exchange_inputs(): pl.pallas_call(halo_kernel, out_shape=[jax.ShapeDtypeStruct(s.shape, s.dt...  24.8 us
    pallas_call x1, Pallas kernels, middle(): pl.pallas_call(mid_kernel, out_shape=[jax.ShapeDtypeStruct((blocks, half,...  21.9 us
    pallas_call x1, Pallas kernels, backward_sum(): pl.pallas_call(backward_kernel, out_shape=jax.ShapeDtypeStruct((3 * block...  17.7 us
    pallas_call x1, Pallas kernels, forward_sum(): pl.pallas_call(forward_kernel, out_shape=jax.ShapeDtypeStruct((blocks, si...  16.9 us
    unnamed x37, local copies, waits for them, and re-layouts  8.41 us
  transfers between devices with their start and end apart: 1, of which 0 were waited for; matrix products, arithmetic and copies ran while one was open for 0% of the time, Pallas kernels for 14%

profile of v2, /device:TPU:1, one launch (start us, length us, event | category | flops | bytes accessed | tf_op | source)
XLA Modules:
  0.0 124.8 jit_solution(12521437565837755280)
XLA Ops:
  0.6 0.0 copy-start.5
  0.6 0.0 copy-start.4
  0.7 0.0 copy-start.3
  0.7 0.0 copy-start.14
  0.7 0.0 copy-start.13
  0.7 0.0 copy-start.11
  1.4 24.8 %exchange_inputs.1 = (bf16[32,128,128]{2,1,0:T(8,128)(2,1)}, bf16[32,128,128]{2,1,0:T(8,128)(2,1)}, bf16[4,128,128]{2,1,0:T(8,128)(2,1)}, bf16[4,128,128]{2,1,0:...) custom-call(bf16[32,128,128]{2,1,0:T(8,128)(2,1)} %bitcast.4, ...), custom_call_target="tpu_custom_call" | custom-call | tf_op jit(solution)/shard_map/exchange_inputs/pallas_call | solution.py:220
  26.2 0.0 copy-start.15
  26.2 0.0 copy-start
  26.2 1.2 copy-done
  27.4 0.0 copy-start.1
  27.4 1.2 copy-done.1
  28.6 0.0 copy-start.2
  28.6 1.2 copy-done.2
  29.9 0.0 copy-start.10
  29.9 0.7 copy-done.10
  30.6 0.0 copy-start.12
  30.6 0.7 copy-done.12
  31.2 0.0 copy-start.6
  31.2 0.0 copy-start.7
  31.2 0.0 copy-start.8
  31.2 0.0 copy-start.9
  31.3 16.9 %forward_sum.1.partial = bf16[32,128,128]{2,1,0:T(8,128)(2,1)S(1)} custom-call(s32[704]{0:T(1024)S(1)} %copy-done.10, s32[704]{0:T(1024)S(1)} %copy-done.12, s32[1]{0:T(128)S(6)} %copy.19.count_ref, bf16[32,128,128]{2,1,0:T(8,128)(2,1)S(1)} %copy-done.1, bf16[32,128,128]{2,1,0:T(8,128)(2,1)S(1)} %bitcast.5, bf16[32,128,128]{2,1,0:T(8,128)(2,1)S(1)} %copy-done.2, ...), custom_call_target="tpu_custom_call" | custom-call | flops 2952790016 | bytes 23068672 | tf_op jit(solution)/shard_map/forward_sum/pallas_call | solution.py:131
  48.2 0.0 copy-done.5
  48.2 0.0 copy-done.4
  48.2 0.0 copy-done.3
  48.2 0.0 copy-done.14
  48.2 0.0 copy-done.15
  48.2 0.0 copy-done.6
  48.2 0.0 copy-done.7
  48.2 0.0 copy-done.8
  48.2 0.0 copy-done.9
  48.2 21.9 %middle.1 = (bf16[32,128,128]{2,1,0:T(8,128)(2,1)S(1)}, bf16[512,128]{1,0:T(8,128)(2,1)S(1)}, f32[512,128]{1,0:T(8,128)S(1)}, f32[512,128]{1,0:T(8,128)S(1)}, f3...) custom-call(bf16[32,128,128]{2,1,0:T(8,128)(2,1)S(1)} %forward_sum.1.partial, bf16[32,128,128]{2,1,0:T(8,128)(2,1)S(1)} %bitcast.6, ...), custom_call_target="tpu_custom_call" | custom-call | tf_op jit(solution)/shard_map/middle/pallas_call | solution.py:354
  70.1 1.5 %collective-permute-start = (bf16[1552,128]{1,0:T(8,128)(2,1)S(1)}, bf16[1552,128]{1,0:T(8,128)(2,1)S(1)}, u32[]{:S(2)}, u32[]{:S(2)}) collective-permute-start(bf16[1552,128]{1,0:T(8,128)(2,1)S(1)} %get-tuple-element.35), channel_id=1, source_target_pairs={{0,4},{4,0},{1,5},{5,1},{2,6},{6,2},{3,7},{7,3},{8,12},{12,8},{9,1... | collective-permute-start | bytes 1191944 | tf_op jit(solution)/shard_map/ppermute | solution.py:577
  71.6 0.0 copy-done.13
  71.6 0.0 copy-done.11
  71.6 17.7 %backward_sum.1.back = bf16[96,128,128]{2,1,0:T(8,128)(2,1)S(1)} custom-call(s32[704]{0:T(1024)S(1)} %copy-done.11, s32[704]{0:T(1024)S(1)} %copy-done.13, s32[1]{0:T(128)S(6)} %copy.19.count_ref, bf16[32,128,128]{2,1,0:T(8,128)(2,1)S(1)} %get-tuple-element.30.grads, bf16[704,128,128]{2,1,0:T(8,128)(2,1)} %tiles.3), custom_call_target="tpu_custom_call" | custom-call | flops 2952790016 | bytes 23068672 | tf_op jit(solution)/shard_map/backward_sum/pallas_call | solution.py:151
  89.4 0.0 collective-permute-done.far
  89.4 32.1 %finish.1 = (bf16[1024,128]{1,0:T(8,128)(2,1)S(1)}, f32[1024,128]{1,0:T(8,128)S(1)}, f32[256,128]{1,0:T(8,128)S(1)}, f32[256,128]{1,0:T(8,128)S(1)}, f32[1,128]{1,0:T(1,128)S(1)}) custom-call(bf16[96,128,128]{2,1,0:T(8,128)(2,1)S(1)} %backward_sum.1.back, bf16[512,128]{1,0:T(8,128)(2,1)S(1)} %get-tuple-element.31.out_near, ...), custom_call_target="tpu_custom_call" | custom-call | tf_op jit(solution)/shard_map/finish/pallas_call | solution.py:527
  121.5 0.7 copy.20
  122.2 0.8 copy.21
  123.0 0.7 copy.22
  123.6 0.7 copy.23
  124.3 0.5 copy.24
Async XLA Ops:
  0.6 47.5 %copy-start.5 = (bf16[256,128]{1,0:T(8,128)(2,1)S(1)}, bf16[256,128]{1,0:T(8,128)(2,1)}, u32[]{:S(2)}) copy-start(bf16[256,128]{1,0:T(8,128)(2,1)} %w_neigh.3) | copy-start | bytes 196612
  0.6 47.5 %copy-start.4 = (bf16[256,128]{1,0:T(8,128)(2,1)S(1)}, bf16[256,128]{1,0:T(8,128)(2,1)}, u32[]{:S(2)}) copy-start(bf16[256,128]{1,0:T(8,128)(2,1)} %w_self.3) | copy-start | bytes 196612
  0.7 47.5 %copy-start.3 = (bf16[1024,128]{1,0:T(8,128)(2,1)S(1)}, bf16[1024,128]{1,0:T(8,128)(2,1)}, u32[]{:S(2)}) copy-start(bf16[1024,128]{1,0:T(8,128)(2,1)} %param.17) | copy-start | bytes 786436
  0.7 47.5 %copy-start.14 = (f32[128]{0:T(128)S(1)}, f32[128]{0:T(128)}, u32[]{:S(2)}) copy-start(f32[128]{0:T(128)} %param.16) | copy-start | bytes 1540
  0.7 71.0 %copy-start.13 = (s32[704]{0:T(1024)S(1)}, s32[704]{0:T(1024)}, u32[]{:S(2)}) copy-start(s32[704]{0:T(1024)} %cols.3) | copy-start | bytes 8452
  0.7 70.9 %copy-start.11 = (s32[704]{0:T(1024)S(1)}, s32[704]{0:T(1024)}, u32[]{:S(2)}) copy-start(s32[704]{0:T(1024)} %rows.3) | copy-start | bytes 8452
  26.2 22.0 %copy-start.15 = (f32[1,128]{1,0:T(1,128)S(1)}, f32[1,128]{1,0:T(1,128)}, u32[]{:S(2)}) copy-start(f32[1,128]{1,0:T(1,128)} %get-tuple-element.29.bias_far) | copy-start | bytes 1540
  26.2 1.2 copy-start
  27.4 1.2 copy-start.1
  28.6 1.2 copy-start.2
  29.9 0.7 copy-start.10
  30.6 0.7 copy-start.12
  31.2 17.0 %copy-start.6 = (bf16[4,128,128]{2,1,0:T(8,128)(2,1)S(1)}, bf16[4,128,128]{2,1,0:T(8,128)(2,1)}, u32[]{:S(2)}) copy-start(bf16[4,128,128]{2,1,0:T(8,128)(2,1)} %get-tuple-element.25.own_far) | copy-start | bytes 393220
  31.2 17.0 %copy-start.7 = (bf16[4,128,128]{2,1,0:T(8,128)(2,1)S(1)}, bf16[4,128,128]{2,1,0:T(8,128)(2,1)}, u32[]{:S(2)}) copy-start(bf16[4,128,128]{2,1,0:T(8,128)(2,1)} %get-tuple-element.26.cot_far) | copy-start | bytes 393220
  31.2 17.0 %copy-start.8 = (bf16[256,128]{1,0:T(8,128)(2,1)S(1)}, bf16[256,128]{1,0:T(8,128)(2,1)}, u32[]{:S(2)}) copy-start(bf16[256,128]{1,0:T(8,128)(2,1)} %get-tuple-element.27.w_self_far) | copy-start | bytes 196612
  31.2 17.0 %copy-start.9 = (bf16[256,128]{1,0:T(8,128)(2,1)S(1)}, bf16[256,128]{1,0:T(8,128)(2,1)}, u32[]{:S(2)}) copy-start(bf16[256,128]{1,0:T(8,128)(2,1)} %get-tuple-element.28.w_neigh_far) | copy-start | bytes 196612
  70.1 19.3 %collective-permute-start = (bf16[1552,128]{1,0:T(8,128)(2,1)S(1)}, bf16[1552,128]{1,0:T(8,128)(2,1)S(1)}, u32[]{:S(2)}, u32[]{:S(2)}) collective-permute-start(bf16[1552,128]{1,0:T(8,128)(2,1)S(1)} %get-tuple-element.35), channel_id=1, source_target_pairs={{0,4},{4,0},{1,5},{5,1},{2,6},{6,2},{3,7},{7,3},{8,12},{12,8},{9,1... | collective-permute-start | bytes 1191944 | tf_op jit(solution)/shard_map/ppermute | solution.py:577

commit v3 on v2

v3 whole, which is shorter than its diff:
```python
import functools
import math

import jax
import jax.numpy as jnp
from jax import lax
from jax.experimental import pallas as pl
from jax.experimental.pallas import tpu as pltpu
from jax.sharding import PartitionSpec as P

F32 = jnp.float32
BF16 = jnp.bfloat16
UNROLL = 88
LAG = 4
LOADS = 16
MIB = 1024 * 1024


MESH = pl.DeviceIdType.MESH


def place():
    row, col, edge = (lax.axis_index(name) for name in ("row", "col", "edge"))
    return row, col, edge, lax.rem(edge, 2), lax.div(edge, 2)


def greet(peers):
    barrier = pltpu.get_barrier_semaphore()
    for peer in peers:
        pl.semaphore_signal(barrier, inc=1, device_id=peer, device_id_type=MESH)
    pl.semaphore_wait(barrier, len(peers))


class Sender:
    def __init__(self, send_sems, recv_sems):
        self.send_sems, self.recv_sems, self.used = send_sems, recv_sems, []

    def __call__(self, src, dst, peer):
        index = len(self.used)
        copy = pltpu.make_async_remote_copy(
            src_ref=src,
            dst_ref=dst,
            send_sem=self.send_sems.at[index],
            recv_sem=self.recv_sems.at[index],
            device_id=peer,
            device_id_type=MESH,
        )
        copy.start()
        self.used.append(copy)
        return copy

    def finish(self):
        for copy in self.used:
            copy.wait_send()


def add_tiles(count, tiles, total, product, target, fetched=lambda g: None):
    spare = total.shape[0] - 1
    total[...] = jnp.zeros_like(total)

    def group_step(g, carry):
        fetched(g)
        start = g * UNROLL
        waiting = {}
        for u in range(UNROLL + LAG):
            if u < UNROLL:
                waiting[u] = product(start + u, tiles[start + u])
            if u >= LAG:
                slot = start + u - LAG
                total[jnp.where(slot < count, target(slot), spare)] += waiting.pop(u - LAG)
        return carry

    lax.fori_loop(0, groups(count), group_step, 0)


def groups(count):
    return lax.div(count + UNROLL - 1, UNROLL)


def forward_kernel(rows, cols, count_ref, window, tiles, out, total):
    add_tiles(
        count_ref[0], tiles, total,
        lambda slot, tile: jnp.dot(tile, window[cols[slot]], preferred_element_type=F32),
        lambda slot: rows[slot],
    )
    out[...] = total[: out.shape[0]].astype(BF16)


def backward_kernel(rows, cols, count_ref, grads, tiles, out, held, total, sems):
    def fetch(g):
        at = pl.ds(g * UNROLL, UNROLL)
        return pltpu.make_async_copy(tiles.at[at], held.at[at], sems.at[g])

    def start(g, carry):
        fetch(g).start()
        return carry

    lax.fori_loop(0, groups(count_ref[0]), start, 0)
    add_tiles(
        count_ref[0], held, total,
        lambda slot, tile: jnp.dot(grads[rows[slot]], tile, preferred_element_type=F32),
        lambda slot: cols[slot],
        lambda g: fetch(g).wait(),
    )
    out[...] = total[: out.shape[0]].astype(BF16)


SMEM = pl.BlockSpec(memory_space=pltpu.SMEM)
VMEM = pl.BlockSpec(memory_space=pltpu.VMEM)
HBM = pl.BlockSpec(memory_space=pltpu.HBM)


def tile_sum(kernel, blocks, tile_rows, tile_cols, tile_count, source, tiles, tiles_spec, scratch, limit):
    slots, size, _ = tiles.shape
    return pl.pallas_call(
        kernel,
        out_shape=pltpu.VMEM((blocks, size, size), BF16),
        in_specs=[SMEM] * 3 + [VMEM, tiles_spec],
        out_specs=VMEM,
        scratch_shapes=scratch,
        compiler_params=pltpu.CompilerParams(vmem_limit_bytes=limit),
        cost_estimate=pl.CostEstimate(flops=2 * slots * size**3, bytes_accessed=slots * 2 * size**2, transcendentals=0),
        name=kernel.__name__.replace("kernel", "sum"),
    )(tile_rows, tile_cols, tile_count, source, tiles)


def forward_sum(tile_rows, tile_cols, tile_count, window, held):
    blocks, size, half = window.shape
    scratch = [pltpu.VMEM((blocks // 3 + 1, size, half), F32)]
    return tile_sum(forward_kernel, blocks // 3, tile_rows, tile_cols, tile_count, window, held, VMEM, scratch, 24 * MIB)


def backward_sum(tile_rows, tile_cols, tile_count, grads, tiles):
    blocks, half, size = grads.shape
    scratch = [
        pltpu.VMEM(tiles.shape, BF16),
        pltpu.VMEM((3 * blocks + 1, half, size), F32),
        pltpu.SemaphoreType.DMA((tiles.shape[0] // UNROLL,)),
    ]
    return tile_sum(backward_kernel, 3 * blocks, tile_rows, tile_cols, tile_count, grads, tiles, HBM, scratch, 50 * MIB)


HALO_CHUNKS = 4


def halo_kernel(
    features, cotangent, w_self, w_neigh, bias, tiles,
    window, held, own_far, cot_far, w_self_far, w_neigh_far, bias_far,
    load_sems, send_sems, recv_sems,
):
    row, col, edge, core, _ = place()
    rows = lax.axis_size("row")
    up, down = {"row": lax.rem(row + 1, rows)}, {"row": lax.rem(row + rows - 1, rows)}
    twin, partner = {"edge": edge + 1 - 2 * core}, {"col": 1 - col}
    blocks = features.shape[0]
    share = blocks // 8
    greet([up, down, twin, partner])
    send = Sender(send_sems, recv_sems)
    step = blocks // 2 // HALO_CHUNKS
    parts = [pl.ds(core * (blocks // 2) + i * step, step) for i in range(HALO_CHUNKS)]
    arriving = []
    for part in parts:
        for side, peer in ((0, up), (2, down)):
            landing = pl.ds(side * blocks + core * (blocks // 2) + (len(arriving) // 2) * step, step)
            arriving.append((landing, send(features.at[part], window.at[landing], peer)))
    theirs = pl.ds(edge * 2 * share + (1 - col) * share, share)
    theirs_cot = pl.ds((1 - col) * share, share)
    swaps = [
        send(features.at[theirs], own_far, partner),
        send(cotangent.at[theirs_cot], cot_far, partner),
        send(w_self, w_self_far, partner),
        send(w_neigh, w_neigh_far, partner),
        send(bias, bias_far, partner),
    ]
    many = tiles.shape[0] // LOADS
    loads = [pltpu.make_async_copy(features, window.at[pl.ds(blocks, blocks)], load_sems.at[LOADS])]
    for i in range(LOADS):
        at = pl.ds(i * many, many)
        loads.append(pltpu.make_async_copy(tiles.at[at], held.at[at], load_sems.at[i]))
    for load in loads:
        load.start()
    handed = []
    for landing, copy in arriving:
        copy.wait_recv()
        handed.append(send(window.at[landing], window.at[landing], twin))
    for copy in swaps + handed:
        copy.wait_recv()
    for load in loads:
        load.wait()
    send.finish()


def exchange_inputs(features, cotangent, w_self, w_neigh, bias, tiles):
    blocks, size, half = features.shape
    share = blocks // 8
    shapes = [
        jax.ShapeDtypeStruct((3 * blocks, size, half), BF16),
        tiles,
        jax.ShapeDtypeStruct((share, size, half), BF16),
        jax.ShapeDtypeStruct((share, size, half), BF16),
        w_self, w_neigh, bias,
    ]
    copies = 4 * HALO_CHUNKS + 5
    return pl.pallas_call(
        halo_kernel,
        out_shape=[pltpu.VMEM(s.shape, s.dtype) for s in shapes],
        in_specs=[HBM] * 6,
        out_specs=[VMEM] * 7,
        scratch_shapes=[
            pltpu.SemaphoreType.DMA((LOADS + 1,)),
            pltpu.SemaphoreType.DMA((copies,)),
            pltpu.SemaphoreType.DMA((copies,)),
        ],
        compiler_params=pltpu.CompilerParams(collective_id=1, has_side_effects=True, vmem_limit_bytes=24 * MIB),
        name="exchange_inputs",
    )(features, cotangent, w_self, w_neigh, bias, tiles)


def mid_kernel(
    partial, features, own_far, cotangent, cot_far, w_self, w_neigh, w_self_far, w_neigh_far, bias, bias_far,
    grads, out_near, self_near, weight_sum, far,
    got_core, sent_pair, kept, got_pair, sent_col, got_col, own, cot, weights, sent_grads,
    w_all, w_bias, w_sent_x, w_got_x, w_sent_z, w_got_z, w_sent_e, w_got_e,
    local_sems, send_sems, recv_sems,
):
    row, col, edge, core, pair_side = place()
    other = 1 - col
    twin, pair, partner = {"edge": edge + 1 - 2 * core}, {"edge": lax.rem(edge + 2, 4)}, {"col": other}
    diagonal = {"edge": lax.rem(edge + 2, 4), "col": other}
    x, z = lax.rem(row, 4), lax.div(row, 4)
    along_x = [lax.rem(x + j, 4) for j in (1, 2, 3)]
    along_z = [lax.rem(z + j, 4) for j in (1, 2, 3)]
    along_e = [lax.rem(edge + j, 4) for j in (1, 2, 3)]
    x_peers = [{"row": z * 4 + to} for to in along_x]
    z_peers = [{"row": to * 4 + x} for to in along_z]
    e_peers = [{"edge": to} for to in along_e]
    blocks, size, half = partial.shape
    share = blocks // 8
    near_rows = own_far.shape[0] * size
    local = [
        pltpu.make_async_copy(features.at[pl.ds(edge * 2 * share + col * share, share)], own, local_sems.at[0]),
        pltpu.make_async_copy(cotangent.at[pl.ds(col * share, share)], cot, local_sems.at[1]),
    ]
    for copy in local:
        copy.start()
    greet([partner, diagonal] + e_peers + x_peers + z_peers)
    send = Sender(send_sems, recv_sems)

    def piece(side, on_core, column):
        return pl.ds((2 * side + on_core) * 2 * share + column * share, share)

    order = [(1 - pair_side, other), (1 - pair_side, col), (pair_side, other), (pair_side, col)]
    to_twin = [
        send(partial.at[piece(side, 1 - core, column)], got_core.at[i], twin)
        for i, (side, column) in enumerate(order)
    ]
    near_w, far_w = pl.ds(pl.multiple_of(col * half, half), half), pl.ds(pl.multiple_of(other * half, half), half)
    for k, (near, away) in enumerate(((w_self, w_self_far), (w_neigh, w_neigh_far))):
        for j, rows in enumerate((near_w, far_w)):
            at = pl.ds((2 * k + j) * half, half)
            weights[at, :half] = near[rows, :]
            weights[at, half:] = away[rows, :]

    def summed(i):
        to_twin[i].wait_recv()
        side, column = order[i]
        return partial[piece(side, core, column)].astype(F32) + got_core[i].astype(F32)

    to_pair = []
    for i in range(2):
        sent_pair[i] = summed(i).astype(BF16)
        to_pair.append(send(sent_pair.at[i], got_pair.at[i], pair))
    for i in range(2):
        kept[i] = summed(2 + i)
    to_pair[0].wait_recv()
    sent_col[...] = (kept[0] + got_pair[0].astype(F32)).astype(BF16)
    to_partner = send(sent_col, got_col, partner)
    for copy in local:
        copy.wait()
    to_pair[1].wait_recv()
    agg_near = (kept[1] + got_pair[1].astype(F32)).astype(BF16)
    to_partner.wait_recv()

    def flat(blocks_of):
        return blocks_of.reshape(near_rows, half)

    mixed = jnp.concatenate(
        [flat(own[...]), flat(own_far[...]), flat(agg_near), flat(got_col[...])], axis=1
    )
    pre = jnp.dot(mixed, weights[...], preferred_element_type=F32) + jnp.concatenate(
        [bias[...], bias_far[...]], axis=1
    )
    sigm = jax.nn.sigmoid(pre)
    cot_full = jnp.concatenate([flat(cot[...]), flat(cot_far[...])], axis=1).astype(F32)
    grad_pre = cot_full * sigm * (1.0 + pre * (1.0 - sigm))
    grad_low = grad_pre.astype(BF16)
    over_cols = (((1,), (1,)), ((), ()))
    agg_back = lax.dot_general(
        weights[2 * half :, :], grad_low, over_cols, preferred_element_type=F32
    ).astype(BF16)
    mine = pl.ds(edge * 2 * share + col * share, share)
    for b in range(share):
        grads[edge * 2 * share + col * share + b] = agg_back[:half, b * size : (b + 1) * size]
        sent_grads[b] = agg_back[half:, b * size : (b + 1) * size]
    crossing = [
        send(sent_grads, grads.at[mine], diagonal),
        send(sent_grads, grads.at[mine], partner),
        send(grads.at[mine], grads.at[mine], pair),
    ]
    handed = [send(grads.at[mine], grads.at[mine], twin)]

    parts = lax.dot_general(mixed, grad_low, (((0,), (0,)), ((), ())), preferred_element_type=F32)
    for k in range(2):
        for j, start in enumerate((col * half, other * half)):
            at = (2 * k + j) * half
            w_all[pl.ds(pl.multiple_of(2 * k * half + start, half), half), :] = parts[at : at + half, :]
    w_bias[...] = jnp.sum(grad_pre.reshape(near_rows // 16, 16, 2 * half), axis=0)

    def spread(start, many, sent, got, targets, peers):
        steps = []
        for j in range(3):
            sent[j, :many] = w_all[pl.ds(pl.multiple_of(start + targets[j] * many, 8), many), :].astype(sent.dtype)
            sent[j, many:] = w_bias[...].astype(sent.dtype)
            steps.append(send(sent.at[j], got.at[j], peers[j]))
        return steps

    def collect(start, many, got, steps):
        for j in range(3):
            steps[j].wait_recv()
        at = pl.ds(start, many)
        got3 = got[...].astype(F32)
        w_all[at, :] += got3[0, :many] + got3[1, :many] + got3[2, :many]
        w_bias[...] += got3[0, many:] + got3[1, many:] + got3[2, many:]

    x_many, z_many, e_many = 4 * half // 4, 4 * half // 16, 4 * half // 64
    x_start = pl.multiple_of(x * x_many, 8)
    z_start = pl.multiple_of(x_start + z * z_many, 8)
    e_start = pl.multiple_of(z_start + edge * e_many, 8)
    steps = spread(0, x_many, w_sent_x, w_got_x, along_x, x_peers)

    output = (pre * sigm).astype(BF16)
    out_near[...] = output[:, :half]
    far[:near_rows] = output[:, half:]
    self_back = lax.dot_general(grad_low, weights[: 2 * half, :], over_cols, preferred_element_type=F32)
    self_near[...] = self_back[:, :half]
    far[near_rows:] = self_back[:, half:].astype(BF16)

    collect(x_start, x_many, w_got_x, steps)
    steps = spread(x_start, z_many, w_sent_z, w_got_z, along_z, z_peers)

    far_edge = lax.rem(edge + 2, 4)
    homes = [
        pl.ds(far_edge * 2 * share + other * share, share),
        pl.ds(edge * 2 * share + other * share, share),
        pl.ds(far_edge * 2 * share + col * share, share),
    ]
    for k in (1, 2, 0):
        crossing[k].wait_recv()
        handed.append(send(grads.at[homes[k]], grads.at[homes[k]], twin))
    collect(z_start, z_many, w_got_z, steps)
    steps = spread(z_start, e_many, w_sent_e, w_got_e, along_e, e_peers)
    collect(e_start, e_many, w_got_e, steps)
    for j in range(2):
        weight_sum[j, :e_many] = w_all[pl.ds(e_start, e_many), j * half : (j + 1) * half]
        weight_sum[j, e_many:] = w_bias[:, j * half : (j + 1) * half]
    for copy in handed:
        copy.wait_recv()
    send.finish()


def middle(partial, features, own_far, cotangent, cot_far, w_self, w_neigh, w_self_far, w_neigh_far, bias, bias_far):
    blocks, size, half = partial.shape
    share = blocks // 8
    rows = share * size
    copies = 4 + 2 + 1 + 3 + 4 + 9
    top = 4 * half
    piece = (share, size, half)
    return pl.pallas_call(
        mid_kernel,
        out_shape=[
            pltpu.VMEM((blocks, half, size), BF16),
            pltpu.VMEM((rows, half), BF16),
            pltpu.VMEM((rows, half), F32),
            pltpu.VMEM((2, top // 64 + 16, half), F32),
            jax.ShapeDtypeStruct((2 * rows, half), BF16),
        ],
        in_specs=[VMEM, HBM, VMEM, HBM] + [VMEM] * 7,
        out_specs=[VMEM] * 5,
        scratch_shapes=[
            pltpu.VMEM((4,) + piece, BF16),
            pltpu.VMEM((2,) + piece, BF16),
            pltpu.VMEM((2,) + piece, F32),
            pltpu.VMEM((2,) + piece, BF16),
            pltpu.VMEM(piece, BF16),
            pltpu.VMEM(piece, BF16),
            pltpu.VMEM(piece, BF16),
            pltpu.VMEM(piece, BF16),
            pltpu.VMEM((4 * half, 2 * half), BF16),
            pltpu.VMEM((share, half, size), BF16),
            pltpu.VMEM((top, 2 * half), F32),
            pltpu.VMEM((16, 2 * half), F32),
            *[pltpu.VMEM((3, top // 4 + 16, 2 * half), BF16)] * 2,
            *[pltpu.VMEM((3, top // 16 + 16, 2 * half), F32)] * 2,
            *[pltpu.VMEM((3, top // 64 + 16, 2 * half), F32)] * 2,
            pltpu.SemaphoreType.DMA((2,)),
            pltpu.SemaphoreType.DMA((copies,)),
            pltpu.SemaphoreType.DMA((copies,)),
        ],
        compiler_params=pltpu.CompilerParams(collective_id=2, has_side_effects=True, vmem_limit_bytes=8 * MIB),
        name="middle",
    )(partial, features, own_far, cotangent, cot_far, w_self, w_neigh, w_self_far, w_neigh_far, bias, bias_far)


def final_kernel(
    back, weight_sum,
    sums, weights, bias_total,
    got_core, sent_row, kept, got_row, sent_pair, got_pair, got_col,
    send_sems, recv_sems,
):
    row, col, edge, core, side = place()
    rows = lax.axis_size("row")
    x, z = lax.rem(row, 4), lax.div(row, 4)
    twin, pair, partner = {"edge": edge + 1 - 2 * core}, {"edge": lax.rem(edge + 2, 4)}, {"col": 1 - col}
    up, down = {"row": lax.rem(row + 1, rows)}, {"row": lax.rem(row + rows - 1, rows)}
    x_peers = [{"row": z * 4 + lax.rem(x + j, 4)} for j in (1, 2, 3)]
    z_peers = [{"row": lax.rem(z + j, 4) * 4 + x} for j in (1, 2, 3)]
    e_peers = [{"edge": lax.rem(edge + j, 4)} for j in (1, 2, 3)]
    greet([partner, up, down] + e_peers + x_peers + z_peers)
    send = Sender(send_sems, recv_sems)
    blocks = back.shape[0] // 3
    share = blocks // 4

    def piece(part, at_side, on_core):
        return pl.ds(part * blocks + (2 * at_side + on_core) * share, share)

    order = [(0, 1 - side), (2, 1 - side), (0, side), (2, side), (1, 1 - side), (1, side)]
    to_twin = [
        send(back.at[piece(part, at, 1 - core)], got_core.at[i], twin) for i, (part, at) in enumerate(order)
    ]
    to_partner = send(weight_sum.at[1], got_col, partner)

    def summed(i):
        to_twin[i].wait_recv()
        part, at = order[i]
        return back[piece(part, at, core)].astype(F32) + got_core[i].astype(F32)

    to_row = []
    for i in range(4):
        sent_row[i] = summed(i).astype(BF16)
        to_row.append(send(sent_row.at[i], got_row.at[i], down if i % 2 == 0 else up))

    top = weights.shape[0]
    many = top // 64
    to_partner.wait_recv()
    start = pl.multiple_of(x * (top // 4) + z * (top // 16) + edge * many, 8)
    weights[pl.ds(start, many), :] = weight_sum[0, :many] + got_col[:many]
    bias_total[...] = weight_sum[0, many:] + got_col[many:]

    def gathered(start, many, peers):
        at = pl.ds(pl.multiple_of(start, 8), many)
        return [send(weights.at[at], weights.at[at], peer) for peer in peers]

    steps = gathered(start, many, e_peers)
    for i in range(2):
        kept[i] = summed(4 + i)
    for step in steps:
        step.wait_recv()
    steps = gathered(x * (top // 4) + z * (top // 16), top // 16, z_peers)
    for i in range(2):
        to_row[i].wait_recv()
    sent_pair[...] = (kept[0] + got_row[0].astype(F32) + got_row[1].astype(F32)).astype(BF16)
    to_pair = send(sent_pair, got_pair, pair)
    for step in steps:
        step.wait_recv()
    steps = gathered(x * (top // 4), top // 4, x_peers)
    for i in range(2, 4):
        to_row[i].wait_recv()
    kept[1] += got_row[2].astype(F32) + got_row[3].astype(F32)
    to_pair.wait_recv()
    sums[...] = kept[1] + got_pair[...].astype(F32)
    for step in steps:
        step.wait_recv()
    send.finish()


def finish(back, weight_sum):
    share, half, size = back.shape[0] // 12, back.shape[1], back.shape[2]
    unit = weight_sum.shape[1]
    copies = 6 + 4 + 1 + 1 + 9
    piece = (share, half, size)
    return pl.pallas_call(
        final_kernel,
        out_shape=[
            pltpu.VMEM(piece, F32),
            pltpu.VMEM((4 * half, half), F32),
            pltpu.VMEM((16, half), F32),
        ],
        in_specs=[VMEM] * 2,
        out_specs=[VMEM] * 3,
        scratch_shapes=[
            pltpu.VMEM((6,) + piece, BF16),
            pltpu.VMEM((4,) + piece, BF16),
            pltpu.VMEM((2,) + piece, F32),
            pltpu.VMEM((4,) + piece, BF16),
            pltpu.VMEM(piece, BF16),
            pltpu.VMEM(piece, BF16),
            pltpu.VMEM((unit, half), F32),
            pltpu.SemaphoreType.DMA((copies,)),
            pltpu.SemaphoreType.DMA((copies,)),
        ],
        compiler_params=pltpu.CompilerParams(collective_id=3, has_side_effects=True, vmem_limit_bytes=8 * MIB),
        name="finish",
    )(back, weight_sum)


def writing_kernel(
    scale, out_near, self_near, far, sums, weights, bias_total,
    output, features_grad, w_self_grad, w_neigh_grad, bias_grad,
):
    col = lax.axis_index("col")
    rows, half = out_near.shape
    near, away = pl.multiple_of(col * rows, 16), pl.multiple_of((1 - col) * rows, 16)
    output[pl.ds(near, rows), :] = out_near[...]
    output[pl.ds(away, rows), :] = far[:rows]
    features_grad[pl.ds(near, rows), :] = self_near[...]
    features_grad[pl.ds(away, rows), :] = far[rows:].astype(F32)
    share, _, size = sums.shape
    for b in range(share):
        features_grad[b * size : (b + 1) * size, :] += sums[b].T
    top = weights.shape[0]
    w_self_grad[...] = weights[: top // 2] * scale
    w_neigh_grad[...] = weights[top // 2 :] * scale
    bias_grad[...] = jnp.sum(bias_total[...], axis=0, keepdims=True) * scale


def written(scale, out_near, self_near, far, sums, weights, bias_total):
    rows, half = out_near.shape
    top = weights.shape[0]
    return pl.pallas_call(
        functools.partial(writing_kernel, scale),
        out_shape=[
            jax.ShapeDtypeStruct((2 * rows, half), BF16),
            jax.ShapeDtypeStruct((2 * rows, half), F32),
            jax.ShapeDtypeStruct((top // 2, half), F32),
            jax.ShapeDtypeStruct((top // 2, half), F32),
            jax.ShapeDtypeStruct((1, half), F32),
        ],
        in_specs=[VMEM] * 6,
        out_specs=[VMEM] * 5,
        compiler_params=pltpu.CompilerParams(vmem_limit_bytes=4 * MIB),
        name="written",
    )(out_near, self_near, far, sums, weights, bias_total)


def local(features, tiles, tile_rows, tile_cols, tile_count, w_self, w_neigh, bias, cotangent):
    rows_dev, half = features.shape
    size = tiles.shape[1]
    blocks = rows_dev // size
    nodes = rows_dev * lax.axis_size("row")
    scale = 1.0 / math.sqrt(nodes)

    own = features.reshape(blocks, size, half)
    cot = cotangent.reshape(-1, size, half)
    bias_row = bias.reshape(1, half)
    window, held, own_far, cot_far, w_self_far, w_neigh_far, bias_far = exchange_inputs(
        own, cot, w_self, w_neigh, bias_row, tiles
    )
    partial = forward_sum(tile_rows, tile_cols, tile_count, window, held)
    grads, out_near, self_near, weight_sum, far = middle(
        partial, own, own_far, cot, cot_far, w_self, w_neigh, w_self_far, w_neigh_far, bias_row, bias_far
    )
    far = lax.ppermute(far, "col", [(0, 1), (1, 0)])
    back = backward_sum(tile_rows, tile_cols, tile_count, grads, tiles)
    sums, weights, bias_total = finish(back, weight_sum)
    output, features_grad, w_self_grad, w_neigh_grad, bias_grad = written(
        scale, out_near, self_near, far, sums, weights, bias_total
    )
    return (output, features_grad, w_self_grad, w_neigh_grad, bias_grad.reshape(half))


def solution(mesh):
    return jax.shard_map(
        local,
        mesh=mesh,
        in_specs=(
            P("row", "col"),
            P(("row", "edge"), None, None),
            P(("row", "edge")),
            P(("row", "edge")),
            P(("row", "edge")),
            P(None, "col"),
            P(None, "col"),
            P("col"),
            P(("row", "edge"), "col"),
        ),
        out_specs=(
            P(("row", "edge"), "col"),
            P(("row", "edge"), "col"),
            P(None, "col"),
            P(None, "col"),
            P("col"),
        ),
        check_vma=False,
    )
```

time: 125 us -> 120 us (0.960)
  Pallas kernels: 113 us -> 94.3 us
  local copies, waits for them, and re-layouts: 8.41 us -> 20.7 us
    pallas_call x5 -> x6, Pallas kernels: 113 us -> 94.3 us  [the longest x1 32.1 us: middle(): pl.pallas_call(mid_kernel, out_shape=[pltpu.VMEM((blocks, half, size), BF...]
    unnamed x37 -> x22, local copies, waits for them, and re-layouts: 8.41 us -> 20.7 us
  transfers between devices with their start and end apart: 1 -> 1, of which waited for: 0 -> 0; matrix products, arithmetic and copies ran while one was open for 0% -> 0% of each run, Pallas kernels for 14% -> 27%
where the time goes in v3:
time: 120 us; the launch traced here: 119 us
  Pallas kernels  94.3 us (79%)
  local copies, waits for them, and re-layouts  20.7 us (17%)
  starting transfers between devices  2.5 us (2%)
  between operations  1.39 us (1%)
    pallas_call x1, Pallas kernels, middle(): pl.pallas_call(mid_kernel, out_shape=[pltpu.VMEM((blocks, half, size), BF...  32.1 us
    pallas_call x1, Pallas kernels, finish(): pl.pallas_call(final_kernel, out_shape=[pltpu.VMEM(piece, F32), pltpu.VME...  25.9 us
    pallas_call x1, Pallas kernels, exchange_inputs(): pl.pallas_call(halo_kernel, out_shape=[pltpu.VMEM(s.shape, s.dtype) for s...  24.2 us
    unnamed x22, local copies, waits for them, and re-layouts  20.7 us
    pallas_call x2, Pallas kernels, tile_sum(): pl.pallas_call(kernel, out_shape=pltpu.VMEM((blocks, size, size), BF16),...  11 us
    ppermute x1, starting transfers between devices, local(): far = lax.ppermute(far, 'col', [(0, 1), (1, 0)])  2.5 us
  transfers between devices with their start and end apart: 1, of which 0 were waited for; matrix products, arithmetic and copies ran while one was open for 0% of the time, Pallas kernels for 27%

profile of v3, /device:TPU:1, one launch (start us, length us, event | category | flops | bytes accessed | tf_op | source)
XLA Modules:
  0.0 118.9 jit_solution(2869417874920078238)
XLA Ops:
  0.6 0.0 copy-start.8
  1.3 0.0 copy-start.2
  1.3 1.2 %copy-done.2 = bf16[4096,128]{1,0:T(8,128)(2,1)S(1)} copy-done((bf16[4096,128]{1,0:T(8,128)(2,1)S(1)}, bf16[4096,128]{1,0:T(8,128)(2,1)}, u32[]{:S(2)}) %copy-start.2) | copy-done | bytes 1048600
  2.5 0.0 copy-start.4
  2.5 0.9 copy-done.4
  3.5 0.0 copy-start.6
  3.5 0.8 copy-done.6
  4.3 0.0 copy-start.7
  4.3 0.8 copy-done.7
  5.2 0.0 copy-start.10
  5.2 0.7 copy-done.10
  5.8 0.0 copy-start.9
  5.8 0.0 copy-start.3
  5.8 24.2 %exchange_inputs.1 = (bf16[96,128,128]{2,1,0:T(8,128)(2,1)S(1)}, bf16[704,128,128]{2,1,0:T(8,128)(2,1)S(1)}, bf16[4,128,128]{2,1,0:T(8,128)(2,1)S(1)}, bf16[4,12...) custom-call(bf16[32,128,128]{2,1,0:T(8,128)(2,1)S(1)} %bitcast.4, ...), custom_call_target="tpu_custom_call" | custom-call | tf_op jit(solution)/shard_map/exchange_inputs/pallas_call | solution.py:204
  30.0 0.0 copy-start
  30.0 7.6 %copy-done = bf16[704,128,128]{2,1,0:T(8,128)(2,1)} copy-done((bf16[704,128,128]{2,1,0:T(8,128)(2,1)}, bf16[704,128,128]{2,1,0:T(8,128)(2,1)S(1)}, u32[]{:S(2)}) %copy-start) | copy-done | bytes 23068696
  37.7 0.0 copy-done.8
  37.7 0.0 copy-done.9
  37.7 0.0 copy-start.1
  37.7 7.6 %copy-done.1 = bf16[704,128,128]{2,1,0:T(8,128)(2,1)S(1)} copy-done((bf16[704,128,128]{2,1,0:T(8,128)(2,1)S(1)}, bf16[704,128,128]{2,1,0:T(8,128)(2,1)}, u32[]{:S(2)}) %copy-start.1) | copy-done | bytes 23068696
  45.2 4.3 %forward_sum.1.partial = bf16[32,128,128]{2,1,0:T(8,128)(2,1)S(1)} custom-call(s32[704]{0:T(1024)S(1)} %copy-done.8, s32[704]{0:T(1024)S(1)} %copy-done.9, s32[1]{0:T(128)S(6)} %copy.14.count_ref, bf16[96,128,128]{2,1,0:T(8,128)(2,1)S(1)} %get-tuple-element.25.window, bf16[704,128,128]{2,1,0:T(8,128)(2,1)S(1)} %copy-done.1), custom_call_target="tpu_custom_call" | custom-call | flops 2952790016 | bytes 23068672 | tf_op jit(solution)/shard_map/forward_sum/pallas_call | solution.py:115
  49.5 0.0 copy-done.3
  49.5 32.1 %middle.1 = (bf16[32,128,128]{2,1,0:T(8,128)(2,1)S(1)}, bf16[512,128]{1,0:T(8,128)(2,1)S(1)}, f32[512,128]{1,0:T(8,128)S(1)}, f32[2,24,128]{2,1,0:T(8,128)S(1)}, bf16[1024,128]{1,0:T(8,128)(2,1)S(1)}) custom-call(bf16[32,128,128]{2,1,0:T(8,128)(2,1)S(1)} %forward_sum.1.partial, bf16[32,128,128]{2,1,0:T(8,128)(2,1)S(1)} %bitcast.5, ...), custom_call_target="tpu_custom_call" | custom-call | tf_op jit(solution)/shard_map/middle/pallas_call | solution.py:378
  81.7 0.0 copy-start.5
  81.7 1.0 copy-done.5
  82.6 2.5 %collective-permute-start = (bf16[1024,128]{1,0:T(8,128)(2,1)S(1)}, bf16[1024,128]{1,0:T(8,128)(2,1)S(1)}, u32[]{:S(2)}, u32[]{:S(2)}) collective-permute-start(bf16[1024,128]{1,0:T(8,128)(2,1)S(1)} %get-tuple-element.34), channel_id=1, source_target_pairs={{0,4},{4,0},{1,5},{5,1},{2,6},{6,2},{3,7},{7,3},{8,12},{12,8},{9,1... | collective-permute-start | bytes 786440 | tf_op jit(solution)/shard_map/ppermute | solution.py:572
  85.1 6.7 %backward_sum.1.back = bf16[96,128,128]{2,1,0:T(8,128)(2,1)S(1)} custom-call(s32[704]{0:T(1024)S(1)} %copy-done.8, s32[704]{0:T(1024)S(1)} %copy-done.9, s32[1]{0:T(128)S(6)} %copy.14.count_ref, bf16[32,128,128]{2,1,0:T(8,128)(2,1)} %copy-done.5, bf16[704,128,128]{2,1,0:T(8,128)(2,1)} %tiles.3), custom_call_target="tpu_custom_call" | custom-call | flops 2952790016 | bytes 23068672 | tf_op jit(solution)/shard_map/backward_sum/pallas_call | solution.py:115
  91.8 25.9 %finish.1 = (f32[8,128,128]{2,1,0:T(8,128)S(1)}, f32[512,128]{1,0:T(8,128)S(1)}, f32[16,128]{1,0:T(8,128)S(1)}) custom-call(bf16[96,128,128]{2,1,0:T(8,128)(2,1)S(1)} %backward_sum.1.back, f32[2,24,128]{2,1,0:T(8,128)S(1)} %get-tuple-element.36.weight_sum), custom_call_target="tpu_custom_call" | custom-call | tf_op jit(solution)/shard_map/finish/pallas_call | solution.py:491
  117.7 0.0 collective-permute-done.far
  117.7 1.1 written.1
Async XLA Ops:
  0.6 37.0 %copy-start.8 = (s32[704]{0:T(1024)S(1)}, s32[704]{0:T(1024)}, u32[]{:S(2)}) copy-start(s32[704]{0:T(1024)} %rows.3) | copy-start | bytes 8452
  1.3 1.2 %copy-start.2 = (bf16[4096,128]{1,0:T(8,128)(2,1)S(1)}, bf16[4096,128]{1,0:T(8,128)(2,1)}, u32[]{:S(2)}) copy-start(bf16[4096,128]{1,0:T(8,128)(2,1)} %param.9) | copy-start | bytes 3145732
  2.5 0.9 copy-start.4
  3.5 0.8 copy-start.6
  4.3 0.8 copy-start.7
  5.2 0.7 copy-start.10
  5.8 31.9 %copy-start.9 = (s32[704]{0:T(1024)S(1)}, s32[704]{0:T(1024)}, u32[]{:S(2)}) copy-start(s32[704]{0:T(1024)} %cols.3) | copy-start | bytes 8452
  5.8 43.7 %copy-start.3 = (bf16[4096,128]{1,0:T(8,128)(2,1)S(1)}, bf16[4096,128]{1,0:T(8,128)(2,1)}, u32[]{:S(2)}) copy-start(bf16[4096,128]{1,0:T(8,128)(2,1)} %param.9) | copy-start | bytes 3145732
  30.0 7.7 %copy-start = (bf16[704,128,128]{2,1,0:T(8,128)(2,1)}, bf16[704,128,128]{2,1,0:T(8,128)(2,1)S(1)}, u32[]{:S(2)}) copy-start(bf16[704,128,128]{2,1,0:T(8,128)(2,1)S(1)} %get-tuple-element.26.tiles) | copy-start | bytes 69206016
  37.7 7.6 %copy-start.1 = (bf16[704,128,128]{2,1,0:T(8,128)(2,1)S(1)}, bf16[704,128,128]{2,1,0:T(8,128)(2,1)}, u32[]{:S(2)}) copy-start(bf16[704,128,128]{2,1,0:T(8,128)(2,1)} %copy-done) | copy-start | bytes 69206016
  81.7 1.0 copy-start.5
  82.6 35.1 %collective-permute-start = (bf16[1024,128]{1,0:T(8,128)(2,1)S(1)}, bf16[1024,128]{1,0:T(8,128)(2,1)S(1)}, u32[]{:S(2)}, u32[]{:S(2)}) collective-permute-start(bf16[1024,128]{1,0:T(8,128)(2,1)S(1)} %get-tuple-element.34), channel_id=1, source_target_pairs={{0,4},{4,0},{1,5},{5,1},{2,6},{6,2},{3,7},{7,3},{8,12},{12,8},{9,1... | collective-permute-start | bytes 786440 | tf_op jit(solution)/shard_map/ppermute | solution.py:572

commit v4 on v3

--- a/solution.py
+++ b/solution.py
@@ -12,7 +12,6 @@
 BF16 = jnp.bfloat16
 UNROLL = 88
 LAG = 4
-LOADS = 16
 MIB = 1024 * 1024
 
 
@@ -54,32 +53,39 @@
             copy.wait_send()
 
 
-def add_tiles(count, tiles, total, product, target, fetched=lambda g: None):
+def add_tiles(count, tiles, held, sems, total, product, target):
     spare = total.shape[0] - 1
+    groups = lax.div(count + UNROLL - 1, UNROLL)
+
+    def fetch(g):
+        at = pl.ds(g * UNROLL, UNROLL)
+        return pltpu.make_async_copy(tiles.at[at], held.at[at], sems.at[g])
+
+    def start_step(g, carry):
+        fetch(g).start()
+        return carry
+
+    lax.fori_loop(0, groups, start_step, 0)
     total[...] = jnp.zeros_like(total)
 
     def group_step(g, carry):
-        fetched(g)
+        fetch(g).wait()
         start = g * UNROLL
         waiting = {}
         for u in range(UNROLL + LAG):
             if u < UNROLL:
-                waiting[u] = product(start + u, tiles[start + u])
+                waiting[u] = product(start + u, held[start + u])
             if u >= LAG:
                 slot = start + u - LAG
                 total[jnp.where(slot < count, target(slot), spare)] += waiting.pop(u - LAG)
         return carry
 
-    lax.fori_loop(0, groups(count), group_step, 0)
-
-
-def groups(count):
-    return lax.div(count + UNROLL - 1, UNROLL)
-
-
-def forward_kernel(rows, cols, count_ref, window, tiles, out, total):
+    lax.fori_loop(0, groups, group_step, 0)
+
+
+def forward_kernel(rows, cols, count_ref, window, tiles, out, held, total, sems):
     add_tiles(
-        count_ref[0], tiles, total,
+        count_ref[0], tiles, held, sems, total,
         lambda slot, tile: jnp.dot(tile, window[cols[slot]], preferred_element_type=F32),
         lambda slot: rows[slot],
     )
@@ -87,20 +93,10 @@
 
 
 def backward_kernel(rows, cols, count_ref, grads, tiles, out, held, total, sems):
-    def fetch(g):
-        at = pl.ds(g * UNROLL, UNROLL)
-        return pltpu.make_async_copy(tiles.at[at], held.at[at], sems.at[g])
-
-    def start(g, carry):
-        fetch(g).start()
-        return carry
-
-    lax.fori_loop(0, groups(count_ref[0]), start, 0)
     add_tiles(
-        count_ref[0], held, total,
+        count_ref[0], tiles, held, sems, total,
         lambda slot, tile: jnp.dot(grads[rows[slot]], tile, preferred_element_type=F32),
         lambda slot: cols[slot],
-        lambda g: fetch(g).wait(),
     )
     out[...] = total[: out.shape[0]].astype(BF16)
 
@@ -110,43 +106,31 @@
 HBM = pl.BlockSpec(memory_space=pltpu.HBM)
 
 
-def tile_sum(kernel, blocks, tile_rows, tile_cols, tile_count, source, tiles, tiles_spec, scratch, limit):
+def tile_sum(kernel, blocks, tile_rows, tile_cols, tile_count, source, tiles):
     slots, size, _ = tiles.shape
     return pl.pallas_call(
         kernel,
         out_shape=pltpu.VMEM((blocks, size, size), BF16),
-        in_specs=[SMEM] * 3 + [VMEM, tiles_spec],
+        in_specs=[SMEM] * 3 + [VMEM, HBM],
         out_specs=VMEM,
-        scratch_shapes=scratch,
-        compiler_params=pltpu.CompilerParams(vmem_limit_bytes=limit),
+        scratch_shapes=[
+            pltpu.VMEM(tiles.shape, BF16),
+            pltpu.VMEM((blocks + 1, size, size), F32),
+            pltpu.SemaphoreType.DMA((slots // UNROLL,)),
+        ],
+        compiler_params=pltpu.CompilerParams(vmem_limit_bytes=32 * MIB),
         cost_estimate=pl.CostEstimate(flops=2 * slots * size**3, bytes_accessed=slots * 2 * size**2, transcendentals=0),
         name=kernel.__name__.replace("kernel", "sum"),
     )(tile_rows, tile_cols, tile_count, source, tiles)
 
 
-def forward_sum(tile_rows, tile_cols, tile_count, window, held):
-    blocks, size, half = window.shape
-    scratch = [pltpu.VMEM((blocks // 3 + 1, size, half), F32)]
-    return tile_sum(forward_kernel, blocks // 3, tile_rows, tile_cols, tile_count, window, held, VMEM, scratch, 24 * MIB)
-
-
-def backward_sum(tile_rows, tile_cols, tile_count, grads, tiles):
-    blocks, half, size = grads.shape
-    scratch = [
-        pltpu.VMEM(tiles.shape, BF16),
-        pltpu.VMEM((3 * blocks + 1, half, size), F32),
-        pltpu.SemaphoreType.DMA((tiles.shape[0] // UNROLL,)),
-    ]
-    return tile_sum(backward_kernel, 3 * blocks, tile_rows, tile_cols, tile_count, grads, tiles, HBM, scratch, 50 * MIB)
-
-
 HALO_CHUNKS = 4
 
 
 def halo_kernel(
-    features, cotangent, w_self, w_neigh, bias, tiles,
-    window, held, own_far, cot_far, w_self_far, w_neigh_far, bias_far,
-    load_sems, send_sems, recv_sems,
+    features, cotangent, w_self, w_neigh, bias,
+    window, own_far, cot_far, w_self_far, w_neigh_far, bias_far,
+    load_sem, send_sems, recv_sems,
 ):
     row, col, edge, core, _ = place()
     rows = lax.axis_size("row")
@@ -172,30 +156,23 @@
         send(w_neigh, w_neigh_far, partner),
         send(bias, bias_far, partner),
     ]
-    many = tiles.shape[0] // LOADS
-    loads = [pltpu.make_async_copy(features, window.at[pl.ds(blocks, blocks)], load_sems.at[LOADS])]
-    for i in range(LOADS):
-        at = pl.ds(i * many, many)
-        loads.append(pltpu.make_async_copy(tiles.at[at], held.at[at], load_sems.at[i]))
-    for load in loads:
-        load.start()
+    load = pltpu.make_async_copy(features, window.at[pl.ds(blocks, blocks)], load_sem)
+    load.start()
     handed = []
     for landing, copy in arriving:
         copy.wait_recv()
         handed.append(send(window.at[landing], window.at[landing], twin))
     for copy in swaps + handed:
         copy.wait_recv()
-    for load in loads:
-        load.wait()
+    load.wait()
     send.finish()
 
 
-def exchange_inputs(features, cotangent, w_self, w_neigh, bias, tiles):
+def exchange_inputs(features, cotangent, w_self, w_neigh, bias):
     blocks, size, half = features.shape
     share = blocks // 8
     shapes = [
         jax.ShapeDtypeStruct((3 * blocks, size, half), BF16),
-        tiles,
         jax.ShapeDtypeStruct((share, size, half), BF16),
         jax.ShapeDtypeStruct((share, size, half), BF16),
         w_self, w_neigh, bias,
@@ -204,16 +181,16 @@
     return pl.pallas_call(
         halo_kernel,
         out_shape=[pltpu.VMEM(s.shape, s.dtype) for s in shapes],
-        in_specs=[HBM] * 6,
-        out_specs=[VMEM] * 7,
+        in_specs=[HBM] * 5,
+        out_specs=[VMEM] * 6,
         scratch_shapes=[
-            pltpu.SemaphoreType.DMA((LOADS + 1,)),
+            pltpu.SemaphoreType.DMA,
             pltpu.SemaphoreType.DMA((copies,)),
             pltpu.SemaphoreType.DMA((copies,)),
         ],
-        compiler_params=pltpu.CompilerParams(collective_id=1, has_side_effects=True, vmem_limit_bytes=24 * MIB),
+        compiler_params=pltpu.CompilerParams(collective_id=1, has_side_effects=True, vmem_limit_bytes=32 * MIB),
         name="exchange_inputs",
-    )(features, cotangent, w_self, w_neigh, bias, tiles)
+    )(features, cotangent, w_self, w_neigh, bias)
 
 
 def mid_kernel(
@@ -406,7 +383,7 @@
             pltpu.SemaphoreType.DMA((copies,)),
             pltpu.SemaphoreType.DMA((copies,)),
         ],
-        compiler_params=pltpu.CompilerParams(collective_id=2, has_side_effects=True, vmem_limit_bytes=8 * MIB),
+        compiler_params=pltpu.CompilerParams(collective_id=2, has_side_effects=True, vmem_limit_bytes=32 * MIB),
         name="middle",
     )(partial, features, own_far, cotangent, cot_far, w_self, w_neigh, w_self_far, w_neigh_far, bias, bias_far)
 
@@ -508,7 +485,7 @@
             pltpu.SemaphoreType.DMA((copies,)),
             pltpu.SemaphoreType.DMA((copies,)),
         ],
-        compiler_params=pltpu.CompilerParams(collective_id=3, has_side_effects=True, vmem_limit_bytes=8 * MIB),
+        compiler_params=pltpu.CompilerParams(collective_id=3, has_side_effects=True, vmem_limit_bytes=32 * MIB),
         name="finish",
     )(back, weight_sum)
 
@@ -562,15 +539,18 @@
     own = features.reshape(blocks, size, half)
     cot = cotangent.reshape(-1, size, half)
     bias_row = bias.reshape(1, half)
-    window, held, own_far, cot_far, w_self_far, w_neigh_far, bias_far = exchange_inputs(
-        own, cot, w_self, w_neigh, bias_row, tiles
-    )
-    partial = forward_sum(tile_rows, tile_cols, tile_count, window, held)
+    own, cot, w_self, w_neigh, bias_row = (
+        pltpu.with_memory_space_constraint(array, pltpu.HBM) for array in (own, cot, w_self, w_neigh, bias_row)
+    )
+    window, own_far, cot_far, w_self_far, w_neigh_far, bias_far = exchange_inputs(
+        own, cot, w_self, w_neigh, bias_row
+    )
+    partial = tile_sum(forward_kernel, blocks, tile_rows, tile_cols, tile_count, window, tiles)
     grads, out_near, self_near, weight_sum, far = middle(
         partial, own, own_far, cot, cot_far, w_self, w_neigh, w_self_far, w_neigh_far, bias_row, bias_far
     )
     far = lax.ppermute(far, "col", [(0, 1), (1, 0)])
-    back = backward_sum(tile_rows, tile_cols, tile_count, grads, tiles)
+    back = tile_sum(backward_kernel, 3 * blocks, tile_rows, tile_cols, tile_count, grads, tiles)
     sums, weights, bias_total = finish(back, weight_sum)
     output, features_grad, w_self_grad, w_neigh_grad, bias_grad = written(
         scale, out_near, self_near, far, sums, weights, bias_total

time: 120 us -> 104 us (0.87)
  local copies, waits for them, and re-layouts: 20.7 us -> 1.38 us
  Pallas kernels: 94.3 us -> 98.6 us
    unnamed x22 -> x8, local copies, waits for them, and re-layouts: 20.7 us -> 1.38 us
    pallas_call x1, Pallas kernels: 25.9 us -> 28.4 us  [finish(): pl.pallas_call(final_kernel, out_shape=[pltpu.VMEM(piece, F32), pltpu.VME...]
    pallas_call x2, Pallas kernels: 11 us -> 12.2 us  [tile_sum(): pl.pallas_call(kernel, out_shape=pltpu.VMEM((blocks, size, size), BF16),...]
  transfers between devices with their start and end apart: 1 -> 1, of which waited for: 0 -> 0; matrix products, arithmetic and copies ran while one was open for 0% -> 0% of each run, Pallas kernels for 27% -> 34%
where the time goes in v4:
time: 104 us; the launch traced here: 103 us
  Pallas kernels  98.6 us (95%)
  starting transfers between devices  1.85 us (2%)
  local copies, waits for them, and re-layouts  1.38 us (1%)
  between operations  1.34 us (1%)
    pallas_call x1, Pallas kernels, middle(): pl.pallas_call(mid_kernel, out_shape=[pltpu.VMEM((blocks, half, size), BF...  32.5 us
    pallas_call x1, Pallas kernels, finish(): pl.pallas_call(final_kernel, out_shape=[pltpu.VMEM(piece, F32), pltpu.VME...  28.4 us
    pallas_call x1, Pallas kernels, exchange_inputs(): pl.pallas_call(halo_kernel, out_shape=[pltpu.VMEM(s.shape, s.dtype) for s...  24.3 us
    pallas_call x2, Pallas kernels, tile_sum(): pl.pallas_call(kernel, out_shape=pltpu.VMEM((blocks, size, size), BF16),...  12.2 us
  transfers between devices with their start and end apart: 1, of which 0 were waited for; matrix products, arithmetic and copies ran while one was open for 0% of the time, Pallas kernels for 34%

profile of v4, /device:TPU:1, one launch (start us, length us, event | category | flops | bytes accessed | tf_op | source)
XLA Modules:
  0.0 103.2 jit_solution(13220003755782314317)
XLA Ops:
  1.3 24.3 %exchange_inputs.1 = (bf16[96,128,128]{2,1,0:T(8,128)(2,1)S(1)}, bf16[4,128,128]{2,1,0:T(8,128)(2,1)S(1)}, bf16[4,128,128]{2,1,0:T(8,128)(2,1)S(1)}, bf16[256,12...) custom-call(bf16[32,128,128]{2,1,0:T(8,128)(2,1)} %bitcast.4, bf16[8,128,128]{2,1,0:T(8,128)(2,1)} %bitcast.6, ...), custom_call_target="tpu_custom_call" | custom-call | tf_op jit(solution)/shard_map/exchange_inputs/pallas_call | solution.py:181
  25.6 0.0 copy-start
  25.6 0.7 copy-done
  26.3 0.0 copy-start.2
  26.3 0.7 copy-done.2
  27.0 0.0 copy-start.1
  27.0 0.0 copy-start.3
  27.0 5.9 %forward_sum.1.partial = bf16[32,128,128]{2,1,0:T(8,128)(2,1)S(1)} custom-call(s32[704]{0:T(1024)S(1)} %copy-done, s32[704]{0:T(1024)S(1)} %copy-done.2, s32[1]{0:T(128)S(6)} %copy.14.count_ref, bf16[96,128,128]{2,1,0:T(8,128)(2,1)S(1)} %get-tuple-element.24.window, bf16[704,128,128]{2,1,0:T(8,128)(2,1)} %tiles.3), custom_call_target="tpu_custom_call" | custom-call | flops 2952790016 | bytes 23068672 | tf_op jit(solution)/shard_map/forward_sum/pallas_call | solution.py:111
  32.9 32.5 %middle.1 = (bf16[32,128,128]{2,1,0:T(8,128)(2,1)S(1)}, bf16[512,128]{1,0:T(8,128)(2,1)S(1)}, f32[512,128]{1,0:T(8,128)S(1)}, f32[2,24,128]{2,1,0:T(8,128)S(1)}, bf16[1024,128]{1,0:T(8,128)(2,1)S(1)}) custom-call(bf16[32,128,128]{2,1,0:T(8,128)(2,1)S(1)} %forward_sum.1.partial, bf16[32,128,128]{2,1,0:T(8,128)(2,1)} %bitcast.5, ...), custom_call_target="tpu_custom_call" | custom-call | tf_op jit(solution)/shard_map/middle/pallas_call | solution.py:355
  65.4 1.8 %collective-permute-start = (bf16[1024,128]{1,0:T(8,128)(2,1)S(1)}, bf16[1024,128]{1,0:T(8,128)(2,1)S(1)}, u32[]{:S(2)}, u32[]{:S(2)}) collective-permute-start(bf16[1024,128]{1,0:T(8,128)(2,1)S(1)} %get-tuple-element.32), channel_id=1, source_target_pairs={{0,4},{4,0},{1,5},{5,1},{2,6},{6,2},{3,7},{7,3},{8,12},{12,8},{9,1... | collective-permute-start | bytes 786440 | tf_op jit(solution)/shard_map/ppermute | solution.py:552
  67.3 0.0 copy-done.1
  67.3 0.0 copy-done.3
  67.3 6.3 %backward_sum.1.back = bf16[96,128,128]{2,1,0:T(8,128)(2,1)S(1)} custom-call(s32[704]{0:T(1024)S(1)} %copy-done.1, s32[704]{0:T(1024)S(1)} %copy-done.3, s32[1]{0:T(128)S(6)} %copy.14.count_ref, bf16[32,128,128]{2,1,0:T(8,128)(2,1)S(1)} %get-tuple-element.33.grads, bf16[704,128,128]{2,1,0:T(8,128)(2,1)} %tiles.3), custom_call_target="tpu_custom_call" | custom-call | flops 2952790016 | bytes 23068672 | tf_op jit(solution)/shard_map/backward_sum/pallas_call | solution.py:111
  73.6 28.4 %finish.1 = (f32[8,128,128]{2,1,0:T(8,128)S(1)}, f32[512,128]{1,0:T(8,128)S(1)}, f32[16,128]{1,0:T(8,128)S(1)}) custom-call(bf16[96,128,128]{2,1,0:T(8,128)(2,1)S(1)} %backward_sum.1.back, f32[2,24,128]{2,1,0:T(8,128)S(1)} %get-tuple-element.34.weight_sum), custom_call_target="tpu_custom_call" | custom-call | tf_op jit(solution)/shard_map/finish/pallas_call | solution.py:468
  102.0 0.0 collective-permute-done.far
  102.0 1.1 %written.1 = (bf16[1024,128]{1,0:T(8,128)(2,1)}, f32[1024,128]{1,0:T(8,128)}, f32[256,128]{1,0:T(8,128)}, f32[256,128]{1,0:T(8,128)}, f32[1,128]{1,0:T(1,128)}) custom-call(bf16[512,128]{1,0:T(8,128)(2,1)S(1)} %get-tuple-element.30.out_near, f32[512,128]{1,0:T(8,128)S(1)} %get-tuple-element.31.self_near, bf16[1024,128]{1,0:T(8,128)(2,1)S(1)} %collective-permute-done.far, ...), custom_call_target="tpu_custom_call" | custom-call | tf_op jit(solution)/shard_map/written/pallas_call | solution.py:516
Async XLA Ops:
  25.6 0.7 copy-start
  26.3 0.7 copy-start.2
  27.0 40.3 %copy-start.1 = (s32[704]{0:T(1024)S(1)}, s32[704]{0:T(1024)}, u32[]{:S(2)}) copy-start(s32[704]{0:T(1024)} %rows.3) | copy-start | bytes 8452
  27.0 40.3 %copy-start.3 = (s32[704]{0:T(1024)S(1)}, s32[704]{0:T(1024)}, u32[]{:S(2)}) copy-start(s32[704]{0:T(1024)} %cols.3) | copy-start | bytes 8452
  65.4 36.6 %collective-permute-start = (bf16[1024,128]{1,0:T(8,128)(2,1)S(1)}, bf16[1024,128]{1,0:T(8,128)(2,1)S(1)}, u32[]{:S(2)}, u32[]{:S(2)}) collective-permute-start(bf16[1024,128]{1,0:T(8,128)(2,1)S(1)} %get-tuple-element.32), channel_id=1, source_target_pairs={{0,4},{4,0},{1,5},{5,1},{2,6},{6,2},{3,7},{7,3},{8,12},{12,8},{9,1... | collective-permute-start | bytes 786440 | tf_op jit(solution)/shard_map/ppermute | solution.py:552

commit v5 on v4

--- a/solution.py
+++ b/solution.py
@@ -196,8 +196,8 @@
 def mid_kernel(
     partial, features, own_far, cotangent, cot_far, w_self, w_neigh, w_self_far, w_neigh_far, bias, bias_far,
     grads, out_near, self_near, weight_sum, far,
-    got_core, sent_pair, kept, got_pair, sent_col, got_col, own, cot, weights, sent_grads,
-    w_all, w_bias, w_sent_x, w_got_x, w_sent_z, w_got_z, w_sent_e, w_got_e,
+    got_core, sent, got, own, cot, weights, sent_grads,
+    w_all, w_bias, w_sent_z, w_got_z, w_sent_x, w_got_x,
     local_sems, send_sems, recv_sems,
 ):
     row, col, edge, core, pair_side = place()
@@ -207,10 +207,8 @@
     x, z = lax.rem(row, 4), lax.div(row, 4)
     along_x = [lax.rem(x + j, 4) for j in (1, 2, 3)]
     along_z = [lax.rem(z + j, 4) for j in (1, 2, 3)]
-    along_e = [lax.rem(edge + j, 4) for j in (1, 2, 3)]
     x_peers = [{"row": z * 4 + to} for to in along_x]
     z_peers = [{"row": to * 4 + x} for to in along_z]
-    e_peers = [{"edge": to} for to in along_e]
     blocks, size, half = partial.shape
     share = blocks // 8
     near_rows = own_far.shape[0] * size
@@ -220,13 +218,13 @@
     ]
     for copy in local:
         copy.start()
-    greet([partner, diagonal] + e_peers + x_peers + z_peers)
+    greet([twin, pair, partner, diagonal] + x_peers + z_peers)
     send = Sender(send_sems, recv_sems)
 
     def piece(side, on_core, column):
         return pl.ds((2 * side + on_core) * 2 * share + column * share, share)
 
-    order = [(1 - pair_side, other), (1 - pair_side, col), (pair_side, other), (pair_side, col)]
+    order = [(pair_side, other), (1 - pair_side, other), (1 - pair_side, col), (pair_side, col)]
     to_twin = [
         send(partial.at[piece(side, 1 - core, column)], got_core.at[i], twin)
         for i, (side, column) in enumerate(order)
@@ -243,26 +241,23 @@
         side, column = order[i]
         return partial[piece(side, core, column)].astype(F32) + got_core[i].astype(F32)
 
-    to_pair = []
-    for i in range(2):
-        sent_pair[i] = summed(i).astype(BF16)
-        to_pair.append(send(sent_pair.at[i], got_pair.at[i], pair))
-    for i in range(2):
-        kept[i] = summed(2 + i)
-    to_pair[0].wait_recv()
-    sent_col[...] = (kept[0] + got_pair[0].astype(F32)).astype(BF16)
-    to_partner = send(sent_col, got_col, partner)
+    crossing = []
+    for i, owner in enumerate((partner, diagonal, pair)):
+        sent[i] = summed(i).astype(BF16)
+        crossing.append(send(sent.at[i], got.at[i], owner))
+    kept = summed(3)
     for copy in local:
         copy.wait()
-    to_pair[1].wait_recv()
-    agg_near = (kept[1] + got_pair[1].astype(F32)).astype(BF16)
-    to_partner.wait_recv()
+    for copy in crossing:
+        copy.wait_recv()
+    agg_near = (kept + got[2].astype(F32)).astype(BF16)
+    agg_far = (got[0].astype(F32) + got[1].astype(F32)).astype(BF16)
 
     def flat(blocks_of):
         return blocks_of.reshape(near_rows, half)
 
     mixed = jnp.concatenate(
-        [flat(own[...]), flat(own_far[...]), flat(agg_near), flat(got_col[...])], axis=1
+        [flat(own[...]), flat(own_far[...]), flat(agg_near), flat(agg_far)], axis=1
     )
     pre = jnp.dot(mixed, weights[...], preferred_element_type=F32) + jnp.concatenate(
         [bias[...], bias_far[...]], axis=1
@@ -309,11 +304,10 @@
         w_all[at, :] += got3[0, :many] + got3[1, :many] + got3[2, :many]
         w_bias[...] += got3[0, many:] + got3[1, many:] + got3[2, many:]
 
-    x_many, z_many, e_many = 4 * half // 4, 4 * half // 16, 4 * half // 64
-    x_start = pl.multiple_of(x * x_many, 8)
-    z_start = pl.multiple_of(x_start + z * z_many, 8)
-    e_start = pl.multiple_of(z_start + edge * e_many, 8)
-    steps = spread(0, x_many, w_sent_x, w_got_x, along_x, x_peers)
+    z_many, x_many = 4 * half // 4, 4 * half // 16
+    z_start = pl.multiple_of(z * z_many, 8)
+    x_start = pl.multiple_of(z_start + x * x_many, 8)
+    steps = spread(0, z_many, w_sent_z, w_got_z, along_z, z_peers)
 
     output = (pre * sigm).astype(BF16)
     out_near[...] = output[:, :half]
@@ -322,8 +316,8 @@
     self_near[...] = self_back[:, :half]
     far[near_rows:] = self_back[:, half:].astype(BF16)
 
-    collect(x_start, x_many, w_got_x, steps)
-    steps = spread(x_start, z_many, w_sent_z, w_got_z, along_z, z_peers)
+    collect(z_start, z_many, w_got_z, steps)
+    steps = spread(z_start, x_many, w_sent_x, w_got_x, along_x, x_peers)
 
     far_edge = lax.rem(edge + 2, 4)
     homes = [
@@ -334,12 +328,10 @@
     for k in (1, 2, 0):
         crossing[k].wait_recv()
         handed.append(send(grads.at[homes[k]], grads.at[homes[k]], twin))
-    collect(z_start, z_many, w_got_z, steps)
-    steps = spread(z_start, e_many, w_sent_e, w_got_e, along_e, e_peers)
-    collect(e_start, e_many, w_got_e, steps)
+    collect(x_start, x_many, w_got_x, steps)
     for j in range(2):
-        weight_sum[j, :e_many] = w_all[pl.ds(e_start, e_many), j * half : (j + 1) * half]
-        weight_sum[j, e_many:] = w_bias[:, j * half : (j + 1) * half]
+        weight_sum[j, :x_many] = w_all[pl.ds(x_start, x_many), j * half : (j + 1) * half]
+        weight_sum[j, x_many:] = w_bias[:, j * half : (j + 1) * half]
     for copy in handed:
         copy.wait_recv()
     send.finish()
@@ -349,7 +341,7 @@
     blocks, size, half = partial.shape
     share = blocks // 8
     rows = share * size
-    copies = 4 + 2 + 1 + 3 + 4 + 9
+    copies = 4 + 3 + 3 + 4 + 6
     top = 4 * half
     piece = (share, size, half)
     return pl.pallas_call(
@@ -358,18 +350,15 @@
             pltpu.VMEM((blocks, half, size), BF16),
             pltpu.VMEM((rows, half), BF16),
             pltpu.VMEM((rows, half), F32),
-            pltpu.VMEM((2, top // 64 + 16, half), F32),
+            pltpu.VMEM((2, top // 16 + 16, half), F32),
             jax.ShapeDtypeStruct((2 * rows, half), BF16),
         ],
         in_specs=[VMEM, HBM, VMEM, HBM] + [VMEM] * 7,
         out_specs=[VMEM] * 5,
         scratch_shapes=[
             pltpu.VMEM((4,) + piece, BF16),
-            pltpu.VMEM((2,) + piece, BF16),
-            pltpu.VMEM((2,) + piece, F32),
-            pltpu.VMEM((2,) + piece, BF16),
-            pltpu.VMEM(piece, BF16),
-            pltpu.VMEM(piece, BF16),
+            pltpu.VMEM((3,) + piece, BF16),
+            pltpu.VMEM((3,) + piece, BF16),
             pltpu.VMEM(piece, BF16),
             pltpu.VMEM(piece, BF16),
             pltpu.VMEM((4 * half, 2 * half), BF16),
@@ -378,7 +367,6 @@
             pltpu.VMEM((16, 2 * half), F32),
             *[pltpu.VMEM((3, top // 4 + 16, 2 * half), BF16)] * 2,
             *[pltpu.VMEM((3, top // 16 + 16, 2 * half), F32)] * 2,
-            *[pltpu.VMEM((3, top // 64 + 16, 2 * half), F32)] * 2,
             pltpu.SemaphoreType.DMA((2,)),
             pltpu.SemaphoreType.DMA((copies,)),
             pltpu.SemaphoreType.DMA((copies,)),
@@ -391,18 +379,19 @@
 def final_kernel(
     back, weight_sum,
     sums, weights, bias_total,
-    got_core, sent_row, kept, got_row, sent_pair, got_pair, got_col,
+    got_core, sent_row, kept, got_row, sent_pair, got_pair, w_sent, w_got,
     send_sems, recv_sems,
 ):
     row, col, edge, core, side = place()
     rows = lax.axis_size("row")
     x, z = lax.rem(row, 4), lax.div(row, 4)
-    twin, pair, partner = {"edge": edge + 1 - 2 * core}, {"edge": lax.rem(edge + 2, 4)}, {"col": 1 - col}
+    twin, pair = {"edge": edge + 1 - 2 * core}, {"edge": lax.rem(edge + 2, 4)}
     up, down = {"row": lax.rem(row + 1, rows)}, {"row": lax.rem(row + rows - 1, rows)}
     x_peers = [{"row": z * 4 + lax.rem(x + j, 4)} for j in (1, 2, 3)]
     z_peers = [{"row": lax.rem(z + j, 4) * 4 + x} for j in (1, 2, 3)]
     e_peers = [{"edge": lax.rem(edge + j, 4)} for j in (1, 2, 3)]
-    greet([partner, up, down] + e_peers + x_peers + z_peers)
+    far_peers = [{"edge": lax.rem(edge + j, 4), "col": 1 - col} for j in range(4)]
+    greet([up, down] + e_peers + far_peers + x_peers + z_peers)
     send = Sender(send_sems, recv_sems)
     blocks = back.shape[0] // 3
     share = blocks // 4
@@ -414,7 +403,15 @@
     to_twin = [
         send(back.at[piece(part, at, 1 - core)], got_core.at[i], twin) for i, (part, at) in enumerate(order)
     ]
-    to_partner = send(weight_sum.at[1], got_col, partner)
+
+    top = weights.shape[0]
+    many, bias_at = top // 64, top // 16
+    to_group = []
+    for i, peer in enumerate(e_peers + far_peers):
+        j, owner = (0, lax.rem(edge + 1 + i, 4)) if i < 3 else (1, lax.rem(edge + i - 3, 4))
+        w_sent[i, :many] = weight_sum[j, pl.ds(pl.multiple_of(owner * many, 8), many), :]
+        w_sent[i, many:] = weight_sum[j, bias_at:]
+        to_group.append(send(w_sent.at[i], w_got.at[i], peer))
 
     def summed(i):
         to_twin[i].wait_recv()
@@ -426,12 +423,14 @@
         sent_row[i] = summed(i).astype(BF16)
         to_row.append(send(sent_row.at[i], got_row.at[i], down if i % 2 == 0 else up))
 
-    top = weights.shape[0]
-    many = top // 64
-    to_partner.wait_recv()
-    start = pl.multiple_of(x * (top // 4) + z * (top // 16) + edge * many, 8)
-    weights[pl.ds(start, many), :] = weight_sum[0, :many] + got_col[:many]
-    bias_total[...] = weight_sum[0, many:] + got_col[many:]
+    for copy in to_group:
+        copy.wait_recv()
+    group_total = w_got[0]
+    for i in range(1, 7):
+        group_total += w_got[i]
+    start = pl.multiple_of(z * (top // 4) + x * (top // 16) + edge * many, 8)
+    weights[pl.ds(start, many), :] = weight_sum[0, pl.ds(pl.multiple_of(edge * many, 8), many), :] + group_total[:many]
+    bias_total[...] = weight_sum[0, bias_at:] + group_total[many:]
 
     def gathered(start, many, peers):
         at = pl.ds(pl.multiple_of(start, 8), many)
@@ -442,14 +441,14 @@
         kept[i] = summed(4 + i)
     for step in steps:
         step.wait_recv()
-    steps = gathered(x * (top // 4) + z * (top // 16), top // 16, z_peers)
+    steps = gathered(z * (top // 4) + x * (top // 16), top // 16, x_peers)
     for i in range(2):
         to_row[i].wait_recv()
     sent_pair[...] = (kept[0] + got_row[0].astype(F32) + got_row[1].astype(F32)).astype(BF16)
     to_pair = send(sent_pair, got_pair, pair)
     for step in steps:
         step.wait_recv()
-    steps = gathered(x * (top // 4), top // 4, x_peers)
+    steps = gathered(z * (top // 4), top // 4, z_peers)
     for i in range(2, 4):
         to_row[i].wait_recv()
     kept[1] += got_row[2].astype(F32) + got_row[3].astype(F32)
@@ -462,8 +461,8 @@
 
 def finish(back, weight_sum):
     share, half, size = back.shape[0] // 12, back.shape[1], back.shape[2]
-    unit = weight_sum.shape[1]
-    copies = 6 + 4 + 1 + 1 + 9
+    unit = half // 16 + 16
+    copies = 6 + 4 + 1 + 7 + 9
     piece = (share, half, size)
     return pl.pallas_call(
         final_kernel,
@@ -481,7 +480,7 @@
             pltpu.VMEM((4,) + piece, BF16),
             pltpu.VMEM(piece, BF16),
             pltpu.VMEM(piece, BF16),
-            pltpu.VMEM((unit, half), F32),
+            *[pltpu.VMEM((7, unit, half), F32)] * 2,
             pltpu.SemaphoreType.DMA((copies,)),
             pltpu.SemaphoreType.DMA((copies,)),
         ],

time: 104 us -> 98.8 us (0.950)
  Pallas kernels: 98.6 us -> 93.9 us
    pallas_call x1, Pallas kernels: 32.5 us -> 26.3 us  [middle(): pl.pallas_call(mid_kernel, out_shape=[pltpu.VMEM((blocks, half, size), BF...]
    pallas_call x1, Pallas kernels: 28.4 us -> 29.9 us  [finish(): pl.pallas_call(final_kernel, out_shape=[pltpu.VMEM(piece, F32), pltpu.VME...]
  transfers between devices with their start and end apart: 1 -> 1, of which waited for: 0 -> 0; matrix products, arithmetic and copies ran while one was open for 0% -> 0% of each run, Pallas kernels for 34% -> 37%
where the time goes in v5:
time: 98.8 us; the launch traced here: 98.1 us
  Pallas kernels  93.9 us (95%)
  starting transfers between devices  1.5 us (2%)
  local copies, waits for them, and re-layouts  1.38 us (1%)
  between operations  1.34 us (1%)
    pallas_call x1, Pallas kernels, finish(): pl.pallas_call(final_kernel, out_shape=[pltpu.VMEM(piece, F32), pltpu.VME...  29.9 us
    pallas_call x1, Pallas kernels, middle(): pl.pallas_call(mid_kernel, out_shape=[pltpu.VMEM((blocks, half, size), BF...  26.3 us
    pallas_call x1, Pallas kernels, exchange_inputs(): pl.pallas_call(halo_kernel, out_shape=[pltpu.VMEM(s.shape, s.dtype) for s...  24.3 us
    pallas_call x2, Pallas kernels, tile_sum(): pl.pallas_call(kernel, out_shape=pltpu.VMEM((blocks, size, size), BF16),...  12.2 us
  transfers between devices with their start and end apart: 1, of which 0 were waited for; matrix products, arithmetic and copies ran while one was open for 0% of the time, Pallas kernels for 37%

profile of v5, /device:TPU:1, one launch (start us, length us, event | category | flops | bytes accessed | tf_op | source)
XLA Modules:
  0.0 98.1 jit_solution(638080961130933785)
XLA Ops:
  1.3 24.3 %exchange_inputs.1 = (bf16[96,128,128]{2,1,0:T(8,128)(2,1)S(1)}, bf16[4,128,128]{2,1,0:T(8,128)(2,1)S(1)}, bf16[4,128,128]{2,1,0:T(8,128)(2,1)S(1)}, bf16[256,12...) custom-call(bf16[32,128,128]{2,1,0:T(8,128)(2,1)} %bitcast.4, bf16[8,128,128]{2,1,0:T(8,128)(2,1)} %bitcast.6, ...), custom_call_target="tpu_custom_call" | custom-call | tf_op jit(solution)/shard_map/exchange_inputs/pallas_call | solution.py:181
  25.6 0.0 copy-start
  25.6 0.7 copy-done
  26.3 0.0 copy-start.2
  26.3 0.7 copy-done.2
  27.0 0.0 copy-start.1
  27.0 0.0 copy-start.3
  27.0 5.9 %forward_sum.1.partial = bf16[32,128,128]{2,1,0:T(8,128)(2,1)S(1)} custom-call(s32[704]{0:T(1024)S(1)} %copy-done, s32[704]{0:T(1024)S(1)} %copy-done.2, s32[1]{0:T(128)S(6)} %copy.14.count_ref, bf16[96,128,128]{2,1,0:T(8,128)(2,1)S(1)} %get-tuple-element.24.window, bf16[704,128,128]{2,1,0:T(8,128)(2,1)} %tiles.3), custom_call_target="tpu_custom_call" | custom-call | flops 2952790016 | bytes 23068672 | tf_op jit(solution)/shard_map/forward_sum/pallas_call | solution.py:111
  32.9 26.3 %middle.1 = (bf16[32,128,128]{2,1,0:T(8,128)(2,1)S(1)}, bf16[512,128]{1,0:T(8,128)(2,1)S(1)}, f32[512,128]{1,0:T(8,128)S(1)}, f32[2,48,128]{2,1,0:T(8,128)S(1)}, bf16[1024,128]{1,0:T(8,128)(2,1)S(1)}) custom-call(bf16[32,128,128]{2,1,0:T(8,128)(2,1)S(1)} %forward_sum.1.partial, bf16[32,128,128]{2,1,0:T(8,128)(2,1)} %bitcast.5, ...), custom_call_target="tpu_custom_call" | custom-call | tf_op jit(solution)/shard_map/middle/pallas_call | solution.py:347
  59.3 1.5 %collective-permute-start = (bf16[1024,128]{1,0:T(8,128)(2,1)S(1)}, bf16[1024,128]{1,0:T(8,128)(2,1)S(1)}, u32[]{:S(2)}, u32[]{:S(2)}) collective-permute-start(bf16[1024,128]{1,0:T(8,128)(2,1)S(1)} %get-tuple-element.32), channel_id=1, source_target_pairs={{0,4},{4,0},{1,5},{5,1},{2,6},{6,2},{3,7},{7,3},{8,12},{12,8},{9,1... | collective-permute-start | bytes 786440 | tf_op jit(solution)/shard_map/ppermute | solution.py:551
  60.8 0.0 copy-done.1
  60.8 0.0 copy-done.3
  60.8 6.3 %backward_sum.1.back = bf16[96,128,128]{2,1,0:T(8,128)(2,1)S(1)} custom-call(s32[704]{0:T(1024)S(1)} %copy-done.1, s32[704]{0:T(1024)S(1)} %copy-done.3, s32[1]{0:T(128)S(6)} %copy.14.count_ref, bf16[32,128,128]{2,1,0:T(8,128)(2,1)S(1)} %get-tuple-element.33.grads, bf16[704,128,128]{2,1,0:T(8,128)(2,1)} %tiles.3), custom_call_target="tpu_custom_call" | custom-call | flops 2952790016 | bytes 23068672 | tf_op jit(solution)/shard_map/backward_sum/pallas_call | solution.py:111
  67.1 29.9 %finish.1 = (f32[8,128,128]{2,1,0:T(8,128)S(1)}, f32[512,128]{1,0:T(8,128)S(1)}, f32[16,128]{1,0:T(8,128)S(1)}) custom-call(bf16[96,128,128]{2,1,0:T(8,128)(2,1)S(1)} %backward_sum.1.back, f32[2,48,128]{2,1,0:T(8,128)S(1)} %get-tuple-element.34.weight_sum), custom_call_target="tpu_custom_call" | custom-call | tf_op jit(solution)/shard_map/finish/pallas_call | solution.py:467
  97.0 0.0 collective-permute-done.far
  97.0 1.1 %written.1 = (bf16[1024,128]{1,0:T(8,128)(2,1)}, f32[1024,128]{1,0:T(8,128)}, f32[256,128]{1,0:T(8,128)}, f32[256,128]{1,0:T(8,128)}, f32[1,128]{1,0:T(1,128)}) custom-call(bf16[512,128]{1,0:T(8,128)(2,1)S(1)} %get-tuple-element.30.out_near, f32[512,128]{1,0:T(8,128)S(1)} %get-tuple-element.31.self_near, bf16[1024,128]{1,0:T(8,128)(2,1)S(1)} %collective-permute-done.far, ...), custom_call_target="tpu_custom_call" | custom-call | tf_op jit(solution)/shard_map/written/pallas_call | solution.py:515
Async XLA Ops:
  25.6 0.7 copy-start
  26.3 0.7 copy-start.2
  27.0 33.8 %copy-start.1 = (s32[704]{0:T(1024)S(1)}, s32[704]{0:T(1024)}, u32[]{:S(2)}) copy-start(s32[704]{0:T(1024)} %rows.3) | copy-start | bytes 8452
  27.0 33.8 %copy-start.3 = (s32[704]{0:T(1024)S(1)}, s32[704]{0:T(1024)}, u32[]{:S(2)}) copy-start(s32[704]{0:T(1024)} %cols.3) | copy-start | bytes 8452
  59.3 37.7 %collective-permute-start = (bf16[1024,128]{1,0:T(8,128)(2,1)S(1)}, bf16[1024,128]{1,0:T(8,128)(2,1)S(1)}, u32[]{:S(2)}, u32[]{:S(2)}) collective-permute-start(bf16[1024,128]{1,0:T(8,128)(2,1)S(1)} %get-tuple-element.32), channel_id=1, source_target_pairs={{0,4},{4,0},{1,5},{5,1},{2,6},{6,2},{3,7},{7,3},{8,12},{12,8},{9,1... | collective-permute-start | bytes 786440 | tf_op jit(solution)/shard_map/ppermute | solution.py:551

commit v6 on v5

--- a/solution.py
+++ b/solution.py
@@ -197,7 +197,7 @@
     partial, features, own_far, cotangent, cot_far, w_self, w_neigh, w_self_far, w_neigh_far, bias, bias_far,
     grads, out_near, self_near, weight_sum, far,
     got_core, sent, got, own, cot, weights, sent_grads,
-    w_all, w_bias, w_sent_z, w_got_z, w_sent_x, w_got_x,
+    w_all, w_bias, w_sent_z, w_got_z, w_got_x,
     local_sems, send_sems, recv_sems,
 ):
     row, col, edge, core, pair_side = place()
@@ -205,9 +205,8 @@
     twin, pair, partner = {"edge": edge + 1 - 2 * core}, {"edge": lax.rem(edge + 2, 4)}, {"col": other}
     diagonal = {"edge": lax.rem(edge + 2, 4), "col": other}
     x, z = lax.rem(row, 4), lax.div(row, 4)
-    along_x = [lax.rem(x + j, 4) for j in (1, 2, 3)]
     along_z = [lax.rem(z + j, 4) for j in (1, 2, 3)]
-    x_peers = [{"row": z * 4 + to} for to in along_x]
+    x_peers = [{"row": z * 4 + lax.rem(x + j, 4)} for j in (1, 2, 3)]
     z_peers = [{"row": to * 4 + x} for to in along_z]
     blocks, size, half = partial.shape
     share = blocks // 8
@@ -288,26 +287,14 @@
             w_all[pl.ds(pl.multiple_of(2 * k * half + start, half), half), :] = parts[at : at + half, :]
     w_bias[...] = jnp.sum(grad_pre.reshape(near_rows // 16, 16, 2 * half), axis=0)
 
-    def spread(start, many, sent, got, targets, peers):
-        steps = []
-        for j in range(3):
-            sent[j, :many] = w_all[pl.ds(pl.multiple_of(start + targets[j] * many, 8), many), :].astype(sent.dtype)
-            sent[j, many:] = w_bias[...].astype(sent.dtype)
-            steps.append(send(sent.at[j], got.at[j], peers[j]))
-        return steps
-
-    def collect(start, many, got, steps):
-        for j in range(3):
-            steps[j].wait_recv()
-        at = pl.ds(start, many)
-        got3 = got[...].astype(F32)
-        w_all[at, :] += got3[0, :many] + got3[1, :many] + got3[2, :many]
-        w_bias[...] += got3[0, many:] + got3[1, many:] + got3[2, many:]
-
-    z_many, x_many = 4 * half // 4, 4 * half // 16
+    z_many = 4 * half // 4
     z_start = pl.multiple_of(z * z_many, 8)
-    x_start = pl.multiple_of(z_start + x * x_many, 8)
-    steps = spread(0, z_many, w_sent_z, w_got_z, along_z, z_peers)
+    steps = []
+    for j in range(3):
+        w_sent_z[j, :z_many] = w_all[pl.ds(pl.multiple_of(along_z[j] * z_many, 8), z_many), :].astype(BF16)
+        w_sent_z[j, z_many:] = w_bias[...].astype(BF16)
+        steps.append(send(w_sent_z.at[j], w_got_z.at[z], z_peers[j]))
+    w_got_z[z, z_many:] = w_bias[...].astype(BF16)
 
     output = (pre * sigm).astype(BF16)
     out_near[...] = output[:, :half]
@@ -316,8 +303,17 @@
     self_near[...] = self_back[:, :half]
     far[near_rows:] = self_back[:, half:].astype(BF16)
 
-    collect(z_start, z_many, w_got_z, steps)
-    steps = spread(z_start, x_many, w_sent_x, w_got_x, along_x, x_peers)
+    for step in steps:
+        step.wait_recv()
+    quarter = w_all[pl.ds(z_start, z_many), :]
+    for j in range(3):
+        quarter += w_got_z[along_z[j], :z_many].astype(F32)
+    bias_sum = w_got_z[0, z_many:].astype(F32)
+    for j in range(1, 4):
+        bias_sum += w_got_z[j, z_many:].astype(F32)
+    w_got_x[x, :z_many] = quarter.astype(BF16)
+    w_got_x[x, z_many:] = bias_sum.astype(BF16)
+    steps = [send(w_got_x.at[x], w_got_x.at[x], peer) for peer in x_peers]
 
     far_edge = lax.rem(edge + 2, 4)
     homes = [
@@ -328,10 +324,13 @@
     for k in (1, 2, 0):
         crossing[k].wait_recv()
         handed.append(send(grads.at[homes[k]], grads.at[homes[k]], twin))
-    collect(x_start, x_many, w_got_x, steps)
+    for step in steps:
+        step.wait_recv()
+    x_total = w_got_x[0].astype(F32)
+    for j in range(1, 4):
+        x_total += w_got_x[j].astype(F32)
     for j in range(2):
-        weight_sum[j, :x_many] = w_all[pl.ds(x_start, x_many), j * half : (j + 1) * half]
-        weight_sum[j, x_many:] = w_bias[:, j * half : (j + 1) * half]
+        weight_sum[j] = x_total[:, j * half : (j + 1) * half]
     for copy in handed:
         copy.wait_recv()
     send.finish()
@@ -350,7 +349,7 @@
             pltpu.VMEM((blocks, half, size), BF16),
             pltpu.VMEM((rows, half), BF16),
             pltpu.VMEM((rows, half), F32),
-            pltpu.VMEM((2, top // 16 + 16, half), F32),
+            pltpu.VMEM((2, top // 4 + 16, half), F32),
             jax.ShapeDtypeStruct((2 * rows, half), BF16),
         ],
         in_specs=[VMEM, HBM, VMEM, HBM] + [VMEM] * 7,
@@ -365,8 +364,9 @@
             pltpu.VMEM((share, half, size), BF16),
             pltpu.VMEM((top, 2 * half), F32),
             pltpu.VMEM((16, 2 * half), F32),
-            *[pltpu.VMEM((3, top // 4 + 16, 2 * half), BF16)] * 2,
-            *[pltpu.VMEM((3, top // 16 + 16, 2 * half), F32)] * 2,
+            pltpu.VMEM((3, top // 4 + 16, 2 * half), BF16),
+            pltpu.VMEM((4, top // 4 + 16, 2 * half), BF16),
+            pltpu.VMEM((4, top // 4 + 16, 2 * half), BF16),
             pltpu.SemaphoreType.DMA((2,)),
             pltpu.SemaphoreType.DMA((copies,)),
             pltpu.SemaphoreType.DMA((copies,)),
@@ -387,11 +387,10 @@
     x, z = lax.rem(row, 4), lax.div(row, 4)
     twin, pair = {"edge": edge + 1 - 2 * core}, {"edge": lax.rem(edge + 2, 4)}
     up, down = {"row": lax.rem(row + 1, rows)}, {"row": lax.rem(row + rows - 1, rows)}
-    x_peers = [{"row": z * 4 + lax.rem(x + j, 4)} for j in (1, 2, 3)]
     z_peers = [{"row": lax.rem(z + j, 4) * 4 + x} for j in (1, 2, 3)]
     e_peers = [{"edge": lax.rem(edge + j, 4)} for j in (1, 2, 3)]
     far_peers = [{"edge": lax.rem(edge + j, 4), "col": 1 - col} for j in range(4)]
-    greet([up, down] + e_peers + far_peers + x_peers + z_peers)
+    greet([up, down] + e_peers + far_peers + z_peers)
     send = Sender(send_sems, recv_sems)
     blocks = back.shape[0] // 3
     share = blocks // 4
@@ -404,8 +403,18 @@
         send(back.at[piece(part, at, 1 - core)], got_core.at[i], twin) for i, (part, at) in enumerate(order)
     ]
 
+    def summed(i):
+        to_twin[i].wait_recv()
+        part, at = order[i]
+        return back[piece(part, at, core)].astype(F32) + got_core[i].astype(F32)
+
+    to_row = []
+    for i in range(4):
+        sent_row[i] = summed(i).astype(BF16)
+        to_row.append(send(sent_row.at[i], got_row.at[i], down if i % 2 == 0 else up))
+
     top = weights.shape[0]
-    many, bias_at = top // 64, top // 16
+    many, bias_at = top // 16, top // 4
     to_group = []
     for i, peer in enumerate(e_peers + far_peers):
         j, owner = (0, lax.rem(edge + 1 + i, 4)) if i < 3 else (1, lax.rem(edge + i - 3, 4))
@@ -413,22 +422,12 @@
         w_sent[i, many:] = weight_sum[j, bias_at:]
         to_group.append(send(w_sent.at[i], w_got.at[i], peer))
 
-    def summed(i):
-        to_twin[i].wait_recv()
-        part, at = order[i]
-        return back[piece(part, at, core)].astype(F32) + got_core[i].astype(F32)
-
-    to_row = []
-    for i in range(4):
-        sent_row[i] = summed(i).astype(BF16)
-        to_row.append(send(sent_row.at[i], got_row.at[i], down if i % 2 == 0 else up))
-
     for copy in to_group:
         copy.wait_recv()
     group_total = w_got[0]
     for i in range(1, 7):
         group_total += w_got[i]
-    start = pl.multiple_of(z * (top // 4) + x * (top // 16) + edge * many, 8)
+    start = pl.multiple_of(z * (top // 4) + edge * many, 8)
     weights[pl.ds(start, many), :] = weight_sum[0, pl.ds(pl.multiple_of(edge * many, 8), many), :] + group_total[:many]
     bias_total[...] = weight_sum[0, bias_at:] + group_total[many:]
 
@@ -441,14 +440,11 @@
         kept[i] = summed(4 + i)
     for step in steps:
         step.wait_recv()
-    steps = gathered(z * (top // 4) + x * (top // 16), top // 16, x_peers)
+    steps = gathered(z * (top // 4), top // 4, z_peers)
     for i in range(2):
         to_row[i].wait_recv()
     sent_pair[...] = (kept[0] + got_row[0].astype(F32) + got_row[1].astype(F32)).astype(BF16)
     to_pair = send(sent_pair, got_pair, pair)
-    for step in steps:
-        step.wait_recv()
-    steps = gathered(z * (top // 4), top // 4, z_peers)
     for i in range(2, 4):
         to_row[i].wait_recv()
     kept[1] += got_row[2].astype(F32) + got_row[3].astype(F32)
@@ -461,8 +457,8 @@
 
 def finish(back, weight_sum):
     share, half, size = back.shape[0] // 12, back.shape[1], back.shape[2]
-    unit = half // 16 + 16
-    copies = 6 + 4 + 1 + 7 + 9
+    unit = half // 4 + 16
+    copies = 6 + 4 + 1 + 7 + 6
     piece = (share, half, size)
     return pl.pallas_call(
         final_kernel,
@@ -538,8 +534,9 @@
     own = features.reshape(blocks, size, half)
     cot = cotangent.reshape(-1, size, half)
     bias_row = bias.reshape(1, half)
-    own, cot, w_self, w_neigh, bias_row = (
-        pltpu.with_memory_space_constraint(array, pltpu.HBM) for array in (own, cot, w_self, w_neigh, bias_row)
+    own, cot, w_self, w_neigh, bias_row, tile_rows, tile_cols = (
+        pltpu.with_memory_space_constraint(array, pltpu.HBM)
+        for array in (own, cot, w_self, w_neigh, bias_row, tile_rows, tile_cols)
     )
     window, own_far, cot_far, w_self_far, w_neigh_far, bias_far = exchange_inputs(
         own, cot, w_self, w_neigh, bias_row

time: 98.8 us -> 94.4 us (0.955)
  Pallas kernels: 93.9 us -> 90.8 us
  local copies, waits for them, and re-layouts: 1.38 us -> 0 us
    pallas_call x2, Pallas kernels: 12.2 us -> 23.7 us  [tile_sum(): pl.pallas_call(kernel, out_shape=pltpu.VMEM((blocks, size, size), BF16),...]
    pallas_call x1, Pallas kernels: 29.9 us -> 20.8 us  [finish(): pl.pallas_call(final_kernel, out_shape=[pltpu.VMEM(piece, F32), pltpu.VME...]
    pallas_call x1, Pallas kernels: 26.3 us -> 20.8 us  [middle(): pl.pallas_call(mid_kernel, out_shape=[pltpu.VMEM((blocks, half, size), BF...]
    unnamed x8 -> x0, local copies, waits for them, and re-layouts: 1.38 us -> none
  transfers between devices with their start and end apart: 1 -> 1, of which waited for: 0 -> 0; matrix products, arithmetic and copies ran while one was open for 0% -> 0% of each run, Pallas kernels for 37% -> 35%
where the time goes in v6:
time: 94.4 us; the launch traced here: 94.2 us
  Pallas kernels  90.8 us (96%)
  starting transfers between devices  2.13 us (2%)
  between operations  1.33 us (1%)
    pallas_call x1, Pallas kernels, exchange_inputs(): pl.pallas_call(halo_kernel, out_shape=[pltpu.VMEM(s.shape, s.dtype) for s...  24.3 us
    pallas_call x2, Pallas kernels, tile_sum(): pl.pallas_call(kernel, out_shape=pltpu.VMEM((blocks, size, size), BF16),...  23.7 us
    pallas_call x1, Pallas kernels, middle(): pl.pallas_call(mid_kernel, out_shape=[pltpu.VMEM((blocks, half, size), BF...  20.8 us
    pallas_call x1, Pallas kernels, finish(): pl.pallas_call(final_kernel, out_shape=[pltpu.VMEM(piece, F32), pltpu.VME...  20.8 us
    ppermute x1, starting transfers between devices, local(): far = lax.ppermute(far, 'col', [(0, 1), (1, 0)])  2.13 us
  transfers between devices with their start and end apart: 1, of which 0 were waited for; matrix products, arithmetic and copies ran while one was open for 0% of the time, Pallas kernels for 35%

profile of v6, /device:TPU:1, one launch (start us, length us, event | category | flops | bytes accessed | tf_op | source)
XLA Modules:
  0.0 94.2 jit_solution(1190554421420512002)
XLA Ops:
  1.3 24.3 %exchange_inputs.1 = (bf16[96,128,128]{2,1,0:T(8,128)(2,1)S(1)}, bf16[4,128,128]{2,1,0:T(8,128)(2,1)S(1)}, bf16[4,128,128]{2,1,0:T(8,128)(2,1)S(1)}, bf16[256,12...) custom-call(bf16[32,128,128]{2,1,0:T(8,128)(2,1)} %bitcast.4, bf16[8,128,128]{2,1,0:T(8,128)(2,1)} %bitcast.6, ...), custom_call_target="tpu_custom_call" | custom-call | tf_op jit(solution)/shard_map/exchange_inputs/pallas_call | solution.py:181
  25.6 11.5 %forward_sum.1.partial = bf16[32,128,128]{2,1,0:T(8,128)(2,1)S(1)} custom-call(s32[704]{0:T(1024)} %rows.3, s32[704]{0:T(1024)} %cols.3, s32[1]{0:T(128)S(6)} %copy.14.count_ref, bf16[96,128,128]{2,1,0:T(8,128)(2,1)S(1)} %get-tuple-element.24.window, bf16[704,128,128]{2,1,0:T(8,128)(2,1)} %tiles.3), custom_call_target="tpu_custom_call" | custom-call | flops 2952790016 | bytes 23068672 | tf_op jit(solution)/shard_map/forward_sum/pallas_call | solution.py:111
  37.2 20.8 %middle.1 = (bf16[32,128,128]{2,1,0:T(8,128)(2,1)S(1)}, bf16[512,128]{1,0:T(8,128)(2,1)S(1)}, f32[512,128]{1,0:T(8,128)S(1)}, f32[2,144,128]{2,1,0:T(8,128)S(1)}, bf16[1024,128]{1,0:T(8,128)(2,1)S(1)}) custom-call(bf16[32,128,128]{2,1,0:T(8,128)(2,1)S(1)} %forward_sum.1.partial, bf16[32,128,128]{2,1,0:T(8,128)(2,1)} %bitcast.5, ...), custom_call_target="tpu_custom_call" | custom-call | tf_op jit(solution)/shard_map/middle/pallas_call | solution.py:346
  58.0 2.1 %collective-permute-start = (bf16[1024,128]{1,0:T(8,128)(2,1)S(1)}, bf16[1024,128]{1,0:T(8,128)(2,1)S(1)}, u32[]{:S(2)}, u32[]{:S(2)}) collective-permute-start(bf16[1024,128]{1,0:T(8,128)(2,1)S(1)} %get-tuple-element.32), channel_id=1, source_target_pairs={{0,4},{4,0},{1,5},{5,1},{2,6},{6,2},{3,7},{7,3},{8,12},{12,8},{9,1... | collective-permute-start | bytes 786440 | tf_op jit(solution)/shard_map/ppermute | solution.py:548
  60.1 12.2 %backward_sum.1.back = bf16[96,128,128]{2,1,0:T(8,128)(2,1)S(1)} custom-call(s32[704]{0:T(1024)} %rows.3, s32[704]{0:T(1024)} %cols.3, s32[1]{0:T(128)S(6)} %copy.14.count_ref, bf16[32,128,128]{2,1,0:T(8,128)(2,1)S(1)} %get-tuple-element.33.grads, bf16[704,128,128]{2,1,0:T(8,128)(2,1)} %tiles.3), custom_call_target="tpu_custom_call" | custom-call | flops 2952790016 | bytes 23068672 | tf_op jit(solution)/shard_map/backward_sum/pallas_call | solution.py:111
  72.3 20.8 %finish.1 = (f32[8,128,128]{2,1,0:T(8,128)S(1)}, f32[512,128]{1,0:T(8,128)S(1)}, f32[16,128]{1,0:T(8,128)S(1)}) custom-call(bf16[96,128,128]{2,1,0:T(8,128)(2,1)S(1)} %backward_sum.1.back, f32[2,144,128]{2,1,0:T(8,128)S(1)} %get-tuple-element.34.weight_sum), custom_call_target="tpu_custom_call" | custom-call | tf_op jit(solution)/shard_map/finish/pallas_call | solution.py:463
  93.1 0.0 collective-permute-done.far
  93.1 1.1 %written.1 = (bf16[1024,128]{1,0:T(8,128)(2,1)}, f32[1024,128]{1,0:T(8,128)}, f32[256,128]{1,0:T(8,128)}, f32[256,128]{1,0:T(8,128)}, f32[1,128]{1,0:T(1,128)}) custom-call(bf16[512,128]{1,0:T(8,128)(2,1)S(1)} %get-tuple-element.30.out_near, f32[512,128]{1,0:T(8,128)S(1)} %get-tuple-element.31.self_near, bf16[1024,128]{1,0:T(8,128)(2,1)S(1)} %collective-permute-done.far, ...), custom_call_target="tpu_custom_call" | custom-call | tf_op jit(solution)/shard_map/written/pallas_call | solution.py:511
Async XLA Ops:
  58.0 35.1 %collective-permute-start = (bf16[1024,128]{1,0:T(8,128)(2,1)S(1)}, bf16[1024,128]{1,0:T(8,128)(2,1)S(1)}, u32[]{:S(2)}, u32[]{:S(2)}) collective-permute-start(bf16[1024,128]{1,0:T(8,128)(2,1)S(1)} %get-tuple-element.32), channel_id=1, source_target_pairs={{0,4},{4,0},{1,5},{5,1},{2,6},{6,2},{3,7},{7,3},{8,12},{12,8},{9,1... | collective-permute-start | bytes 786440 | tf_op jit(solution)/shard_map/ppermute | solution.py:548

commit v7 on v6

--- a/solution.py
+++ b/solution.py
@@ -53,48 +53,52 @@
             copy.wait_send()
 
 
-def add_tiles(count, tiles, held, sems, total, product, target):
+def add_tiles(count, head, tiles, held, sems, total, product, target):
     spare = total.shape[0] - 1
     groups = lax.div(count + UNROLL - 1, UNROLL)
 
     def fetch(g):
         at = pl.ds(g * UNROLL, UNROLL)
-        return pltpu.make_async_copy(tiles.at[at], held.at[at], sems.at[g])
+        return pltpu.make_async_copy(tiles.at[at], held.at[pl.ds((g - 1) * UNROLL, UNROLL)], sems.at[g - 1])
 
     def start_step(g, carry):
         fetch(g).start()
         return carry
 
-    lax.fori_loop(0, groups, start_step, 0)
+    lax.fori_loop(1, groups, start_step, 0)
     total[...] = jnp.zeros_like(total)
 
-    def group_step(g, carry):
-        fetch(g).wait()
-        start = g * UNROLL
+    def add_group(source, first, start):
         waiting = {}
         for u in range(UNROLL + LAG):
             if u < UNROLL:
-                waiting[u] = product(start + u, held[start + u])
+                waiting[u] = product(start + u, source[first + u])
             if u >= LAG:
                 slot = start + u - LAG
                 total[jnp.where(slot < count, target(slot), spare)] += waiting.pop(u - LAG)
+
+    add_group(head, 0, 0)
+
+    def group_step(g, carry):
+        fetch(g).wait()
+        add_group(held, (g - 1) * UNROLL, g * UNROLL)
         return carry
 
-    lax.fori_loop(0, groups, group_step, 0)
-
-
-def forward_kernel(rows, cols, count_ref, window, tiles, out, held, total, sems):
+    lax.fori_loop(1, groups, group_step, 0)
+
+
+def forward_kernel(rows, cols, count_ref, window, head, tiles, out, held, total, sems):
     add_tiles(
-        count_ref[0], tiles, held, sems, total,
+        count_ref[0], head, tiles, held, sems, total,
         lambda slot, tile: jnp.dot(tile, window[cols[slot]], preferred_element_type=F32),
         lambda slot: rows[slot],
     )
     out[...] = total[: out.shape[0]].astype(BF16)
 
 
-def backward_kernel(rows, cols, count_ref, grads, tiles, out, held, total, sems):
+def backward_kernel(rows, cols, count_ref, grads, head, tiles, out, held, total, sems):
     add_tiles(
-        count_ref[0], tiles, held, sems, total,
+        count_ref[0], head, tiles, held, sems, total,
         lambda slot, tile: jnp.dot(grads[rows[slot]], tile, preferred_element_type=F32),
         lambda slot: cols[slot],
     )
@@ -106,31 +110,31 @@
 HBM = pl.BlockSpec(memory_space=pltpu.HBM)
 
 
-def tile_sum(kernel, blocks, tile_rows, tile_cols, tile_count, source, tiles):
+def tile_sum(kernel, blocks, tile_rows, tile_cols, tile_count, source, head, tiles):
     slots, size, _ = tiles.shape
     return pl.pallas_call(
         kernel,
         out_shape=pltpu.VMEM((blocks, size, size), BF16),
-        in_specs=[SMEM] * 3 + [VMEM, HBM],
+        in_specs=[SMEM] * 3 + [VMEM, VMEM, HBM],
         out_specs=VMEM,
         scratch_shapes=[
-            pltpu.VMEM(tiles.shape, BF16),
+            pltpu.VMEM((slots - UNROLL, size, size), BF16),
             pltpu.VMEM((blocks + 1, size, size), F32),
-            pltpu.SemaphoreType.DMA((slots // UNROLL,)),
+            pltpu.SemaphoreType.DMA((slots // UNROLL - 1,)),
         ],
         compiler_params=pltpu.CompilerParams(vmem_limit_bytes=32 * MIB),
         cost_estimate=pl.CostEstimate(flops=2 * slots * size**3, bytes_accessed=slots * 2 * size**2, transcendentals=0),
         name=kernel.__name__.replace("kernel", "sum"),
-    )(tile_rows, tile_cols, tile_count, source, tiles)
+    )(tile_rows, tile_cols, tile_count, source, head, tiles)
 
 
 HALO_CHUNKS = 4
 
 
 def halo_kernel(
-    features, cotangent, w_self, w_neigh, bias,
-    window, own_far, cot_far, w_self_far, w_neigh_far, bias_far,
-    load_sem, send_sems, recv_sems,
+    features, cotangent, w_self, w_neigh, bias, tiles,
+    window, head, own_far, cot_far, w_self_far, w_neigh_far, bias_far,
+    load_sems, send_sems, recv_sems,
 ):
     row, col, edge, core, _ = place()
     rows = lax.axis_size("row")
@@ -156,23 +160,29 @@
         send(w_neigh, w_neigh_far, partner),
         send(bias, bias_far, partner),
     ]
-    load = pltpu.make_async_copy(features, window.at[pl.ds(blocks, blocks)], load_sem)
-    load.start()
+    loads = [
+        pltpu.make_async_copy(features, window.at[pl.ds(blocks, blocks)], load_sems.at[0]),
+        pltpu.make_async_copy(tiles.at[pl.ds(0, UNROLL)], head, load_sems.at[1]),
+    ]
+    for load in loads:
+        load.start()
     handed = []
     for landing, copy in arriving:
         copy.wait_recv()
         handed.append(send(window.at[landing], window.at[landing], twin))
     for copy in swaps + handed:
         copy.wait_recv()
-    load.wait()
+    for load in loads:
+        load.wait()
     send.finish()
 
 
-def exchange_inputs(features, cotangent, w_self, w_neigh, bias):
+def exchange_inputs(features, cotangent, w_self, w_neigh, bias, tiles):
     blocks, size, half = features.shape
     share = blocks // 8
     shapes = [
         jax.ShapeDtypeStruct((3 * blocks, size, half), BF16),
+        jax.ShapeDtypeStruct((UNROLL,) + tiles.shape[1:], BF16),
         jax.ShapeDtypeStruct((share, size, half), BF16),
         jax.ShapeDtypeStruct((share, size, half), BF16),
         w_self, w_neigh, bias,
@@ -181,21 +191,21 @@
     return pl.pallas_call(
         halo_kernel,
         out_shape=[pltpu.VMEM(s.shape, s.dtype) for s in shapes],
-        in_specs=[HBM] * 5,
-        out_specs=[VMEM] * 6,
+        in_specs=[HBM] * 6,
+        out_specs=[VMEM] * 7,
         scratch_shapes=[
-            pltpu.SemaphoreType.DMA,
+            pltpu.SemaphoreType.DMA((2,)),
             pltpu.SemaphoreType.DMA((copies,)),
             pltpu.SemaphoreType.DMA((copies,)),
         ],
         compiler_params=pltpu.CompilerParams(collective_id=1, has_side_effects=True, vmem_limit_bytes=32 * MIB),
         name="exchange_inputs",
-    )(features, cotangent, w_self, w_neigh, bias)
+    )(features, cotangent, w_self, w_neigh, bias, tiles)
 
 
 def mid_kernel(
-    partial, features, own_far, cotangent, cot_far, w_self, w_neigh, w_self_far, w_neigh_far, bias, bias_far,
-    grads, out_near, self_near, weight_sum, far,
+    partial, features, own_far, cotangent, cot_far, w_self, w_neigh, w_self_far, w_neigh_far, bias, bias_far, tiles,
+    grads, out_near, self_near, weight_sum, far, head,
     got_core, sent, got, own, cot, weights, sent_grads,
     w_all, w_bias, w_sent_z, w_got_z, w_got_x,
     local_sems, send_sems, recv_sems,
@@ -215,8 +225,10 @@
         pltpu.make_async_copy(features.at[pl.ds(edge * 2 * share + col * share, share)], own, local_sems.at[0]),
         pltpu.make_async_copy(cotangent.at[pl.ds(col * share, share)], cot, local_sems.at[1]),
     ]
+    ahead = pltpu.make_async_copy(tiles.at[pl.ds(0, UNROLL)], head, local_sems.at[2])
     for copy in local:
         copy.start()
+    ahead.start()
     greet([twin, pair, partner, diagonal] + x_peers + z_peers)
     send = Sender(send_sems, recv_sems)
 
@@ -333,10 +345,11 @@
         weight_sum[j] = x_total[:, j * half : (j + 1) * half]
     for copy in handed:
         copy.wait_recv()
+    ahead.wait()
     send.finish()
 
 
-def middle(partial, features, own_far, cotangent, cot_far, w_self, w_neigh, w_self_far, w_neigh_far, bias, bias_far):
+def middle(partial, features, own_far, cotangent, cot_far, w_self, w_neigh, w_self_far, w_neigh_far, bias, bias_far, tiles):
     blocks, size, half = partial.shape
     share = blocks // 8
     rows = share * size
@@ -350,10 +363,11 @@
             pltpu.VMEM((rows, half), BF16),
             pltpu.VMEM((rows, half), F32),
             pltpu.VMEM((2, top // 4 + 16, half), F32),
-            jax.ShapeDtypeStruct((2 * rows, half), BF16),
-        ],
-        in_specs=[VMEM, HBM, VMEM, HBM] + [VMEM] * 7,
-        out_specs=[VMEM] * 5,
+            pltpu.VMEM((2 * rows, half), BF16),
+            pltpu.VMEM((UNROLL,) + tiles.shape[1:], BF16),
+        ],
+        in_specs=[VMEM, HBM, VMEM, HBM] + [VMEM] * 7 + [HBM],
+        out_specs=[VMEM] * 6,
         scratch_shapes=[
             pltpu.VMEM((4,) + piece, BF16),
             pltpu.VMEM((3,) + piece, BF16),
@@ -367,18 +381,18 @@
             pltpu.VMEM((3, top // 4 + 16, 2 * half), BF16),
             pltpu.VMEM((4, top // 4 + 16, 2 * half), BF16),
             pltpu.VMEM((4, top // 4 + 16, 2 * half), BF16),
-            pltpu.SemaphoreType.DMA((2,)),
+            pltpu.SemaphoreType.DMA((3,)),
             pltpu.SemaphoreType.DMA((copies,)),
             pltpu.SemaphoreType.DMA((copies,)),
         ],
         compiler_params=pltpu.CompilerParams(collective_id=2, has_side_effects=True, vmem_limit_bytes=32 * MIB),
         name="middle",
-    )(partial, features, own_far, cotangent, cot_far, w_self, w_neigh, w_self_far, w_neigh_far, bias, bias_far)
+    )(partial, features, own_far, cotangent, cot_far, w_self, w_neigh, w_self_far, w_neigh_far, bias, bias_far, tiles)
 
 
 def final_kernel(
-    back, weight_sum,
-    sums, weights, bias_total,
+    back, weight_sum, far,
+    sums, weights, bias_total, far_got,
     got_core, sent_row, kept, got_row, sent_pair, got_pair, w_sent, w_got,
     send_sems, recv_sems,
 ):
@@ -403,6 +417,8 @@
         send(back.at[piece(part, at, 1 - core)], got_core.at[i], twin) for i, (part, at) in enumerate(order)
     ]
 
+    to_partner = send(far, far_got, far_peers[0])
+
     def summed(i):
         to_twin[i].wait_recv()
         part, at = order[i]
@@ -450,15 +466,16 @@
     kept[1] += got_row[2].astype(F32) + got_row[3].astype(F32)
     to_pair.wait_recv()
     sums[...] = kept[1] + got_pair[...].astype(F32)
+    to_partner.wait_recv()
     for step in steps:
         step.wait_recv()
     send.finish()
 
 
-def finish(back, weight_sum):
+def finish(back, weight_sum, far):
     share, half, size = back.shape[0] // 12, back.shape[1], back.shape[2]
     unit = half // 4 + 16
-    copies = 6 + 4 + 1 + 7 + 6
+    copies = 6 + 1 + 4 + 1 + 7 + 6
     piece = (share, half, size)
     return pl.pallas_call(
         final_kernel,
@@ -466,9 +483,10 @@
             pltpu.VMEM(piece, F32),
             pltpu.VMEM((4 * half, half), F32),
             pltpu.VMEM((16, half), F32),
-        ],
-        in_specs=[VMEM] * 2,
-        out_specs=[VMEM] * 3,
+            pltpu.VMEM(far.shape, BF16),
+        ],
+        in_specs=[VMEM] * 3,
+        out_specs=[VMEM] * 4,
         scratch_shapes=[
             pltpu.VMEM((6,) + piece, BF16),
             pltpu.VMEM((4,) + piece, BF16),
@@ -482,7 +500,7 @@
         ],
         compiler_params=pltpu.CompilerParams(collective_id=3, has_side_effects=True, vmem_limit_bytes=32 * MIB),
         name="finish",
-    )(back, weight_sum)
+    )(back, weight_sum, far)
 
 
 def writing_kernel(
@@ -534,20 +552,19 @@
     own = features.reshape(blocks, size, half)
     cot = cotangent.reshape(-1, size, half)
     bias_row = bias.reshape(1, half)
-    own, cot, w_self, w_neigh, bias_row, tile_rows, tile_cols = (
+    own, cot, w_self, w_neigh, bias_row, tile_rows, tile_cols, tiles = (
         pltpu.with_memory_space_constraint(array, pltpu.HBM)
-        for array in (own, cot, w_self, w_neigh, bias_row, tile_rows, tile_cols)
-    )
-    window, own_far, cot_far, w_self_far, w_neigh_far, bias_far = exchange_inputs(
-        own, cot, w_self, w_neigh, bias_row
-    )
-    partial = tile_sum(forward_kernel, blocks, tile_rows, tile_cols, tile_count, window, tiles)
-    grads, out_near, self_near, weight_sum, far = middle(
-        partial, own, own_far, cot, cot_far, w_self, w_neigh, w_self_far, w_neigh_far, bias_row, bias_far
-    )
-    far = lax.ppermute(far, "col", [(0, 1), (1, 0)])
-    back = tile_sum(backward_kernel, 3 * blocks, tile_rows, tile_cols, tile_count, grads, tiles)
-    sums, weights, bias_total = finish(back, weight_sum)
+        for array in (own, cot, w_self, w_neigh, bias_row, tile_rows, tile_cols, tiles)
+    )
+    window, head, own_far, cot_far, w_self_far, w_neigh_far, bias_far = exchange_inputs(
+        own, cot, w_self, w_neigh, bias_row, tiles
+    )
+    partial = tile_sum(forward_kernel, blocks, tile_rows, tile_cols, tile_count, window, head, tiles)
+    grads, out_near, self_near, weight_sum, far, head = middle(
+        partial, own, own_far, cot, cot_far, w_self, w_neigh, w_self_far, w_neigh_far, bias_row, bias_far, tiles
+    )
+    back = tile_sum(backward_kernel, 3 * blocks, tile_rows, tile_cols, tile_count, grads, head, tiles)
+    sums, weights, bias_total, far = finish(back, weight_sum, far)
     output, features_grad, w_self_grad, w_neigh_grad, bias_grad = written(
         scale, out_near, self_near, far, sums, weights, bias_total
     )

time: 94.4 us -> 93.4 us (0.989)
  starting transfers between devices: 2.13 us -> 0 us
  Pallas kernels: 90.8 us -> 91.8 us
    pallas_call x2, Pallas kernels: 23.7 us -> 7.95 us  [tile_sum(): pl.pallas_call(kernel, out_shape=pltpu.VMEM((blocks, size, size), BF16),...]
    pallas_call x1, Pallas kernels: 20.8 us -> 30.5 us  [finish(): pl.pallas_call(final_kernel, out_shape=[pltpu.VMEM(piece, F32), pltpu.VME...]
    pallas_call x1, Pallas kernels: 20.8 us -> 27.9 us  [middle(): pl.pallas_call(mid_kernel, out_shape=[pltpu.VMEM((blocks, half, size), BF...]
    ppermute x1 -> x0, starting transfers between devices: 2.13 us -> none  [local(): far = lax.ppermute(far, 'col', [(0, 1), (1, 0)])]
  transfers between devices with their start and end apart: 1 -> 0, of which waited for: 0 -> 0; matrix products, arithmetic and copies ran while one was open for 0% -> 0% of each run, Pallas kernels for 35% -> 0%
where the time goes in v7:
time: 93.4 us; the launch traced here: 93.1 us
  Pallas kernels  91.8 us (98%)
  between operations  1.32 us (1%)
    pallas_call x1, Pallas kernels, finish(): pl.pallas_call(final_kernel, out_shape=[pltpu.VMEM(piece, F32), pltpu.VME...  30.5 us
    pallas_call x1, Pallas kernels, middle(): pl.pallas_call(mid_kernel, out_shape=[pltpu.VMEM((blocks, half, size), BF...  27.9 us
    pallas_call x1, Pallas kernels, exchange_inputs(): pl.pallas_call(halo_kernel, out_shape=[pltpu.VMEM(s.shape, s.dtype) for s...  24.4 us
    pallas_call x2, Pallas kernels, tile_sum(): pl.pallas_call(kernel, out_shape=pltpu.VMEM((blocks, size, size), BF16),...  7.95 us

profile of v7, /device:TPU:1, one launch (start us, length us, event | category | flops | bytes accessed | tf_op | source)
XLA Modules:
  0.0 93.1 jit_solution(3021520470164506490)
XLA Ops:
  1.3 24.4 %exchange_inputs.1 = (bf16[96,128,128]{2,1,0:T(8,128)(2,1)S(1)}, bf16[88,128,128]{2,1,0:T(8,128)(2,1)S(1)}, bf16[4,128,128]{2,1,0:T(8,128)(2,1)S(1)}, bf16[4,128...) custom-call(bf16[32,128,128]{2,1,0:T(8,128)(2,1)} %bitcast.4, ...), custom_call_target="tpu_custom_call" | custom-call | tf_op jit(solution)/shard_map/exchange_inputs/pallas_call | solution.py:191
  25.6 3.8 %forward_sum.1.partial = bf16[32,128,128]{2,1,0:T(8,128)(2,1)S(1)} custom-call(s32[704]{0:T(1024)} %rows.3, s32[704]{0:T(1024)} %cols.3, s32[1]{0:T(128)S(6)} %copy.14.count_ref, bf16[96,128,128]{2,1,0:T(8,128)(2,1)S(1)} %get-tuple-element.27.window, bf16[88,128,128]{2,1,0:T(8,128)(2,1)S(1)} %get-tuple-element.28.head, bf16[704,128,128]{2,1,0:T(8,128)(2,1)} %tiles.7), custom_call_target="tpu_custom_call" | custom-call | flops 2952790016 | bytes 23068672 | tf_op jit(solution)/shard_map/forward_sum/pallas_call | solution.py:115
  29.5 27.9 %middle.1 = (bf16[32,128,128]{2,1,0:T(8,128)(2,1)S(1)}, bf16[512,128]{1,0:T(8,128)(2,1)S(1)}, f32[512,128]{1,0:T(8,128)S(1)}, f32[2,144,128]{2,1,0:T(8,128)S(1)}...) custom-call(bf16[32,128,128]{2,1,0:T(8,128)(2,1)S(1)} %forward_sum.1.partial, ...), custom_call_target="tpu_custom_call" | custom-call | tf_op jit(solution)/shard_map/middle/pallas_call | solution.py:359
  57.4 4.1 %backward_sum.1.back = bf16[96,128,128]{2,1,0:T(8,128)(2,1)S(1)} custom-call(s32[704]{0:T(1024)} %rows.3, s32[704]{0:T(1024)} %cols.3, s32[1]{0:T(128)S(6)} %copy.14.count_ref, bf16[32,128,128]{2,1,0:T(8,128)(2,1)S(1)} %get-tuple-element.36.grads, bf16[88,128,128]{2,1,0:T(8,128)(2,1)S(1)} %get-tuple-element.37.head, bf16[704,128,128]{2,1,0:T(8,128)(2,1)} %tiles.7), custom_call_target="tpu_custom_call" | custom-call | flops 2952790016 | bytes 23068672 | tf_op jit(solution)/shard_map/backward_sum/pallas_call | solution.py:115
  61.5 30.5 %finish.1 = (f32[8,128,128]{2,1,0:T(8,128)S(1)}, f32[512,128]{1,0:T(8,128)S(1)}, f32[16,128]{1,0:T(8,128)S(1)}, bf16[1024,128]{1,0:T(8,128)(2,1)S(1)}) custom-call(bf16[96,128,128]{2,1,0:T(8,128)(2,1)S(1)} %backward_sum.1.back, f32[2,144,128]{2,1,0:T(8,128)S(1)} %get-tuple-element.38.weight_sum, bf16[1024,128]{1,0:T(8,128)(2,1)S(1)} %get-tuple-element.39.far), custom_call_target="tpu_custom_call" | custom-call | tf_op jit(solution)/shard_map/finish/pallas_call | solution.py:480
  92.0 1.1 %written.1 = (bf16[1024,128]{1,0:T(8,128)(2,1)}, f32[1024,128]{1,0:T(8,128)}, f32[256,128]{1,0:T(8,128)}, f32[256,128]{1,0:T(8,128)}, f32[1,128]{1,0:T(1,128)}) custom-call(bf16[512,128]{1,0:T(8,128)(2,1)S(1)} %get-tuple-element.34.out_near, f32[512,128]{1,0:T(8,128)S(1)} %get-tuple-element.35.self_near, bf16[1024,128]{1,0:T(8,128)(2,1)S(1)} %get-tuple-element.40.far, ...), custom_call_target="tpu_custom_call" | custom-call | tf_op jit(solution)/shard_map/written/pallas_call | solution.py:529

commit v8 on v7

--- a/solution.py
+++ b/solution.py
@@ -417,17 +417,10 @@
         send(back.at[piece(part, at, 1 - core)], got_core.at[i], twin) for i, (part, at) in enumerate(order)
     ]
 
-    to_partner = send(far, far_got, far_peers[0])
-
     def summed(i):
         to_twin[i].wait_recv()
         part, at = order[i]
         return back[piece(part, at, core)].astype(F32) + got_core[i].astype(F32)
-
-    to_row = []
-    for i in range(4):
-        sent_row[i] = summed(i).astype(BF16)
-        to_row.append(send(sent_row.at[i], got_row.at[i], down if i % 2 == 0 else up))
 
     top = weights.shape[0]
     many, bias_at = top // 16, top // 4
@@ -438,6 +431,12 @@
         w_sent[i, many:] = weight_sum[j, bias_at:]
         to_group.append(send(w_sent.at[i], w_got.at[i], peer))
 
+    to_row = []
+    for i in range(4):
+        sent_row[i] = summed(i).astype(BF16)
+        to_row.append(send(sent_row.at[i], got_row.at[i], down if i % 2 == 0 else up))
+
+    to_partner = send(far, far_got, far_peers[0])
     for copy in to_group:
         copy.wait_recv()
     group_total = w_got[0]

time: 93.4 us -> 92.7 us (level)
    pallas_call x1, Pallas kernels: 30.5 us -> 27.6 us  [finish(): pl.pallas_call(final_kernel, out_shape=[pltpu.VMEM(piece, F32), pltpu.VME...]
    pallas_call x1, Pallas kernels: 27.9 us -> 30.1 us  [middle(): pl.pallas_call(mid_kernel, out_shape=[pltpu.VMEM((blocks, half, size), BF...]
where the time goes in v8:
time: 92.7 us; the launch traced here: 92.4 us
  Pallas kernels  91.1 us (98%)
  between operations  1.32 us (1%)
    pallas_call x1, Pallas kernels, middle(): pl.pallas_call(mid_kernel, out_shape=[pltpu.VMEM((blocks, half, size), BF...  30.1 us
    pallas_call x1, Pallas kernels, finish(): pl.pallas_call(final_kernel, out_shape=[pltpu.VMEM(piece, F32), pltpu.VME...  27.6 us
    pallas_call x1, Pallas kernels, exchange_inputs(): pl.pallas_call(halo_kernel, out_shape=[pltpu.VMEM(s.shape, s.dtype) for s...  24.4 us
    pallas_call x2, Pallas kernels, tile_sum(): pl.pallas_call(kernel, out_shape=pltpu.VMEM((blocks, size, size), BF16),...  7.96 us

profile of v8, /device:TPU:1, one launch (start us, length us, event | category | flops | bytes accessed | tf_op | source)
XLA Modules:
  0.0 92.4 jit_solution(10556805565787779987)
XLA Ops:
  1.3 24.4 %exchange_inputs.1 = (bf16[96,128,128]{2,1,0:T(8,128)(2,1)S(1)}, bf16[88,128,128]{2,1,0:T(8,128)(2,1)S(1)}, bf16[4,128,128]{2,1,0:T(8,128)(2,1)S(1)}, bf16[4,128...) custom-call(bf16[32,128,128]{2,1,0:T(8,128)(2,1)} %bitcast.4, ...), custom_call_target="tpu_custom_call" | custom-call | tf_op jit(solution)/shard_map/exchange_inputs/pallas_call | solution.py:191
  25.6 3.8 %forward_sum.1.partial = bf16[32,128,128]{2,1,0:T(8,128)(2,1)S(1)} custom-call(s32[704]{0:T(1024)} %rows.3, s32[704]{0:T(1024)} %cols.3, s32[1]{0:T(128)S(6)} %copy.14.count_ref, bf16[96,128,128]{2,1,0:T(8,128)(2,1)S(1)} %get-tuple-element.27.window, bf16[88,128,128]{2,1,0:T(8,128)(2,1)S(1)} %get-tuple-element.28.head, bf16[704,128,128]{2,1,0:T(8,128)(2,1)} %tiles.7), custom_call_target="tpu_custom_call" | custom-call | flops 2952790016 | bytes 23068672 | tf_op jit(solution)/shard_map/forward_sum/pallas_call | solution.py:115
  29.5 30.1 %middle.1 = (bf16[32,128,128]{2,1,0:T(8,128)(2,1)S(1)}, bf16[512,128]{1,0:T(8,128)(2,1)S(1)}, f32[512,128]{1,0:T(8,128)S(1)}, f32[2,144,128]{2,1,0:T(8,128)S(1)}...) custom-call(bf16[32,128,128]{2,1,0:T(8,128)(2,1)S(1)} %forward_sum.1.partial, ...), custom_call_target="tpu_custom_call" | custom-call | tf_op jit(solution)/shard_map/middle/pallas_call | solution.py:359
  59.6 4.1 %backward_sum.1.back = bf16[96,128,128]{2,1,0:T(8,128)(2,1)S(1)} custom-call(s32[704]{0:T(1024)} %rows.3, s32[704]{0:T(1024)} %cols.3, s32[1]{0:T(128)S(6)} %copy.14.count_ref, bf16[32,128,128]{2,1,0:T(8,128)(2,1)S(1)} %get-tuple-element.36.grads, bf16[88,128,128]{2,1,0:T(8,128)(2,1)S(1)} %get-tuple-element.37.head, bf16[704,128,128]{2,1,0:T(8,128)(2,1)} %tiles.7), custom_call_target="tpu_custom_call" | custom-call | flops 2952790016 | bytes 23068672 | tf_op jit(solution)/shard_map/backward_sum/pallas_call | solution.py:115
  63.7 27.6 %finish.1 = (f32[8,128,128]{2,1,0:T(8,128)S(1)}, f32[512,128]{1,0:T(8,128)S(1)}, f32[16,128]{1,0:T(8,128)S(1)}, bf16[1024,128]{1,0:T(8,128)(2,1)S(1)}) custom-call(bf16[96,128,128]{2,1,0:T(8,128)(2,1)S(1)} %backward_sum.1.back, f32[2,144,128]{2,1,0:T(8,128)S(1)} %get-tuple-element.38.weight_sum, bf16[1024,128]{1,0:T(8,128)(2,1)S(1)} %get-tuple-element.39.far), custom_call_target="tpu_custom_call" | custom-call | tf_op jit(solution)/shard_map/finish/pallas_call | solution.py:479
  91.3 1.1 %written.1 = (bf16[1024,128]{1,0:T(8,128)(2,1)}, f32[1024,128]{1,0:T(8,128)}, f32[256,128]{1,0:T(8,128)}, f32[256,128]{1,0:T(8,128)}, f32[1,128]{1,0:T(1,128)}) custom-call(bf16[512,128]{1,0:T(8,128)(2,1)S(1)} %get-tuple-element.34.out_near, f32[512,128]{1,0:T(8,128)S(1)} %get-tuple-element.35.self_near, bf16[1024,128]{1,0:T(8,128)(2,1)S(1)} %get-tuple-element.40.far, ...), custom_call_target="tpu_custom_call" | custom-call | tf_op jit(solution)/shard_map/written/pallas_call | solution.py:528

commit v9 on v8

--- a/solution.py
+++ b/solution.py
@@ -252,45 +252,57 @@
         side, column = order[i]
         return partial[piece(side, core, column)].astype(F32) + got_core[i].astype(F32)
 
-    crossing = []
-    for i, owner in enumerate((partner, diagonal, pair)):
+    part = share // 2
+    halves = [slice(h * part, (h + 1) * part) for h in range(2)]
+    owners = (partner, diagonal, pair)
+    for i in range(3):
         sent[i] = summed(i).astype(BF16)
-        crossing.append(send(sent.at[i], got.at[i], owner))
+        send(sent.at[i, :part], got.at[i, :part], owners[i])
+    for i in range(3):
+        send(sent.at[i, part:], got.at[i, part:], owners[i])
+    arriving = send.used[-6:]
     kept = summed(3)
     for copy in local:
         copy.wait()
-    for copy in crossing:
-        copy.wait_recv()
-    agg_near = (kept + got[2].astype(F32)).astype(BF16)
-    agg_far = (got[0].astype(F32) + got[1].astype(F32)).astype(BF16)
 
     def flat(blocks_of):
-        return blocks_of.reshape(near_rows, half)
-
-    mixed = jnp.concatenate(
-        [flat(own[...]), flat(own_far[...]), flat(agg_near), flat(agg_far)], axis=1
-    )
-    pre = jnp.dot(mixed, weights[...], preferred_element_type=F32) + jnp.concatenate(
+        return blocks_of.reshape(-1, half)
+
+    own_full = jnp.concatenate([flat(own[...]), flat(own_far[...])], axis=1)
+    own_pre = jnp.dot(own_full, weights[: 2 * half, :], preferred_element_type=F32) + jnp.concatenate(
         [bias[...], bias_far[...]], axis=1
     )
-    sigm = jax.nn.sigmoid(pre)
     cot_full = jnp.concatenate([flat(cot[...]), flat(cot_far[...])], axis=1).astype(F32)
-    grad_pre = cot_full * sigm * (1.0 + pre * (1.0 - sigm))
-    grad_low = grad_pre.astype(BF16)
     over_cols = (((1,), (1,)), ((), ()))
-    agg_back = lax.dot_general(
-        weights[2 * half :, :], grad_low, over_cols, preferred_element_type=F32
-    ).astype(BF16)
-    mine = pl.ds(edge * 2 * share + col * share, share)
-    for b in range(share):
-        grads[edge * 2 * share + col * share + b] = agg_back[:half, b * size : (b + 1) * size]
-        sent_grads[b] = agg_back[half:, b * size : (b + 1) * size]
-    crossing = [
-        send(sent_grads, grads.at[mine], diagonal),
-        send(sent_grads, grads.at[mine], partner),
-        send(grads.at[mine], grads.at[mine], pair),
-    ]
-    handed = [send(grads.at[mine], grads.at[mine], twin)]
+    mine = edge * 2 * share + col * share
+    crossing, handed, done = [], [], []
+    for h, at in enumerate(halves):
+        for copy in arriving[3 * h : 3 * h + 3]:
+            copy.wait_recv()
+        rows = slice(h * part * size, (h + 1) * part * size)
+        agg_near = (kept[at] + got[2, at].astype(F32)).astype(BF16)
+        agg_far = (got[0, at].astype(F32) + got[1, at].astype(F32)).astype(BF16)
+        agg = jnp.concatenate([flat(agg_near), flat(agg_far)], axis=1)
+        pre = own_pre[rows] + jnp.dot(agg, weights[2 * half :, :], preferred_element_type=F32)
+        sigm = jax.nn.sigmoid(pre)
+        grad_pre = cot_full[rows] * sigm * (1.0 + pre * (1.0 - sigm))
+        grad_low = grad_pre.astype(BF16)
+        agg_back = lax.dot_general(
+            weights[2 * half :, :], grad_low, over_cols, preferred_element_type=F32
+        ).astype(BF16)
+        for b in range(part):
+            grads[mine + h * part + b] = agg_back[:half, b * size : (b + 1) * size]
+            sent_grads[h * part + b] = agg_back[half:, b * size : (b + 1) * size]
+        home = pl.ds(mine + h * part, part)
+        crossing += [
+            send(sent_grads.at[at], grads.at[home], partner),
+            send(sent_grads.at[at], grads.at[home], diagonal),
+            send(grads.at[home], grads.at[home], pair),
+        ]
+        handed.append(send(grads.at[home], grads.at[home], twin))
+        done.append((agg, pre * sigm, grad_pre, grad_low))
+    agg, output, grad_pre, grad_low = (jnp.concatenate(both, axis=0) for both in zip(*done))
+    mixed = jnp.concatenate([own_full, agg], axis=1)
 
     parts = lax.dot_general(mixed, grad_low, (((0,), (0,)), ((), ())), preferred_element_type=F32)
     for k in range(2):
@@ -308,7 +320,7 @@
         steps.append(send(w_sent_z.at[j], w_got_z.at[z], z_peers[j]))
     w_got_z[z, z_many:] = w_bias[...].astype(BF16)
 
-    output = (pre * sigm).astype(BF16)
+    output = output.astype(BF16)
     out_near[...] = output[:, :half]
     far[:near_rows] = output[:, half:]
     self_back = lax.dot_general(grad_low, weights[: 2 * half, :], over_cols, preferred_element_type=F32)
@@ -329,13 +341,15 @@
 
     far_edge = lax.rem(edge + 2, 4)
     homes = [
-        pl.ds(far_edge * 2 * share + other * share, share),
-        pl.ds(edge * 2 * share + other * share, share),
-        pl.ds(far_edge * 2 * share + col * share, share),
+        edge * 2 * share + other * share,
+        far_edge * 2 * share + other * share,
+        far_edge * 2 * share + col * share,
     ]
-    for k in (1, 2, 0):
-        crossing[k].wait_recv()
-        handed.append(send(grads.at[homes[k]], grads.at[homes[k]], twin))
+    for h in range(2):
+        for k in range(3):
+            crossing[3 * h + k].wait_recv()
+            home = pl.ds(homes[k] + h * part, part)
+            handed.append(send(grads.at[home], grads.at[home], twin))
     for step in steps:
         step.wait_recv()
     x_total = w_got_x[0].astype(F32)
@@ -353,7 +367,7 @@
     blocks, size, half = partial.shape
     share = blocks // 8
     rows = share * size
-    copies = 4 + 3 + 3 + 4 + 6
+    copies = 4 + 6 + 6 + 8 + 6
     top = 4 * half
     piece = (share, size, half)
     return pl.pallas_call(

time: 92.7 us -> 92.8 us (level)
    pallas_call x1, Pallas kernels: 30.1 us -> 26.1 us  [middle(): pl.pallas_call(mid_kernel, out_shape=[pltpu.VMEM((blocks, half, size), BF...]
    pallas_call x2, Pallas kernels: 7.96 us -> 10.2 us  [tile_sum(): pl.pallas_call(kernel, out_shape=pltpu.VMEM((blocks, size, size), BF16),...]
    pallas_call x1, Pallas kernels: 27.6 us -> 28.9 us  [finish(): pl.pallas_call(final_kernel, out_shape=[pltpu.VMEM(piece, F32), pltpu.VME...]
where the time goes in v9:
time: 92.8 us; the launch traced here: 92 us
  Pallas kernels  90.7 us (98%)
  between operations  1.32 us (1%)
    pallas_call x1, Pallas kernels, finish(): pl.pallas_call(final_kernel, out_shape=[pltpu.VMEM(piece, F32), pltpu.VME...  28.9 us
    pallas_call x1, Pallas kernels, middle(): pl.pallas_call(mid_kernel, out_shape=[pltpu.VMEM((blocks, half, size), BF...  26.1 us
    pallas_call x1, Pallas kernels, exchange_inputs(): pl.pallas_call(halo_kernel, out_shape=[pltpu.VMEM(s.shape, s.dtype) for s...  24.4 us
    pallas_call x2, Pallas kernels, tile_sum(): pl.pallas_call(kernel, out_shape=pltpu.VMEM((blocks, size, size), BF16),...  10.2 us

profile of v9, /device:TPU:1, one launch (start us, length us, event | category | flops | bytes accessed | tf_op | source)
XLA Modules:
  0.0 92.0 jit_solution(18381626456346487442)
XLA Ops:
  1.3 24.4 %exchange_inputs.1 = (bf16[96,128,128]{2,1,0:T(8,128)(2,1)S(1)}, bf16[88,128,128]{2,1,0:T(8,128)(2,1)S(1)}, bf16[4,128,128]{2,1,0:T(8,128)(2,1)S(1)}, bf16[4,128...) custom-call(bf16[32,128,128]{2,1,0:T(8,128)(2,1)} %bitcast.4, ...), custom_call_target="tpu_custom_call" | custom-call | tf_op jit(solution)/shard_map/exchange_inputs/pallas_call | solution.py:191
  25.6 4.9 %forward_sum.1.partial = bf16[32,128,128]{2,1,0:T(8,128)(2,1)S(1)} custom-call(s32[704]{0:T(1024)} %rows.3, s32[704]{0:T(1024)} %cols.3, s32[1]{0:T(128)S(6)} %copy.14.count_ref, bf16[96,128,128]{2,1,0:T(8,128)(2,1)S(1)} %get-tuple-element.27.window, bf16[88,128,128]{2,1,0:T(8,128)(2,1)S(1)} %get-tuple-element.28.head, bf16[704,128,128]{2,1,0:T(8,128)(2,1)} %tiles.7), custom_call_target="tpu_custom_call" | custom-call | flops 2952790016 | bytes 23068672 | tf_op jit(solution)/shard_map/forward_sum/pallas_call | solution.py:115
  30.6 26.1 %middle.1 = (bf16[32,128,128]{2,1,0:T(8,128)(2,1)S(1)}, bf16[512,128]{1,0:T(8,128)(2,1)S(1)}, f32[512,128]{1,0:T(8,128)S(1)}, f32[2,144,128]{2,1,0:T(8,128)S(1)}...) custom-call(bf16[32,128,128]{2,1,0:T(8,128)(2,1)S(1)} %forward_sum.1.partial, ...), custom_call_target="tpu_custom_call" | custom-call | tf_op jit(solution)/shard_map/middle/pallas_call | solution.py:373
  56.7 5.3 %backward_sum.1.back = bf16[96,128,128]{2,1,0:T(8,128)(2,1)S(1)} custom-call(s32[704]{0:T(1024)} %rows.3, s32[704]{0:T(1024)} %cols.3, s32[1]{0:T(128)S(6)} %copy.14.count_ref, bf16[32,128,128]{2,1,0:T(8,128)(2,1)S(1)} %get-tuple-element.36.grads, bf16[88,128,128]{2,1,0:T(8,128)(2,1)S(1)} %get-tuple-element.37.head, bf16[704,128,128]{2,1,0:T(8,128)(2,1)} %tiles.7), custom_call_target="tpu_custom_call" | custom-call | flops 2952790016 | bytes 23068672 | tf_op jit(solution)/shard_map/backward_sum/pallas_call | solution.py:115
  62.0 28.9 %finish.1 = (f32[8,128,128]{2,1,0:T(8,128)S(1)}, f32[512,128]{1,0:T(8,128)S(1)}, f32[16,128]{1,0:T(8,128)S(1)}, bf16[1024,128]{1,0:T(8,128)(2,1)S(1)}) custom-call(bf16[96,128,128]{2,1,0:T(8,128)(2,1)S(1)} %backward_sum.1.back, f32[2,144,128]{2,1,0:T(8,128)S(1)} %get-tuple-element.38.weight_sum, bf16[1024,128]{1,0:T(8,128)(2,1)S(1)} %get-tuple-element.39.far), custom_call_target="tpu_custom_call" | custom-call | tf_op jit(solution)/shard_map/finish/pallas_call | solution.py:493
  90.9 1.1 %written.1 = (bf16[1024,128]{1,0:T(8,128)(2,1)}, f32[1024,128]{1,0:T(8,128)}, f32[256,128]{1,0:T(8,128)}, f32[256,128]{1,0:T(8,128)}, f32[1,128]{1,0:T(1,128)}) custom-call(bf16[512,128]{1,0:T(8,128)(2,1)S(1)} %get-tuple-element.34.out_near, f32[512,128]{1,0:T(8,128)S(1)} %get-tuple-element.35.self_near, bf16[1024,128]{1,0:T(8,128)(2,1)S(1)} %get-tuple-element.40.far, ...), custom_call_target="tpu_custom_call" | custom-call | tf_op jit(solution)/shard_map/written/pallas_call | solution.py:542
